TPU v7x, 32 devices: a whole 2x2x4 slice. The times are simulated.
32 devices in a mesh: seq: 8 (over y, x, core), row: 4 (over z).
Axes of the slice: x: 2, y: 2, z: 4, core: 2. Of those that a mesh axis runs over, the one named last changes fastest.
Arguments:
- inputs: bfloat16 [12, 2048, 1024], P('row', 'seq'), may hold values from -6 to 6
- lengths: int32 [12, 8], P('row'), may hold values from 0 to 2048, as said below
- norm_gain: bfloat16 [1024], P('seq'), may hold values from 0.5 to 1.5
- w_qkv: bfloat16 [1024, 3072], P('seq'), may hold values from -0.1875 to 0.1875
- w_beta: bfloat16 [1024, 8], P('seq'), may hold values from -0.1875 to 0.1875
- beta_bias: bfloat16 [8], replicated, may hold values from -4 to -1
- w_conv: bfloat16 [4, 3072], P(None, 'seq'), may hold values from -2.5 to 2.5
- w_out: bfloat16 [1024, 1024], P('seq'), may hold values from -0.75 to 0.75
- ffn_gain: bfloat16 [1024], P('seq'), may hold values from 0.5 to 1.5
- w_gate: bfloat16 [1024, 2816], P('seq'), may hold values from -0.1875 to 0.1875
- w_up: bfloat16 [1024, 2816], P('seq'), may hold values from -0.1875 to 0.1875
- w_down: bfloat16 [2816, 1024], P('seq'), may hold values from -0.109375 to 0.109375
- cotangent: bfloat16 [12, 2048, 1024], P('row', 'seq'), may hold values from -6 to 6
Outputs:
- output: bfloat16 [12, 2048, 1024], P('row', 'seq')
- grad_inputs: bfloat16 [12, 2048, 1024], P('row', 'seq')
- grad_norm_gain: float32 [1024], P('seq')
- grad_w_qkv: float32 [1024, 3072], P('seq')
- grad_w_beta: float32 [1024, 8], P('seq')
- grad_beta_bias: float32 [8], replicated
- grad_w_conv: float32 [4, 3072], P(None, 'seq')
- grad_w_out: float32 [1024, 1024], P('seq')
- grad_ffn_gain: float32 [1024], P('seq')
- grad_w_gate: float32 [1024, 2816], P('seq')
- grad_w_up: float32 [1024, 2816], P('seq')
- grad_w_down: float32 [2816, 1024], P('seq')
Inputs may be any that keep to these rules, and one draw needn't show every extreme that they name: Each row's entries are document lengths laid end to end from the row's first slot, with zeros only after its last nonzero entry; they sum to 2048 at most and the slots after them are padding. In each aligned block of 3 rows one row is a single document of 2048 tokens.
All inputs are finite; a program needn't handle non-finite values.
Results may differ from a plain program's by a relative error of at most 0.019.
Values may be sent and summed in bfloat16 or wider, within the bound.
No kernel may reach another device: no remote copies, remote signals or barrier semaphores. Data moves between devices by JAX's collectives and lax.ppermute only.
A program may use at most 384 MiB of HBM per device.

v0:
```python
import jax
import jax.numpy as jnp
from jax import lax
from jax.sharding import PartitionSpec as P

BLOCK = 64


EPSILON = 1e-06
PRECISE = lax.Precision.HIGHEST


def shifted(value, axis, steps):
    count = lax.axis_size(axis)
    leading, last = (max(0, -steps), min(count, count - steps))
    return lax.ppermute(value, axis, [(source, source + steps) for source in range(leading, last)])


def matmul(left, right):
    return jnp.einsum("...ij,...jk->...ik", left, right, precision=PRECISE)


def rms_scale(values):
    return lax.rsqrt(jnp.mean(values * values, axis=-1, keepdims=True) + EPSILON)


def unit_rows(values):
    return values * lax.rsqrt(jnp.sum(values * values, axis=-1, keepdims=True) + EPSILON)


def block_masks(doc_block, doc_before):
    same_doc = (doc_block[..., :, None] == doc_block[..., None, :]).astype(jnp.float32)
    carried = (doc_block == doc_before[..., None]).astype(jnp.float32)
    last_doc = (doc_block == doc_block[..., -1:]).astype(jnp.float32)
    return (same_doc, carried, last_doc)


def block_weights(key_rows, values, beta_rate, same_doc, carried):
    length = key_rows.shape[-3]
    head_size = key_rows.shape[-1]
    strict = jnp.tril(jnp.ones((length, length), jnp.float32), -1)
    key_gram = jnp.einsum("...thd,...shd->...hts", key_rows, key_rows, precision=PRECISE)
    row_rates = jnp.swapaxes(beta_rate, -1, -2)[..., :, :, None]
    system = key_gram * (same_doc * strict)[..., None, :, :] * row_rates + jnp.eye(
        length, dtype=jnp.float32
    )
    right_side = jnp.concatenate(
        [(beta_rate * carried[..., None])[..., None] * key_rows, beta_rate[..., None] * values],
        axis=-1,
    )
    solved = jax.scipy.linalg.solve_triangular(
        system, jnp.swapaxes(right_side, -3, -2), lower=True, unit_diagonal=True
    )
    return (solved[..., :head_size], solved[..., head_size:])


def block_apply(queries, key_rows, weight_keys, weight_values, same_doc, carried, last_doc, memory):
    length = queries.shape[-3]
    inclusive = jnp.tril(jnp.ones((length, length), jnp.float32))
    fresh = weight_values - jnp.einsum(
        "...hcd,...hed->...hce", weight_keys, memory, precision=PRECISE
    )
    scores = (
        jnp.einsum("...thd,...shd->...hts", queries, key_rows, precision=PRECISE)
        * (same_doc * inclusive)[..., None, :, :]
    )
    reading = carried[..., :, None, None] * jnp.einsum(
        "...thd,...hed->...the", queries, memory, precision=PRECISE
    )
    outputs = reading + jnp.einsum("...hts,...hse->...the", scores, fresh, precision=PRECISE)
    last_keys = last_doc[..., :, None, None] * key_rows
    memory = carried[..., -1][..., None, None, None] * memory + jnp.einsum(
        "...hce,...chd->...hed", fresh, last_keys, precision=PRECISE
    )
    return (outputs, memory)


def block_transition(key_rows, weight_keys, weight_values, carried, last_doc):
    head_size = key_rows.shape[-1]
    last_keys = last_doc[..., :, None, None] * key_rows
    decays = carried[..., -1][..., None, None, None] * jnp.eye(
        head_size, dtype=jnp.float32
    ) - jnp.einsum("...hcd,...chf->...hdf", weight_keys, last_keys, precision=PRECISE)
    writes = jnp.einsum("...hce,...chd->...hed", weight_values, last_keys, precision=PRECISE)
    return (decays, writes)


def chain_step(earlier, later):
    return (matmul(earlier[0], later[0]), matmul(earlier[1], later[0]) + later[1])


def to_blocks(array):
    return array.reshape((array.shape[0], array.shape[1] // BLOCK, BLOCK) + array.shape[2:])


def prepare(convolved, logits, valid_mask, head_count):
    row_count, slot_count, triple = convolved.shape
    mixed_acts = jax.nn.silu(convolved).reshape(
        row_count, slot_count, 3, head_count, triple // (3 * head_count)
    )
    queries = unit_rows(mixed_acts[:, :, 0])
    key_rows = unit_rows(mixed_acts[:, :, 1])
    values = mixed_acts[:, :, 2]
    beta_rate = valid_mask[..., None] * jax.nn.sigmoid(logits)
    return (queries, key_rows, values, beta_rate)


def sweep(queries, key_rows, weight_keys, weight_values, masks, memory):
    same_doc, carried, last_doc = masks
    stacked = tuple(
        (
            jnp.moveaxis(member, 1, 0)
            for member in (
                queries,
                key_rows,
                weight_keys,
                weight_values,
                same_doc,
                carried,
                last_doc,
            )
        )
    )

    def advance(current, block_data):
        outputs, current = block_apply(*block_data, current)
        return (current, outputs)

    closing, outputs = lax.scan(advance, memory, stacked)
    outputs = jnp.moveaxis(outputs, 0, 1)
    return (outputs.reshape(outputs.shape[0], -1, outputs.shape[-2] * outputs.shape[-1]), closing)


def on_device(
    inputs,
    lengths,
    norm_gain,
    w_qkv,
    w_beta,
    beta_bias,
    w_conv,
    w_out,
    ffn_gain,
    w_gate,
    w_up,
    w_down,
    cotangent,
):
    row_count, slot_count, width = inputs.shape
    head_count = beta_bias.shape[0]
    head_size = width // head_count
    tap_count = w_conv.shape[0]
    rim_size = tap_count - 1
    seq_count = lax.axis_size("seq")
    position = lax.axis_index("seq")
    full_gain, full_qkv, full_beta, full_conv, full_out = (
        lax.all_gather(norm_gain, "seq", axis=0, tiled=True),
        lax.all_gather(w_qkv, "seq", axis=0, tiled=True),
        lax.all_gather(w_beta, "seq", axis=0, tiled=True),
        lax.all_gather(w_conv, "seq", axis=1, tiled=True),
        lax.all_gather(w_out, "seq", axis=0, tiled=True),
    )
    full_ffn_gain, full_gate, full_up, full_down = (
        lax.all_gather(ffn_gain, "seq", axis=0, tiled=True),
        lax.all_gather(w_gate, "seq", axis=0, tiled=True),
        lax.all_gather(w_up, "seq", axis=0, tiled=True),
        lax.all_gather(w_down, "seq", axis=0, tiled=True),
    )
    conv_wide = full_conv.astype(jnp.float32)
    doc_ends = jnp.cumsum(lengths, axis=1, dtype=jnp.int32)
    spots = position * slot_count - rim_size + jnp.arange(slot_count + rim_size, dtype=jnp.int32)
    ext_docs = jnp.sum(
        (spots[None, :, None] >= doc_ends[:, None, :]).astype(jnp.int32), axis=2, dtype=jnp.int32
    )
    ext_docs = jnp.where(spots[None, :] < 0, -1, ext_docs)
    own_docs = ext_docs[:, rim_size:]
    valid_mask = (spots[None, rim_size:] < doc_ends[:, -1:]).astype(jnp.float32)
    before = ext_docs[:, rim_size - 1 : rim_size - 1 + slot_count : BLOCK]
    masks = block_masks(to_blocks(own_docs), before)
    same_doc, carried, last_doc = masks
    mask_col = valid_mask[..., None]
    wide_inputs = inputs.astype(jnp.float32)
    first_scale = rms_scale(wide_inputs)
    normed = (wide_inputs * first_scale * full_gain).astype(jnp.bfloat16)
    projected = jnp.dot(normed, full_qkv, preferred_element_type=jnp.float32).astype(jnp.bfloat16)
    logits = jnp.dot(normed, full_beta, preferred_element_type=jnp.float32) + beta_bias.astype(
        jnp.float32
    )
    rim_rows = shifted(projected[:, slot_count - rim_size :], "seq", 1)
    extended = jnp.concatenate([rim_rows, projected], axis=1)
    conv_masks = [
        (ext_docs[:, rim_size - offset : rim_size - offset + slot_count] == own_docs).astype(
            jnp.float32
        )[..., None]
        for offset in range(tap_count)
    ]
    convolved = jnp.zeros(projected.shape, jnp.float32)
    for offset in range(tap_count):
        window = extended[:, rim_size - offset : rim_size - offset + slot_count].astype(jnp.float32)
        convolved = convolved + conv_wide[offset] * window * conv_masks[offset]
    prepared = prepare(convolved, logits, valid_mask, head_count)
    block_query, block_key, block_value, block_rate = (to_blocks(member) for member in prepared)
    weight_keys, weight_values = block_weights(
        block_key, block_value, block_rate, same_doc, carried
    )
    decays, writes = block_transition(block_key, weight_keys, weight_values, carried, last_doc)
    identity = jnp.broadcast_to(
        jnp.eye(head_size, dtype=jnp.float32), (row_count, head_count, head_size, head_size)
    )
    zero_state = jnp.zeros((row_count, head_count, head_size, head_size), jnp.float32)

    def fold_blocks(pair_now, pair_next):
        return (chain_step(pair_now, pair_next), None)

    (dev_decay, dev_write), _ = lax.scan(
        fold_blocks,
        (identity, zero_state),
        (jnp.moveaxis(decays, 1, 0), jnp.moveaxis(writes, 1, 0)),
    )
    device_order = jnp.arange(seq_count, dtype=jnp.int32)
    all_decay, all_write = (
        lax.all_gather(dev_decay, "seq", axis=0, tiled=True),
        lax.all_gather(dev_write, "seq", axis=0, tiled=True),
    )
    all_decay = all_decay.reshape((seq_count,) + dev_decay.shape)
    all_write = all_write.reshape((seq_count,) + dev_write.shape)

    def forward_step(current, entry):
        source_rank, step_decay, step_write = entry
        advanced = matmul(current, step_decay) + step_write
        return (jnp.where(source_rank < position, advanced, current), None)

    entry_state, _ = lax.scan(forward_step, zero_state, (device_order, all_decay, all_write))
    heads_out, _ = sweep(block_query, block_key, weight_keys, weight_values, masks, entry_state)
    heads_low = heads_out.astype(jnp.bfloat16)
    hidden = wide_inputs + jnp.dot(heads_low, full_out, preferred_element_type=jnp.float32)
    second_scale = rms_scale(hidden)
    second = (hidden * second_scale * full_ffn_gain).astype(jnp.bfloat16)
    gated = jnp.dot(second, full_gate, preferred_element_type=jnp.float32)
    lifted = jnp.dot(second, full_up, preferred_element_type=jnp.float32)
    activated = (jax.nn.silu(gated) * lifted).astype(jnp.bfloat16)
    output = (
        mask_col * (hidden + jnp.dot(activated, full_down, preferred_element_type=jnp.float32))
    ).astype(jnp.bfloat16)
    upstream = cotangent.astype(jnp.float32) * mask_col
    upstream_low = upstream.astype(jnp.bfloat16)
    grad_down = jnp.einsum(
        "rsf,rsd->fd", activated, upstream_low, preferred_element_type=jnp.float32
    )
    grad_act = jnp.einsum(
        "rsd,fd->rsf", upstream_low, full_down, preferred_element_type=jnp.float32
    )
    sigmoid_gate = jax.nn.sigmoid(gated)
    grad_gated = (grad_act * lifted * sigmoid_gate * (1.0 + gated * (1.0 - sigmoid_gate))).astype(
        jnp.bfloat16
    )
    grad_lifted = (grad_act * gated * sigmoid_gate).astype(jnp.bfloat16)
    grad_gate_w = jnp.einsum("rsd,rsf->df", second, grad_gated, preferred_element_type=jnp.float32)
    grad_up_w = jnp.einsum("rsd,rsf->df", second, grad_lifted, preferred_element_type=jnp.float32)
    grad_second = jnp.einsum(
        "rsf,df->rsd", grad_gated, full_gate, preferred_element_type=jnp.float32
    ) + jnp.einsum("rsf,df->rsd", grad_lifted, full_up, preferred_element_type=jnp.float32)
    grad_ffn_gain = jnp.sum(grad_second * hidden * second_scale, axis=(0, 1))
    scaled_second = full_ffn_gain.astype(jnp.float32) * grad_second
    grad_hidden = (
        upstream
        + second_scale * scaled_second
        - hidden * second_scale**3 * jnp.mean(scaled_second * hidden, axis=-1, keepdims=True)
    )
    grad_mix_low = grad_hidden.astype(jnp.bfloat16)
    grad_out_w = jnp.einsum(
        "rsd,rse->de", heads_low, grad_mix_low, preferred_element_type=jnp.float32
    )
    grad_heads = jnp.einsum(
        "rse,de->rsd", grad_mix_low, full_out, preferred_element_type=jnp.float32
    )

    def reading(memory):
        return sweep(block_query, block_key, weight_keys, weight_values, masks, memory)[0]

    _, pull_reading = jax.vjp(reading, entry_state)
    (local_grad,) = pull_reading(grad_heads)
    all_grad = (
        lax.all_gather(local_grad.astype(jnp.bfloat16), "seq", axis=0, tiled=True)
        .astype(local_grad.dtype)
        .reshape((seq_count,) + local_grad.shape)
    )

    def backward_step(current, entry):
        source_rank, step_decay, step_grad = entry
        advanced = step_grad + jnp.einsum(
            "...ek,...jk->...ej", current, step_decay, precision=PRECISE
        )
        return (jnp.where(source_rank > position, advanced, current), None)

    exit_grad, _ = lax.scan(
        backward_step, zero_state, (device_order, all_decay, all_grad), reverse=True
    )

    def mixer(conv_in, logit_in, memory):
        mix_query, mix_key, mix_value, mix_rate = (
            to_blocks(member) for member in prepare(conv_in, logit_in, valid_mask, head_count)
        )
        mix_wkeys, mix_wvalues = block_weights(mix_key, mix_value, mix_rate, same_doc, carried)
        return sweep(mix_query, mix_key, mix_wkeys, mix_wvalues, masks, memory)

    _, pull_mixer = jax.vjp(mixer, convolved, logits, entry_state)
    grad_conv, grad_logits, _ = pull_mixer((grad_heads, exit_grad))
    grad_ext = jnp.zeros(extended.shape, jnp.float32)
    grad_taps = []
    for offset in range(tap_count):
        window = extended[:, rim_size - offset : rim_size - offset + slot_count].astype(jnp.float32)
        masked_grad = grad_conv * conv_masks[offset]
        grad_taps.append(jnp.sum(masked_grad * window, axis=(0, 1)))
        grad_ext = grad_ext.at[:, rim_size - offset : rim_size - offset + slot_count].add(
            conv_wide[offset] * masked_grad
        )
    grad_conv_w = jnp.stack(grad_taps)
    back_rim = shifted(grad_ext[:, :rim_size].astype(jnp.bfloat16), "seq", -1).astype(jnp.float32)
    grad_proj = grad_ext[:, rim_size:] + jnp.pad(
        back_rim, ((0, 0), (slot_count - rim_size, 0), (0, 0))
    )
    grad_proj_low = grad_proj.astype(jnp.bfloat16)
    grad_qkv_w = jnp.einsum(
        "rsd,rse->de", normed, grad_proj_low, preferred_element_type=jnp.float32
    )
    grad_beta_w = jnp.einsum(
        "rsd,rsh->dh", normed.astype(jnp.float32), grad_logits, precision=PRECISE
    )
    bias_local = jnp.sum(grad_logits, axis=(0, 1))
    grad_normed = jnp.einsum(
        "rse,de->rsd", grad_proj_low, full_qkv, preferred_element_type=jnp.float32
    ) + jnp.einsum("rsh,dh->rsd", grad_logits, full_beta.astype(jnp.float32), precision=PRECISE)
    grad_norm_gain = jnp.sum(grad_normed * wide_inputs * first_scale, axis=(0, 1))
    scaled_first = full_gain.astype(jnp.float32) * grad_normed
    grad_inputs = (
        grad_hidden
        + first_scale * scaled_first
        - wide_inputs
        * first_scale**3
        * jnp.mean(scaled_first * wide_inputs, axis=-1, keepdims=True)
    )
    shards = (
        lax.psum_scatter(
            grad_norm_gain.astype(jnp.bfloat16), "seq", scatter_dimension=0, tiled=True
        ).astype(jnp.float32),
        lax.psum_scatter(
            grad_qkv_w.astype(jnp.bfloat16), "seq", scatter_dimension=0, tiled=True
        ).astype(jnp.float32),
        lax.psum_scatter(
            grad_beta_w.astype(jnp.bfloat16), "seq", scatter_dimension=0, tiled=True
        ).astype(jnp.float32),
        lax.psum_scatter(
            grad_conv_w.astype(jnp.bfloat16), "seq", scatter_dimension=1, tiled=True
        ).astype(jnp.float32),
        lax.psum_scatter(
            grad_out_w.astype(jnp.bfloat16), "seq", scatter_dimension=0, tiled=True
        ).astype(jnp.float32),
        lax.psum_scatter(
            grad_ffn_gain.astype(jnp.bfloat16), "seq", scatter_dimension=0, tiled=True
        ).astype(jnp.float32),
        lax.psum_scatter(
            grad_gate_w.astype(jnp.bfloat16), "seq", scatter_dimension=0, tiled=True
        ).astype(jnp.float32),
        lax.psum_scatter(
            grad_up_w.astype(jnp.bfloat16), "seq", scatter_dimension=0, tiled=True
        ).astype(jnp.float32),
        lax.psum_scatter(
            grad_down.astype(jnp.bfloat16), "seq", scatter_dimension=0, tiled=True
        ).astype(jnp.float32),
    )
    summed = (
        lax.psum(shards[0].astype(jnp.bfloat16), "row").astype(jnp.float32),
        lax.psum(shards[1].astype(jnp.bfloat16), "row").astype(jnp.float32),
        lax.psum(shards[2].astype(jnp.bfloat16), "row").astype(jnp.float32),
        lax.psum(shards[3].astype(jnp.bfloat16), "row").astype(jnp.float32),
        lax.psum(shards[4].astype(jnp.bfloat16), "row").astype(jnp.float32),
        lax.psum(shards[5].astype(jnp.bfloat16), "row").astype(jnp.float32),
        lax.psum(shards[6].astype(jnp.bfloat16), "row").astype(jnp.float32),
        lax.psum(shards[7].astype(jnp.bfloat16), "row").astype(jnp.float32),
        lax.psum(shards[8].astype(jnp.bfloat16), "row").astype(jnp.float32),
    )
    bias_total = lax.psum(bias_local, ("seq", "row"))
    return (
        output,
        grad_inputs.astype(jnp.bfloat16),
        summed[0],
        summed[1],
        summed[2],
        bias_total,
        summed[3],
        summed[4],
        summed[5],
        summed[6],
        summed[7],
        summed[8],
    )


def solution(mesh):
    placed = (
        P("row", "seq", None),
        P("row", None),
        P("seq"),
        P("seq", None),
        P("seq", None),
        P(),
        P(None, "seq"),
        P("seq", None),
        P("seq"),
        P("seq", None),
        P("seq", None),
        P("seq", None),
        P("row", "seq", None),
    )
    return jax.shard_map(
        on_device,
        mesh=mesh,
        in_specs=placed,
        out_specs=(
            P("row", "seq", None),
            P("row", "seq", None),
            P("seq"),
            P("seq", None),
            P("seq", None),
            P(),
            P(None, "seq"),
            P("seq", None),
            P("seq"),
            P("seq", None),
            P("seq", None),
            P("seq", None),
        ),
        check_vma=False,
    )
```

profile of v0, /device:TPU:0, one launch (start us, length us, event | category | flops | bytes accessed | tf_op | source)
XLA Modules:
  0.0 2040.1 jit_solution(18311928252116066996)
XLA Ops:
  12.8 10.3 all-gather
  25.5 8.9 all_gather.36
  35.1 8.0 all_gather.39
  46.4 11.9 all-gather.11.cloned.1.call-done
  58.3 8.2 fusion.220
  72.1 14.5 fusion.196
  94.8 7.3 fusion.325
  102.2 7.0 fusion.306
  113.1 473.3 %custom-call.15 = f32[3,4,8,1,64,64]{4,5,3,2,1,0:T(8,128)} custom-call(f32[3,4,8,1,64,64]{5,4,3,2,1,0:T(8,128)} %add_bitcast_fusion), custom_call_target="InvertDiagBlocksLowerTriangular" | custom-call | tf_op jit(solution)/shard_map/jit(_solve_triangular)/vmap(vmap(vmap()))/triangular_solve/custom-call.1 | solution.py:51
  592.6 6.5 fusion.197
  599.1 12.9 fusion.254
  612.1 13.3 bitcast_subtract_fusion
  626.7 61.6 %while.141 = (s32[]{:T(128)}, f32[3,8,128,128]{2,3,1,0:T(8,128)}, f32[3,8,128,128]{2,3,1,0:T(8,128)}, f32[4,3,8,128,128]{4,3,2,0,1:T(8,128)}, f32[4,3,8,128,128]{4,3,2,0,1:T(8,128)}, /*index=5*/s32[]{:T(128)}, s32[]{:T(128)}) while((s32[]{:T(128)}, f32[3,8,128,128]{2,3,1,0:T(8,128)}, f32[3,8,128,128]{2,3,1,0:T(8,128)}, ...), condition=%wide.region_5.7_spmd.clone, body=%wide.region_4.6_spmd.clone.sunk | while | flops 1208745984 | bytes 23593064 | solution.py:215
  628.1 5.3 fusion.483
  643.4 5.3 fusion.483
  658.7 5.3 fusion.483
  674.0 5.3 fusion.483
  697.7 13.3 all-gather.1
  711.0 9.6 fusion.208
  743.9 34.1 %while.139 = (s32[]{:T(128)}, f32[4,3,64,1,1]{2,1,4,3,0:T(4,128)}, f32[4,3,8,64,64]{4,3,2,1,0:T(8,128)}, f32[4,3,1,1,1]{1,4,3,2,0:T(1,128)}, f32[4,3,64,8,128]{4...) while((s32[]{:T(128)}, f32[4,3,64,1,1]{2,1,4,3,0:T(4,128)}, ...), condition=%wide.region_14.16_spmd.clone, body=%wide.region_13.15_spmd.clone.sunk | while | flops 151310336 | bytes 4173197 | solution.py:129
  778.0 64.8 %all-gather.15.cloned.1.call-done = f32[24,8,128,128]{3,2,1,0:T(8,128)} async-done(((f32[3,8,128,128]{3,2,1,0:T(8,128)}), f32[24,8,128,128]{3,2,1,0:T(8,128)}) %all-gather.15.cloned.1.call-update) | async-done | bytes 12582928 | tf_op jit(solution)/shard_map/all_gather | solution.py:223
  842.8 110.7 %while.142 = (s32[]{:T(128)}, f32[3,8,128,128]{2,3,1,0:T(8,128)}, s32[8]{0:T(128)S(1)}, s32[]{:T(128)}, f32[8,3,8,128,128]{4,3,2,1,0:T(8,128)}, /*index=5*/f32[8,3,8,128,128]{4,3,2,1,0:T(8,128)}, s32[]{:T(128)}, s32[]{:T(128)}) while((s32[]{:T(128)}, f32[3,8,128,128]{2,3,1,0:T(8,128)}, s32[8]{0:T(128)S(1)}, s32[]{:T(128)}, ...), condition=%wide.region_7.9_spmd.clone, body=%wide.region_6.8_spmd.clone.sunk | while | flops 605552640 | bytes 23595164 | solution.py:233
  955.6 78.9 %while.137 = (s32[]{:T(128)}, f32[3,8,128,128]{3,2,1,0:T(8,128)S(1)}, bf16[4,3,64,8,128]{4,2,3,1,0:T(8,128)(2,1)}, f32[4,3,64]{1,2,0:T(8,128)}, f32[4,3,8,64,128...) while((s32[]{:T(128)}, ...), condition=%wide.region_10.12_spmd, body=%wide.region_9.11_spmd.sunk | while | flops 1209651200 | bytes 42313720 | solution.py:129
  1048.4 10.1 fusion.214
  1058.5 17.6 multiply_convert_fusion.1
  1076.1 6.7 fusion.212
  1082.8 9.3 multiply_reduce_fusion
  1098.5 76.2 %while.143 = (s32[]{:T(128)}, f32[3,8,128,128]{3,2,1,0:T(8,128)S(1)}, f32[4,3,1,1,1]{1,4,3,2,0:T(1,128)}, f32[4,3,64,1,1]{2,1,4,3,0:T(4,128)}, f32[4,3,64,8,128]...) while((s32[]{:T(128)}, ...), condition=%wide.region_16.18_spmd.clone, body=%wide.region_15.17_spmd.clone.sunk | while | flops 1059520512 | bytes 22024676 | solution.py:129
  1176.0 5.7 bitcast_convert_fusion.4
  1181.8 9.1 bitcast_convert_fusion.3
  1192.5 10.1 bitcast_convert_fusion.2
  1202.7 8.9 bitcast_convert_fusion.1
  1218.2 73.3 %while.140 = (s32[]{:T(128)}, f32[3,8,128,128]{3,2,1,0:T(8,128)S(1)}, f32[4,3,8,128,128]{4,3,2,1,0:T(8,128)}, f32[4,3,1,64,64]{4,3,1,2,0:T(8,128)}, f32[4,3,64,1...) while((s32[]{:T(128)}, ...), condition=%wide.region_20.22_spmd.clone.clone, body=%wide.region_19.21_spmd.clone.clone.sunk | while | flops 756482048 | bytes 16878068 | solution.py:129
  1219.5 5.5 bitcast_dynamic-update-slice_fusion.7
  1238.0 5.4 bitcast_dynamic-update-slice_fusion.7
  1256.1 5.5 bitcast_dynamic-update-slice_fusion.7
  1274.4 5.5 bitcast_dynamic-update-slice_fusion.7
  1291.6 9.8 convert.37
  1301.4 72.7 %while.144 = (s32[]{:T(128)}, f32[3,8,128,128]{2,3,1,0:T(8,128)}, s32[8]{0:T(128)S(1)}, s32[]{:T(128)}, f32[8,3,8,128,128]{4,3,2,1,0:T(8,128)}, /*index=5*/f32[8...) while((s32[]{:T(128)}, f32[3,8,128,128]{2,3,1,0:T(8,128)}, s32[8]{0:T(128)S(1)}, ...), condition=%wide.region_18.20_spmd.clone, body=%wide.region_17.19_spmd.clone.sunk | while | flops 605552640 | bytes 17303700 | solution.py:296
  1384.1 136.5 %while.138 = (s32[]{:T(128)}, f32[3,8,128,128]{3,2,1,0:T(8,128)S(1)}, f32[4,3,64,8,128]{4,3,2,0,1:T(8,128)}, f32[4,3,64,8,128]{4,2,3,0,1:T(8,128)}, f32[4,3,8,64...) while((s32[]{:T(128)}, ...), condition=%wide.region_22.24_spmd, body=%wide.region_21.23_spmd.sunk | while | flops 2418769920 | bytes 79641192 | solution.py:129
  1520.6 12.9 fusion.204
  1533.5 8.8 fusion.259
  1542.4 8.3 multiply_reduce_fusion.1
  1550.7 5.5 multiply_reduce_fusion.2
  1556.2 5.8 fusion.264
  1562.0 11.7 bitcast_add_fusion.3
  1588.2 5.9 copy.466
  1594.1 7.2 add_add_fusion.3
  1607.8 11.0 reshape.514
  1618.8 23.9 %fusion.188 = (bf16[3072]{0:T(1024)(128)(2,1)S(1)}, bf16[3072]{0:T(1024)(128)(2,1)S(1)}, bf16[3072]{0:T(1024)(128)(2,1)S(1)}, bf16[3072]{0:T(1024)(128)(2,1)S(1)}, f32[3,256,3072]{2,1,0:T(8,128)S(1)}) fusion(f32[3,256]{1,0:T(4,128)S(1)} %copy-done.90, bf16[3,256,3072]{2,1,0:T(8,128)(2,1)} %copy-done.22, bf16[3,3,3072]{2,1,0:T(4,128)(2,1)S(1)} %copy-done.60, ...), kind=kLoop, calls=%fused_computation.239 | loop fusion | flops 120311808 | bytes 23731200 | tf_op jit(solution)/shard_map/reduce_sum | solution.py:314
  1656.4 13.4 multiply_add_fusion.2
  1669.8 23.1 %scatter-add.15 = f32[3,259,3072]{2,1,0:T(8,128)} dynamic-update-slice(f32[3,259,3072]{2,1,0:T(8,128)} %scatter-add.14, f32[3,256,3072]{2,1,0:T(8,128)} %multiply_add_fusion.2, s32[]{:T(128)} %constant.391.clone.1, s32[]{:T(128)} %constant.398.clone.1, s32[]{:T(128)} %constant.391.clone.1) | dynamic-update-slice | bytes 18874372 | tf_op jit(solution)/shard_map/scatter-add | solution.py:315
  1692.9 13.5 slice_add_fusion.2
  1706.5 23.1 %scatter-add.16 = f32[3,259,3072]{2,1,0:T(8,128)} dynamic-update-slice(f32[3,259,3072]{2,1,0:T(8,128)} %scatter-add.15, f32[3,256,3072]{2,1,0:T(8,128)} %slice_add_fusion.2, s32[]{:T(128)} %constant.391.clone.1, s32[]{:T(128)} %constant.399.clone.1, s32[]{:T(128)} %constant.391.clone.1) | dynamic-update-slice | bytes 18874372 | tf_op jit(solution)/shard_map/scatter-add | solution.py:315
  1729.5 12.2 constant_dynamic-update-slice_fusion.5
  1744.9 11.2 bitcast_convert_fusion
  1761.9 59.7 %reduce-scatter.12.cloned.1.call-done = bf16[128,3072]{1,0:T(8,128)(2,1)} async-done(((bf16[1024,3072]{1,0:T(8,128)(2,1)}), bf16[128,3072]{1,0:T(8,128)(2,1)}) %reduce-scatter.12.cloned.1.call-update) | async-done | bytes 786448 | tf_op jit(solution)/shard_map/reduce_scatter | solution.py:347
  1821.6 9.7 multiply_convert_fusion.3
  1831.3 39.3 %psum.73 = f32[8]{0:T(128)} all-reduce(f32[8]{0:T(128)S(1)} %get-tuple-element.1854), channel_id=1, replica_groups=mesh['seq'=8,'row'=4] {'seq','row'}, use_global_device_ids=true, to_apply=%region_37.39 | all-reduce | flops 8 | bytes 64 | tf_op jit(solution)/shard_map/psum | solution.py:383
  1874.6 22.9 %reduce-scatter.24.cloned.1.call-done = bf16[384,4]{1,0:T(8,128)(2,1)} async-done(((bf16[3072,4]{1,0:T(8,128)(2,1)}), bf16[384,4]{1,0:T(8,128)(2,1)}) %reduce-scatter.24.cloned.1.call-update) | async-done | bytes 3088
  1898.5 14.2 fusion.233
  1912.7 13.2 all-reduce.9
  1926.0 12.9 all-reduce.10
  1945.5 79.8 %all-reduce.14.cloned.1.call-done = (bf16[128,3072]{1,0:T(8,128)(2,1)}, bf16[128,1024]{1,0:T(8,128)(2,1)}, bf16[128,2816]{1,0:T(8,128)(2,1)}, bf16[128,2816]{1,0:T(8,128)(2,1)}, bf16[352,1024]{1,0:T(8,128)(2,1)}) async-done(((bf16[128,3072]{1,0:T(8,128)(2,1)}, bf16[128,1024]{1,0:T(8,128)(2,1)}, bf16[128,2816]{1,0:T(8,128)(2,1)}, bf16[128,2816]{1,0:T(8,128)(2,1)}, bf16[352,1024]{1,0:T(8,128)(2,1)}), ...) | async-done | bytes 3211280 | tf_op jit(solution)/shard_map/psum | solution.py:374
  (800 shorter events, 762.1 us)
Async XLA Ops:
  7.2 36.0 %copy-start.32 = (bf16[3,256,1024]{2,1,0:T(8,128)(2,1)S(1)}, bf16[3,256,1024]{2,1,0:T(8,128)(2,1)}, u32[]{:S(2)}) copy-start(bf16[3,256,1024]{2,1,0:T(8,128)(2,1)} %param.39) | copy-start | bytes 4718596
  7.2 18.3 copy-start.104
  7.2 27.9 %copy-start.111 = (bf16[8]{0:T(256)(128)(2,1)S(1)}, bf16[8]{0:T(256)(128)(2,1)}, u32[]{:S(2)}) copy-start(bf16[8]{0:T(256)(128)(2,1)} %param.44) | copy-start | bytes 52
  7.2 27.9 %copy-start.105 = (bf16[128,8]{0,1:T(8,128)(2,1)S(1)}, bf16[128,8]{0,1:T(8,128)(2,1)}, u32[]{:S(2)}) copy-start(bf16[128,8]{0,1:T(8,128)(2,1)} %param.43) | copy-start | bytes 6148
  7.2 51.1 %all-gather.11.cloned.1.call-start = ((), (), s32[]{:S(2)}) async-start(), calls=%async_computation.7 | async-start | bytes 7077888 | tf_op jit(solution)/shard_map/all_gather | solution.py:158
  8.0 703.0 %all-gather.23.cloned.1.call-start = ((), (), s32[]{:S(2)}) async-start(), calls=%async_computation.13 | async-start | bytes 6488064 | tf_op jit(solution)/shard_map/all_gather | solution.py:167
  8.7 769.3 %all-gather.13.cloned.1.call-start = ((), (), s32[]{:S(2)}) async-start(), calls=%async_computation.8 | async-start | bytes 14155776 | tf_op jit(solution)/shard_map/all_gather | solution.py:222
  8.8 37.6 %copy-start.54 = (f32[128,128]{0,1:T(8,128)}, f32[128,128]{0,1:T(8,128)S(1)}, u32[]{:S(2)}) copy-start(f32[128,128]{0,1:T(8,128)S(1)} %fusion.307) | copy-start | bytes 196612
  11.5 97.7 %copy-start.64 = (pred[64,64]{1,0:T(8,128)(4,1)}, pred[64,64]{1,0:T(8,128)(4,1)S(1)}, u32[]{:S(2)}) copy-start(pred[64,64]{1,0:T(8,128)(4,1)S(1)} %get-tuple-element.1908) | copy-start | bytes 12292
  12.7 31.9 %copy-start.77 = (f32[3,4,64]{2,1,0:T(4,128)}, f32[3,4,64]{2,1,0:T(4,128)S(1)}, u32[]{:S(2)}) copy-start(f32[3,4,64]{2,1,0:T(4,128)S(1)} %get-tuple-element.1892) | copy-start | bytes 9220
  23.1 35.2 %copy-start.102 = (f32[8,1,128]{2,1,0:T(1,128)}, f32[8,1,128]{2,1,0:T(1,128)S(1)}, u32[]{:S(2)}) copy-start(f32[8,1,128]{2,1,0:T(1,128)S(1)} %convert_element_type.268) | copy-start | bytes 12292
  25.5 41.0 %copy-start.100 = (f32[3,256]{1,0:T(4,128)}, f32[3,256]{1,0:T(4,128)S(1)}, u32[]{:S(2)}) copy-start(f32[3,256]{1,0:T(4,128)S(1)} %get-tuple-element.1897) | copy-start | bytes 9220
  35.1 36.9 %copy-start.66 = (f32[1,3072]{1,0:T(1,128)}, f32[1,3072]{1,0:T(1,128)S(1)}, u32[]{:S(2)}) copy-start(f32[1,3072]{1,0:T(1,128)S(1)} %get-tuple-element.1890) | copy-start | bytes 36868
  35.1 36.9 %copy-start.68 = (f32[1,3072]{1,0:T(1,128)}, f32[1,3072]{1,0:T(1,128)S(1)}, u32[]{:S(2)}) copy-start(f32[1,3072]{1,0:T(1,128)S(1)} %get-tuple-element.1889) | copy-start | bytes 36868
  35.1 36.9 %copy-start.70 = (f32[1,3072]{1,0:T(1,128)}, f32[1,3072]{1,0:T(1,128)S(1)}, u32[]{:S(2)}) copy-start(f32[1,3072]{1,0:T(1,128)S(1)} %get-tuple-element.1888) | copy-start | bytes 36868
  43.1 23.4 %copy-start.83 = (bf16[1024,8]{0,1:T(8,128)(2,1)}, bf16[1024,8]{0,1:T(8,128)(2,1)S(1)}, u32[]{:S(2)}) copy-start(bf16[1024,8]{0,1:T(8,128)(2,1)S(1)} %all_gather.39) | copy-start | bytes 49156
  43.2 23.3 %copy-start.92 = (f32[3,256]{1,0:T(4,128)}, f32[3,256]{1,0:T(4,128)S(1)}, u32[]{:S(2)}) copy-start(f32[3,256]{1,0:T(4,128)S(1)} %compare_convert_fusion.3) | copy-start | bytes 9220
  45.4 63.8 %copy-start.30 = (f32[3,4,64,64]{3,2,1,0:T(8,128)}, f32[3,4,64,64]{3,2,1,0:T(8,128)S(1)}, u32[]{:S(2)}) copy-start(f32[3,4,64,64]{3,2,1,0:T(8,128)S(1)} %compare_select_fusion) | copy-start | bytes 589828
  46.4 25.6 %copy-start.75 = (f32[1,3072]{1,0:T(1,128)S(1)}, f32[1,3072]{1,0:T(1,128)}, u32[]{:S(2)}) copy-start(f32[1,3072]{1,0:T(1,128)} %get-tuple-element.1887) | copy-start | bytes 36868
  46.4 25.6 %copy-start.85 = (f32[3,256]{1,0:T(4,128)S(1)}, f32[3,256]{1,0:T(4,128)}, u32[]{:S(2)}) copy-start(f32[3,256]{1,0:T(4,128)} %get-tuple-element.1894) | copy-start | bytes 9220
  46.4 25.6 %copy-start.87 = (f32[3,256]{1,0:T(4,128)S(1)}, f32[3,256]{1,0:T(4,128)}, u32[]{:S(2)}) copy-start(f32[3,256]{1,0:T(4,128)} %get-tuple-element.1895) | copy-start | bytes 9220
  46.4 25.7 %copy-start.89 = (f32[3,256]{1,0:T(4,128)S(1)}, f32[3,256]{1,0:T(4,128)}, u32[]{:S(2)}) copy-start(f32[3,256]{1,0:T(4,128)} %get-tuple-element.1893) | copy-start | bytes 9220
  68.7 3.3 collective-permute-start
  72.0 14.6 copy-start.59
  102.2 509.9 %copy-start.3 = (f32[3,256,1,8,128]{4,3,2,1,0:T(8,128)}, f32[3,256,1,8,128]{4,3,2,1,0:T(8,128)S(1)}, u32[]{:S(2)}) copy-start(f32[3,256,1,8,128]{4,3,2,1,0:T(8,128)S(1)} %get-tuple-element.1878) | copy-start | bytes 9437188
  599.1 13.0 copy-start.11
  599.1 13.0 copy-start.37
  612.1 13.3 copy-start.55
  691.4 151.3 %all-gather.15.cloned.1.call-start = ((), (), s32[]{:S(2)}) async-start(), calls=%async_computation.9 | async-start | bytes 14155776 | tf_op jit(solution)/shard_map/all_gather | solution.py:223
  693.1 17.9 copy-start.42
  693.1 17.9 copy-start.93
  693.1 349.2 %all-gather.17.cloned.1.call-start = ((), (), s32[]{:S(2)}) async-start(), calls=%async_computation.10 | async-start | bytes 2359296 | tf_op jit(solution)/shard_map/all_gather | solution.py:161
  693.7 354.7 %all-gather.21.cloned.1.call-start = ((), (), s32[]{:S(2)}) async-start(), calls=%async_computation.12 | async-start | bytes 6488064 | tf_op jit(solution)/shard_map/all_gather | solution.py:166
  694.3 364.2 %all-gather.19.cloned.1.call-start = ((), (), s32[]{:S(2)}) async-start(), calls=%async_computation.11 | async-start | bytes 6488064 | tf_op jit(solution)/shard_map/all_gather | solution.py:165
  695.1 596.5 %all-gather.25.cloned.1.call-start = ((), (), s32[]{:S(2)}) async-start(), calls=%async_computation.14 | async-start | bytes 7077888 | tf_op jit(solution)/shard_map/all_gather | solution.py:284
  778.0 64.8 %copy-start = (f32[4,3,64,8,128]{4,2,3,1,0:T(8,128)}, f32[4,3,64,8,128]{4,2,3,1,0:T(8,128)S(1)}, u32[]{:S(2)}) copy-start(f32[4,3,64,8,128]{4,2,3,1,0:T(8,128)S(1)} %get-tuple-element.2743) | copy-start | bytes 9437188
  1058.5 17.6 copy-start.109
  1175.8 586.0 %reduce-scatter.14.cloned.1.call-start = ((), (), s32[]{:S(2)}) async-start(), calls=%async_computation.16 | async-start | bytes 2359296 | tf_op jit(solution)/shard_map/reduce_scatter | solution.py:356
  1181.7 580.1 %reduce-scatter.16.cloned.1.call-start = ((), (), s32[]{:S(2)}) async-start(), calls=%async_computation.17 | async-start | bytes 6488064 | tf_op jit(solution)/shard_map/reduce_scatter | solution.py:362
  1190.9 570.9 %reduce-scatter.18.cloned.1.call-start = ((), (), s32[]{:S(2)}) async-start(), calls=%async_computation.18 | async-start | bytes 6488064 | tf_op jit(solution)/shard_map/reduce_scatter | solution.py:365
  1211.6 550.3 %reduce-scatter.20.cloned.1.call-start = ((), (), s32[]{:S(2)}) async-start(), calls=%async_computation.19 | async-start | bytes 6488064 | tf_op jit(solution)/shard_map/reduce_scatter | solution.py:368
  1291.5 530.0 %reduce-scatter.12.cloned.1.call-start = ((), (), s32[]{:S(2)}) async-start(), calls=%async_computation.15 | async-start | bytes 7077888 | tf_op jit(solution)/shard_map/reduce_scatter | solution.py:347
  1397.0 13.5 slice-start.3
  1431.1 13.4 slice-start.3
  1465.1 13.4 slice-start.3
  1498.9 13.4 slice-start.3
  1520.6 12.9 copy-start.20
  1520.6 12.9 copy-start.21
  1561.9 16.0 slice-start
  1562.0 16.0 slice-start.1
  1562.0 16.0 slice-start.2
  1607.7 11.0 copy-start.76
  1729.5 15.3 copy-start.34
  1729.5 15.4 copy-start.101
  1729.5 15.4 copy-start.103
  1741.7 3.2 collective-permute-start.1
  1756.2 117.7 %reduce-scatter.22.cloned.1.call-start = ((), (), s32[]{:S(2)}) async-start(), calls=%async_computation.20 | async-start | bytes 294912
  1758.1 63.4 %copy-start.26 = (f32[3,256,1024]{2,1,0:T(8,128)S(1)}, f32[3,256,1024]{2,1,0:T(8,128)}, u32[]{:S(2)}) copy-start(f32[3,256,1024]{2,1,0:T(8,128)} %copy-done.24) | copy-start | bytes 9437188
  1759.1 138.4 %reduce-scatter.24.cloned.1.call-start = ((), (), s32[]{:S(2)}) async-start(), calls=%async_computation.21 | async-start | bytes 884736
  1760.5 264.9 %all-reduce.14.cloned.1.call-start = ((), (), s32[]{:S(2)}) async-start(), calls=%async_computation.22 | async-start | bytes 6422528 | tf_op jit(solution)/shard_map/psum | solution.py:374
  1821.6 49.0 %copy-start.84 = (bf16[1024,8]{0,1:T(8,128)(2,1)S(1)}, bf16[1024,8]{0,1:T(8,128)(2,1)}, u32[]{:S(2)}) copy-start(bf16[1024,8]{0,1:T(8,128)(2,1)} %copy-done.83) | copy-start | bytes 49156
  1898.5 14.2 copy-start.107
  1898.5 42.6 %copy-start.29 = (f32[3,256,1024]{2,1,0:T(8,128)S(1)}, f32[3,256,1024]{2,1,0:T(8,128)}, u32[]{:S(2)}) copy-start(f32[3,256,1024]{2,1,0:T(8,128)} %copy-done.28) | copy-start | bytes 9437188
  1898.5 42.6 %copy-start.99 = (f32[3,256]{1,0:T(4,128)S(1)}, f32[3,256]{1,0:T(4,128)}, u32[]{:S(2)}) copy-start(f32[3,256]{1,0:T(4,128)} %get-tuple-element.1896) | copy-start | bytes 9220
  (103 other events, 591.1 us)
Sparse Core Ops, SparseCore 0:
  9.9 48.3 all-gather.10
  60.2 43.7 all-gather.22
  691.6 76.6 all-gather.12
  770.6 72.1 all-gather.14
  844.5 27.8 all-gather.16
  874.2 43.3 all-gather.20
  919.4 43.3 all-gather.18
  1175.9 45.2 all-gather.24
  1224.4 41.2 reduce-scatter.13
  1269.4 59.0 reduce-scatter.15
  1331.9 59.0 reduce-scatter.17
  1394.6 59.0 reduce-scatter.19
  1756.3 65.2 reduce-scatter.11
  1825.3 33.5 reduce-scatter.21
  1862.5 34.9 reduce-scatter.23
  1900.1 125.1 all-reduce.13
where the time goes:
time: 2050 us; the launch traced here: 2040 us
  matrix products  667 us (33%)
  other arithmetic  640 us (31%)
  local copies, waits for them, and re-layouts  348 us (17%)
  waiting for transfers between devices  244 us (12%)
  blocking collectives  106 us (5%)
    another operation x5, other arithmetic, block_weights(): jax.scipy.linalg.solve_triangular(system, jnp.swapaxes(right_side, -3, -2...  477 us
    dot_general x16, matrix products, matmul(): return jnp.einsum('...ij,...jk->...ik', left, right, precision=PRECISE)  83.6 us
    dot_general x20, matrix products, block_apply(): jnp.einsum('...hcd,...hed->...hce', weight_keys, memory, precision=PRECISE)  83.5 us
    psum x1, waiting for transfers between devices, on_device(): lax.psum(shards[1].astype(jnp.bfloat16), 'row').astype(jnp.float32)  79.8 us
    dot_general x20, matrix products, block_apply(): jnp.einsum('...hce,...chd->...hed', fresh, last_keys, precision=PRECISE)  75.9 us
    dynamic_slice x48, local copies, waits for them, and re-layouts, on_device(): lax.scan(forward_step, zero_state, (device_order, all_decay, all_write))  71.7 us
    all_gather x1, waiting for transfers between devices, on_device(): lax.all_gather(dev_write, 'seq', axis=0, tiled=True)  64.8 us
    dot_general x16, matrix products, block_apply(): jnp.einsum('...thd,...hed->...the', queries, memory, precision=PRECISE)  61.2 us
  transfers between devices with their start and end apart: 18, of which 6 were waited for; matrix products, arithmetic and copies ran while one was open for 74% of the time, Pallas kernels for 0%

commit v1 on v0

v1 whole, which is shorter than its diff:
```python
import functools

import jax
import jax.numpy as jnp
from jax import lax
from jax.experimental import pallas as pl
from jax.experimental.pallas import tpu as pltpu
from jax.sharding import PartitionSpec as P

EPSILON = 1e-06
LOW = jnp.bfloat16
WIDE = jnp.float32
HEADS_STEP = 4
RIM = 8
VMEM_BYTES = 56 * 1024 * 1024


def nn(left, right):
    return lax.dot_general(
        left.astype(LOW), right.astype(LOW), (((1,), (0,)), ((), ())), preferred_element_type=WIDE
    )


def nt(left, right):
    return lax.dot_general(
        left.astype(LOW), right.astype(LOW), (((1,), (1,)), ((), ())), preferred_element_type=WIDE
    )


def tn(left, right):
    return lax.dot_general(
        left.astype(LOW), right.astype(LOW), (((0,), (0,)), ((), ())), preferred_element_type=WIDE
    )


def split(value):
    high = value.astype(LOW)
    return high, (value - high.astype(WIDE)).astype(LOW)


def nn_fine(left, right):
    left_high, left_low = split(left)
    right_high, right_low = split(right)
    return nn(left_high, right_high) + nn(left_high, right_low) + nn(left_low, right_high)


def rms_scale(values):
    return lax.rsqrt(jnp.mean(values * values, axis=-1, keepdims=True) + EPSILON)


def windows_of(rim, block, taps):
    size = block.shape[0]
    joined = jnp.concatenate([rim, block], axis=0)
    return [block] + [
        pltpu.roll(joined, step, axis=0)[RIM : RIM + size] for step in range(1, taps)
    ]


def convolve(windows, weights, tap_masks):
    total = weights[0:1] * windows[0]
    for step in range(1, len(windows)):
        total = total + weights[step : step + 1] * (windows[step] * tap_masks[step - 1])
    return total


def pair_distance(size):
    row = lax.broadcasted_iota(jnp.int32, (size, size), 0)
    column = lax.broadcasted_iota(jnp.int32, (size, size), 1)
    return row, column


def inverse_unit_lower(strict, row, column):
    size = strict.shape[0]
    apart = row ^ column
    eye = (row == column).astype(WIDE)
    strict_low = strict.astype(LOW)
    result = eye - jnp.where(apart == 1, strict, 0.0)
    level = 1
    while (1 << level) < size:
        corner = jnp.where((apart >> level) == 1, strict, 0.0)
        result_low = result.astype(LOW)
        result = result - nn(result_low, nn(corner, result_low))
        level += 1
    if REFINE:
        result_high, result_rest = split(result)
        rest = (
            eye
            - result
            - nn(strict_low, result_high)
            - nn(strict_low, result_rest)
            - nn(strict - strict_low.astype(WIDE), result_high)
        )
        result = result + nn(result_high, rest)
    return result


REFINE = True


def unit_and_scale(values):
    scale = lax.rsqrt(jnp.sum(values * values, axis=-1, keepdims=True) + EPSILON)
    return values * scale, scale


def head_masks(cols, rows):
    doc_col, doc_row = cols[:, 0:1], rows[0:1, :]
    size = cols.shape[0]
    row, column = pair_distance(size)
    same = doc_col == doc_row
    inclusive = same & (row >= column)
    strict = same & (row > column)
    tap_masks = [cols[:, 1:2], cols[:, 2:3], cols[:, 3:4]]
    return row, column, inclusive, strict, tap_masks, cols[:, 4:5], cols[:, 5:6]


def pick_head(table, head):
    lane = lax.broadcasted_iota(jnp.int32, table.shape, 1)
    return jnp.sum(jnp.where(lane == head, table, 0.0), axis=1, keepdims=True)


def prepare_kernel(
    cols_ref, rows_ref, beta_ref, taps_q, taps_k, taps_v, rim_q, rim_k, rim_v, in_q, in_k, in_v,
    eff_ref, local_ref, maps_ref, solve_ref, weights_ref,
):
    cols, rows = cols_ref[0], rows_ref[0]
    row, column, inclusive, strict, tap_masks, carried, last = head_masks(cols, rows)
    beta_all = beta_ref[0]
    tap_count = taps_q.shape[0]
    for local in range(HEADS_STEP):
        head = pl.program_id(1) * HEADS_STEP + local
        lanes = slice(local * 128, (local + 1) * 128)
        acts = []
        for taps, rim, block in ((taps_q, rim_q, in_q), (taps_k, rim_k, in_k), (taps_v, rim_v, in_v)):
            windows = windows_of(
                rim[0, :, lanes].astype(WIDE), block[0, :, lanes].astype(WIDE), tap_count
            )
            acts.append(jax.nn.silu(convolve(windows, taps[:, lanes].astype(WIDE), tap_masks)))
        query = unit_and_scale(acts[0])[0]
        key = unit_and_scale(acts[1])[0]
        value = acts[2]
        beta = pick_head(beta_all, head)
        gram = nt(jnp.concatenate([key, query], axis=0), key)
        size = key.shape[0]
        system = jnp.where(strict, gram[:size] * beta, 0.0)
        scores = jnp.where(inclusive, gram[size:], 0.0)
        solve = inverse_unit_lower(system, row, column).astype(LOW)
        right = jnp.concatenate([(beta * carried) * key, beta * value], axis=1)
        weights = nn(solve, right).astype(LOW)
        mixed = nn(scores, weights)
        eff_ref[0, local] = (carried * query - mixed[:, :128]).astype(LOW)
        local_ref[0, :, lanes] = mixed[:, 128:]
        maps_ref[0, local] = tn(last * key, weights).astype(LOW)
        solve_ref[0, local] = solve
        weights_ref[0, local] = weights


def prepare_call(cols, rows, beta, taps, rim, projected):
    row_count, size, triple = projected.shape
    head_count = triple // (3 * 128)
    groups = head_count // HEADS_STEP
    wide = HEADS_STEP * 128
    tap_count = taps.shape[0]

    def of_row(block):
        return pl.BlockSpec(block, lambda r, g: (r, 0, 0))

    def part(rows_in, index):
        return pl.BlockSpec((1, rows_in, wide), lambda r, g: (r, 0, index * groups + g))

    def tap_part(index):
        return pl.BlockSpec((tap_count, wide), lambda r, g: (0, index * groups + g))

    def per_head(*block):
        return pl.BlockSpec((1, HEADS_STEP) + block, lambda r, g: (r, g, 0, 0))

    return pl.pallas_call(
        prepare_kernel,
        grid=(row_count, groups),
        in_specs=[of_row((1,) + cols.shape[1:]), of_row((1,) + rows.shape[1:]), of_row((1,) + beta.shape[1:])]
        + [tap_part(i) for i in range(3)]
        + [part(RIM, i) for i in range(3)]
        + [part(size, i) for i in range(3)],
        out_specs=[
            per_head(size, 128),
            pl.BlockSpec((1, size, wide), lambda r, g: (r, 0, g)),
            per_head(128, 256),
            per_head(size, size),
            per_head(size, 256),
        ],
        out_shape=[
            jax.ShapeDtypeStruct((row_count, head_count, size, 128), LOW),
            jax.ShapeDtypeStruct((row_count, size, head_count * 128), WIDE),
            jax.ShapeDtypeStruct((row_count, head_count, 128, 256), LOW),
            jax.ShapeDtypeStruct((row_count, head_count, size, size), LOW),
            jax.ShapeDtypeStruct((row_count, head_count, size, 256), LOW),
        ],
        compiler_params=pltpu.CompilerParams(vmem_limit_bytes=VMEM_BYTES),
        name="prepare",
    )(cols, rows, beta, taps, taps, taps, rim, rim, rim, projected, projected, projected)


def chain_forward_kernel(keep_ref, maps_ref, out_ref):
    count, pairs = maps_ref.shape[0], maps_ref.shape[1]
    states = [jnp.zeros((128, 128), WIDE) for _ in range(pairs)]
    for device in range(count):
        for pair in range(pairs):
            state = states[pair]
            out_ref[device, pair] = state.astype(LOW)
            decay = maps_ref[device, pair, :, :128]
            write = maps_ref[device, pair, :, 128:]
            states[pair] = (
                keep_ref[pair, device] * state - nn(decay, state) + write.astype(WIDE)
            )


def chain_backward_kernel(keep_ref, maps_ref, grads_ref, out_ref):
    count, pairs = maps_ref.shape[0], maps_ref.shape[1]
    states = [jnp.zeros((128, 128), WIDE) for _ in range(pairs)]
    for device in reversed(range(count)):
        for pair in range(pairs):
            state = states[pair]
            out_ref[device, pair] = state.astype(LOW)
            decay = maps_ref[device, pair, :, :128]
            states[pair] = (
                keep_ref[pair, device] * state
                - tn(decay, state)
                + grads_ref[device, pair].astype(WIDE)
            )


def chain_call(kernel, keep, *arrays):
    count, pairs = arrays[0].shape[:2]
    return pl.pallas_call(
        kernel,
        in_specs=[pl.BlockSpec(memory_space=pltpu.SMEM)]
        + [pl.BlockSpec(memory_space=pltpu.VMEM) for _ in arrays],
        out_specs=pl.BlockSpec(memory_space=pltpu.VMEM),
        out_shape=jax.ShapeDtypeStruct((count, pairs, 128, 128), LOW),
        compiler_params=pltpu.CompilerParams(vmem_limit_bytes=VMEM_BYTES),
        name="chain",
    )(keep, *arrays)


def exchange(value, count):
    pairs = value.shape[0]
    share = -(-pairs // count)
    padded = jnp.pad(value, ((0, share * count - pairs),) + ((0, 0),) * (value.ndim - 1))
    cut = padded.reshape((count, share) + value.shape[1:])
    return lax.all_to_all(cut, "seq", split_axis=0, concat_axis=0)


def to_home(value, pairs):
    moved = lax.all_to_all(value, "seq", split_axis=0, concat_axis=0)
    return moved.reshape((-1,) + value.shape[2:])[:pairs]


def read_kernel(eff_ref, local_ref, state_ref, out_ref):
    for local in range(HEADS_STEP):
        lanes = slice(local * 128, (local + 1) * 128)
        out_ref[0, :, lanes] = (
            local_ref[0, :, lanes] + nn(eff_ref[0, local], state_ref[0, local])
        ).astype(LOW)


def read_call(eff, local, state):
    row_count, size, width = local.shape
    groups = width // (128 * HEADS_STEP)
    wide = HEADS_STEP * 128
    return pl.pallas_call(
        read_kernel,
        grid=(row_count, groups),
        in_specs=[
            pl.BlockSpec((1, HEADS_STEP, size, 128), lambda r, g: (r, g, 0, 0)),
            pl.BlockSpec((1, size, wide), lambda r, g: (r, 0, g)),
            pl.BlockSpec((1, HEADS_STEP, 128, 128), lambda r, g: (r, g, 0, 0)),
        ],
        out_specs=pl.BlockSpec((1, size, wide), lambda r, g: (r, 0, g)),
        out_shape=jax.ShapeDtypeStruct((row_count, size, width), LOW),
        compiler_params=pltpu.CompilerParams(vmem_limit_bytes=VMEM_BYTES),
        name="read",
    )(eff, local, state)


def pull_read_kernel(eff_ref, grad_ref, out_ref):
    for local in range(HEADS_STEP):
        lanes = slice(local * 128, (local + 1) * 128)
        out_ref[0, local] = tn(eff_ref[0, local], grad_ref[0, :, lanes]).astype(LOW)


def pull_read_call(eff, grad):
    row_count, size, width = grad.shape
    groups = width // (128 * HEADS_STEP)
    wide = HEADS_STEP * 128
    return pl.pallas_call(
        pull_read_kernel,
        grid=(row_count, groups),
        in_specs=[
            pl.BlockSpec((1, HEADS_STEP, size, 128), lambda r, g: (r, g, 0, 0)),
            pl.BlockSpec((1, size, wide), lambda r, g: (r, 0, g)),
        ],
        out_specs=pl.BlockSpec((1, HEADS_STEP, 128, 128), lambda r, g: (r, g, 0, 0)),
        out_shape=jax.ShapeDtypeStruct((row_count, width // 128, 128, 128), LOW),
        compiler_params=pltpu.CompilerParams(vmem_limit_bytes=VMEM_BYTES),
        name="pull_read",
    )(eff, grad)


def back_kernel(
    cols_ref, rows_ref, beta_ref, taps_q, taps_k, taps_v, rim_q, rim_k, rim_v, in_q, in_k, in_v,
    solve_ref, weights_ref, state_ref, exit_ref, grad_ref,
    out_q, out_k, out_v, edge_q, edge_k, edge_v, tail_q, tail_k, tail_v, tap_q, tap_k, tap_v, rate_ref,
):
    cols, rows = cols_ref[0], rows_ref[0]
    row, column, inclusive, strict, tap_masks, carried, last = head_masks(cols, rows)
    beta_all = beta_ref[0]
    tap_count = taps_q.shape[0]

    @pl.when(pl.program_id(1) == 0)
    def _():
        rate_ref[0] = jnp.zeros(rate_ref.shape[1:], WIDE)

    for local in range(HEADS_STEP):
        head = pl.program_id(1) * HEADS_STEP + local
        lanes = slice(local * 128, (local + 1) * 128)
        moved, acts, slopes = [], [], []
        for taps, rim, block in ((taps_q, rim_q, in_q), (taps_k, rim_k, in_k), (taps_v, rim_v, in_v)):
            windows = windows_of(
                rim[0, :, lanes].astype(WIDE), block[0, :, lanes].astype(WIDE), tap_count
            )
            convolved = convolve(windows, taps[:, lanes].astype(WIDE), tap_masks)
            gate = jax.nn.sigmoid(convolved)
            moved.append(windows)
            acts.append(convolved * gate)
            slopes.append(gate * (1.0 + convolved * (1.0 - gate)))
        query, query_scale = unit_and_scale(acts[0])
        key, key_scale = unit_and_scale(acts[1])
        value = acts[2]
        beta = pick_head(beta_all, head)
        size = key.shape[0]
        state = state_ref[0, local]
        exit_grad = exit_ref[0, local]
        grad_out = grad_ref[0, :, lanes]
        query_low, key_low, grad_low = query.astype(LOW), key.astype(LOW), grad_out.astype(LOW)
        both = jnp.concatenate([key_low, query_low], axis=0)
        gram = nt(both, key_low)
        scores = jnp.where(inclusive, gram[size:], 0.0)
        solve = solve_ref[0, local]
        weights = weights_ref[0, local]
        fresh = weights[:, 128:].astype(WIDE) - nn(weights[:, :128], state)
        fresh_low = fresh.astype(LOW)
        grad_fresh = tn(scores, grad_low) + last * nn(key_low, exit_grad)
        grad_right = tn(solve, grad_fresh)
        right_low = grad_right.astype(LOW)
        sides = jnp.concatenate([right_low, grad_low], axis=0)
        outer = nt(sides, fresh_low)
        grad_system = jnp.where(strict, -outer[:size], 0.0)
        grad_scores = jnp.where(inclusive, outer[size:], 0.0)
        grad_rate = jnp.sum(grad_system * gram[:size], axis=1, keepdims=True)
        grad_gram = beta * grad_system
        grads = jnp.concatenate([grad_gram.astype(LOW), grad_scores.astype(LOW)], axis=0)
        by_key = nn(grads, key_low)
        by_state = nt(sides, state)
        residual = value - carried * nn(key_low, state)
        grad_rate = grad_rate + jnp.sum(grad_right * residual, axis=1, keepdims=True)
        grad_query = carried * by_state[size:] + by_key[size:]
        grad_key = (
            by_key[:size]
            + tn(grads, both)
            + last * nt(fresh_low, exit_grad)
            - (beta * carried) * by_state[:size]
        )
        grad_value = beta * grad_right
        grad_query = query_scale * (
            grad_query - query * jnp.sum(query * grad_query, axis=1, keepdims=True)
        )
        grad_key = key_scale * (grad_key - key * jnp.sum(key * grad_key, axis=1, keepdims=True))
        lane = lax.broadcasted_iota(jnp.int32, rate_ref.shape[1:], 1)
        rate_ref[0] = jnp.where(lane == head, grad_rate, rate_ref[0])
        zeros = jnp.zeros((RIM, 128), WIDE)
        for index, (grad_act, taps, out, edge, tail, tap_out) in enumerate(
            (
                (grad_query, taps_q, out_q, edge_q, tail_q, tap_q),
                (grad_key, taps_k, out_k, edge_k, tail_k, tap_k),
                (grad_value, taps_v, out_v, edge_v, tail_v, tap_v),
            )
        ):
            grad_conv = grad_act * slopes[index]
            weight = taps[:, lanes].astype(WIDE)
            own = weight[0:1] * grad_conv
            edge_sum = zeros
            tap_out[0, 0:1, lanes] = jnp.sum(grad_conv * moved[index][0], axis=0, keepdims=True)
            for step in range(1, tap_count):
                masked = grad_conv * tap_masks[step - 1]
                tap_out[0, step : step + 1, lanes] = jnp.sum(
                    masked * moved[index][step], axis=0, keepdims=True
                )
                joined = jnp.concatenate([zeros, weight[step : step + 1] * masked], axis=0)
                back = pltpu.roll(joined, size + RIM - step, axis=0)
                own = own + back[RIM:]
                edge_sum = edge_sum + back[:RIM]
            out[0, :, lanes] = own.astype(LOW)
            edge[0, :, lanes] = edge_sum
            tail[0, :, lanes] = own[size - RIM :]


def back_call(cols, rows, beta, taps, rim, projected, solve, weights, state, exit_grad, grad):
    row_count, size, triple = projected.shape
    head_count = triple // (3 * 128)
    groups = head_count // HEADS_STEP
    wide = HEADS_STEP * 128
    width = triple // 3
    tap_count = taps.shape[0]

    def of_row(block):
        return pl.BlockSpec(block, lambda r, g: (r, 0, 0))

    def part(rows_in, index):
        return pl.BlockSpec((1, rows_in, wide), lambda r, g: (r, 0, index * groups + g))

    def tap_part(index):
        return pl.BlockSpec((tap_count, wide), lambda r, g: (0, index * groups + g))

    def per_head(*block):
        return pl.BlockSpec((1, HEADS_STEP) + block, lambda r, g: (r, g, 0, 0))

    return pl.pallas_call(
        back_kernel,
        grid=(row_count, groups),
        in_specs=[of_row((1,) + cols.shape[1:]), of_row((1,) + rows.shape[1:]), of_row((1,) + beta.shape[1:])]
        + [tap_part(i) for i in range(3)]
        + [part(RIM, i) for i in range(3)]
        + [part(size, i) for i in range(3)]
        + [per_head(size, size), per_head(size, 256), per_head(128, 128), per_head(128, 128), part(size, 0)],
        out_specs=[part(size, 0)] * 3
        + [part(RIM, 0)] * 6
        + [pl.BlockSpec((1, tap_count, wide), lambda r, g: (r, 0, g))] * 3
        + [of_row((1, size, 128))],
        out_shape=[jax.ShapeDtypeStruct((row_count, size, width), LOW)] * 3
        + [jax.ShapeDtypeStruct((row_count, RIM, width), WIDE)] * 6
        + [jax.ShapeDtypeStruct((row_count, tap_count, width), WIDE)] * 3
        + [jax.ShapeDtypeStruct((row_count, size, 128), WIDE)],
        compiler_params=pltpu.CompilerParams(vmem_limit_bytes=VMEM_BYTES),
        name="mixer_back",
    )(
        cols, rows, beta, taps, taps, taps, rim, rim, rim, projected, projected, projected,
        solve, weights, state, exit_grad, grad,
    )


def shifted(value, axis, steps):
    count = lax.axis_size(axis)
    leading, last = (max(0, -steps), min(count, count - steps))
    return lax.ppermute(value, axis, [(source, source + steps) for source in range(leading, last)])


def on_device(
    inputs,
    lengths,
    norm_gain,
    w_qkv,
    w_beta,
    beta_bias,
    w_conv,
    w_out,
    ffn_gain,
    w_gate,
    w_up,
    w_down,
    cotangent,
):
    row_count, slot_count, width = inputs.shape
    head_count = beta_bias.shape[0]
    tap_count = w_conv.shape[0]
    rim_size = tap_count - 1
    pairs = row_count * head_count
    seq_count = lax.axis_size("seq")
    position = lax.axis_index("seq")
    gather = functools.partial(lax.all_gather, axis_name="seq", tiled=True)
    full_qkv = gather(w_qkv, axis=0)
    small = jnp.concatenate(
        [norm_gain, ffn_gain, w_beta.reshape(-1), w_conv.reshape(-1)], axis=0
    )
    all_small = lax.all_gather(small, "seq", axis=0)
    shard = norm_gain.shape[0]
    full_gain = all_small[:, :shard].reshape(-1)
    full_ffn_gain = all_small[:, shard : 2 * shard].reshape(-1)
    full_beta = all_small[:, 2 * shard : (2 + head_count) * shard].reshape(-1, head_count)
    full_conv = jnp.swapaxes(
        all_small[:, (2 + head_count) * shard :].reshape(seq_count, tap_count, -1), 0, 1
    ).reshape(tap_count, -1)
    full_out = gather(w_out, axis=0)
    full_gate = gather(w_gate, axis=0)
    full_up = gather(w_up, axis=0)
    full_down = gather(w_down, axis=0)

    doc_ends = jnp.cumsum(lengths, axis=1, dtype=jnp.int32)
    spots = position * slot_count - rim_size + jnp.arange(slot_count + rim_size, dtype=jnp.int32)
    ext_docs = jnp.sum(
        (spots[None, :, None] >= doc_ends[:, None, :]).astype(jnp.int32), axis=2, dtype=jnp.int32
    )
    ext_docs = jnp.where(spots[None, :] < 0, -1, ext_docs)
    own_docs = ext_docs[:, rim_size:]
    valid_mask = (spots[None, rim_size:] < doc_ends[:, -1:]).astype(WIDE)
    mask_col = valid_mask[..., None]
    shown = [own_docs.astype(WIDE)]
    for offset in range(1, tap_count):
        before = ext_docs[:, rim_size - offset : rim_size - offset + slot_count]
        shown.append((before == own_docs).astype(WIDE))
    shown.append((own_docs == ext_docs[:, rim_size - 1 : rim_size]).astype(WIDE))
    shown.append((own_docs == own_docs[:, -1:]).astype(WIDE))
    shown += [valid_mask, valid_mask]
    cols = jnp.stack(shown, axis=-1)
    rows = jnp.broadcast_to(own_docs.astype(WIDE)[:, None, :], (row_count, 8, slot_count))
    bounds = jnp.arange(seq_count, dtype=jnp.int32) * slot_count
    doc_first = jnp.sum((bounds[None, :, None] - 1 >= doc_ends[:, None, :]).astype(jnp.int32), axis=2)
    doc_last = jnp.sum(
        (bounds[None, :, None] + slot_count - 1 >= doc_ends[:, None, :]).astype(jnp.int32), axis=2
    )
    keep = (doc_first == doc_last).astype(WIDE)
    share = -(-pairs // seq_count)
    keep_pairs = jnp.pad(
        jnp.repeat(keep, head_count, axis=0), ((0, share * seq_count - pairs), (0, 0))
    )
    keep_own = lax.dynamic_slice_in_dim(keep_pairs, position * share, share, axis=0)

    wide_inputs = inputs.astype(WIDE)
    first_scale = rms_scale(wide_inputs)
    normed = (wide_inputs * first_scale * full_gain).astype(LOW)
    projected = jnp.dot(normed, full_qkv, preferred_element_type=WIDE).astype(LOW)
    logits = jnp.dot(normed, full_beta, preferred_element_type=WIDE) + beta_bias.astype(WIDE)
    beta_open = jax.nn.sigmoid(logits)
    beta_rate = mask_col * beta_open
    rim_rows = shifted(projected[:, slot_count - rim_size :], "seq", 1)
    rim = jnp.pad(rim_rows, ((0, 0), (RIM - rim_size, 0), (0, 0)))

    eff, local_out, maps, solve, weights = prepare_call(
        cols, rows, beta_rate, full_conv, rim, projected
    )
    maps_here = exchange(maps.reshape((pairs,) + maps.shape[2:]), seq_count)
    states_here = chain_call(chain_forward_kernel, keep_own, maps_here)
    state = to_home(states_here, pairs).reshape((row_count, head_count, 128, 128))
    heads_low = read_call(eff, local_out, state)

    hidden = wide_inputs + jnp.dot(heads_low, full_out, preferred_element_type=WIDE)
    second_scale = rms_scale(hidden)
    second = (hidden * second_scale * full_ffn_gain).astype(LOW)
    gated = jnp.dot(second, full_gate, preferred_element_type=WIDE)
    lifted = jnp.dot(second, full_up, preferred_element_type=WIDE)
    activated = (jax.nn.silu(gated) * lifted).astype(LOW)
    output = (
        mask_col * (hidden + jnp.dot(activated, full_down, preferred_element_type=WIDE))
    ).astype(LOW)
    upstream = cotangent.astype(WIDE) * mask_col
    upstream_low = upstream.astype(LOW)
    grad_act = jnp.einsum("rsd,fd->rsf", upstream_low, full_down, preferred_element_type=WIDE)
    sigmoid_gate = jax.nn.sigmoid(gated)
    grad_gated = (grad_act * lifted * sigmoid_gate * (1.0 + gated * (1.0 - sigmoid_gate))).astype(LOW)
    grad_lifted = (grad_act * gated * sigmoid_gate).astype(LOW)
    grad_second = jnp.einsum(
        "rsf,df->rsd", grad_gated, full_gate, preferred_element_type=WIDE
    ) + jnp.einsum("rsf,df->rsd", grad_lifted, full_up, preferred_element_type=WIDE)
    grad_ffn_gain = jnp.sum(grad_second * hidden * second_scale, axis=(0, 1))
    scaled_second = full_ffn_gain.astype(WIDE) * grad_second
    grad_hidden = (
        upstream
        + second_scale * scaled_second
        - hidden * second_scale**3 * jnp.mean(scaled_second * hidden, axis=-1, keepdims=True)
    )
    grad_mix_low = grad_hidden.astype(LOW)
    grad_heads = jnp.einsum("rse,de->rsd", grad_mix_low, full_out, preferred_element_type=WIDE)
    grad_heads = grad_heads.astype(LOW)

    local_grad = pull_read_call(eff, grad_heads)
    grads_here = exchange(local_grad.reshape((pairs, 128, 128)), seq_count)
    exits_here = chain_call(chain_backward_kernel, keep_own, maps_here, grads_here)
    exit_grad = to_home(exits_here, pairs).reshape((row_count, head_count, 128, 128))

    scatter = functools.partial(lax.psum_scatter, axis_name="seq", scatter_dimension=0, tiled=True)
    grad_down = jnp.einsum("rsf,rsd->fd", activated, upstream_low, preferred_element_type=WIDE)
    grad_gate_w = jnp.einsum("rsd,rsf->df", second, grad_gated, preferred_element_type=WIDE)
    grad_up_w = jnp.einsum("rsd,rsf->df", second, grad_lifted, preferred_element_type=WIDE)
    grad_out_w = jnp.einsum("rsd,rse->de", heads_low, grad_mix_low, preferred_element_type=WIDE)
    shard_down = scatter(grad_down.astype(LOW))
    shard_gate = scatter(grad_gate_w.astype(LOW))
    shard_up = scatter(grad_up_w.astype(LOW))
    shard_out = scatter(grad_out_w.astype(LOW))

    pulled = back_call(
        cols, rows, beta_rate, full_conv, rim, projected, solve, weights, state, exit_grad, grad_heads
    )
    grad_parts, edges, tails, tap_sums, rate = (
        pulled[0:3], pulled[3:6], pulled[6:9], pulled[9:12], pulled[12]
    )
    back_rim = shifted(
        jnp.concatenate([edge[:, RIM - rim_size :] for edge in edges], axis=-1).astype(LOW), "seq", -1
    ).astype(WIDE)
    fixed = []
    for index in range(3):
        tail = tails[index][:, RIM - rim_size :] + back_rim[:, :, index * width : (index + 1) * width]
        fixed.append(
            lax.dynamic_update_slice(
                grad_parts[index], tail.astype(LOW), (0, slot_count - rim_size, 0)
            )
        )
    grad_conv_w = jnp.concatenate([jnp.sum(tap, axis=0) for tap in tap_sums], axis=-1)
    grad_logits = rate[:, :, :head_count] * beta_rate * (1.0 - beta_open)

    grad_qkv_w = [
        jnp.einsum("rsd,rse->de", normed, part, preferred_element_type=WIDE) for part in fixed
    ]
    shard_qkv = jnp.concatenate([scatter(part.astype(LOW)) for part in grad_qkv_w], axis=-1)
    grad_beta_w = jnp.einsum(
        "rsd,rsh->dh", normed.astype(WIDE), grad_logits, precision=lax.Precision.HIGHEST
    )
    bias_local = jnp.sum(grad_logits, axis=(0, 1))
    grad_normed = jnp.einsum(
        "rsh,dh->rsd", grad_logits, full_beta.astype(WIDE), precision=lax.Precision.HIGHEST
    )
    for index in range(3):
        grad_normed = grad_normed + jnp.einsum(
            "rse,de->rsd",
            fixed[index],
            full_qkv[:, index * width : (index + 1) * width],
            preferred_element_type=WIDE,
        )
    grad_norm_gain = jnp.sum(grad_normed * wide_inputs * first_scale, axis=(0, 1))
    scaled_first = full_gain.astype(WIDE) * grad_normed
    grad_inputs = (
        grad_hidden
        + first_scale * scaled_first
        - wide_inputs
        * first_scale**3
        * jnp.mean(scaled_first * wide_inputs, axis=-1, keepdims=True)
    )
    minor = jnp.concatenate(
        [
            grad_norm_gain.reshape(seq_count, -1),
            grad_ffn_gain.reshape(seq_count, -1),
            grad_beta_w.reshape(seq_count, -1),
            jnp.swapaxes(grad_conv_w.reshape(tap_count, seq_count, -1), 0, 1).reshape(seq_count, -1),
            jnp.broadcast_to(bias_local[None], (seq_count, head_count)),
        ],
        axis=1,
    )
    minor_total = lax.psum(lax.psum_scatter(minor, "seq", scatter_dimension=0, tiled=True), "row")[0]
    total = [
        lax.psum(shard, "row").astype(WIDE)
        for shard in (shard_qkv, shard_out, shard_gate, shard_up, shard_down)
    ]
    cuts = [shard, 2 * shard, (2 + head_count) * shard, minor_total.shape[0] - head_count]
    return (
        output,
        grad_inputs.astype(LOW),
        minor_total[: cuts[0]],
        total[0],
        minor_total[cuts[1] : cuts[2]].reshape(shard, head_count),
        minor_total[cuts[3] :],
        minor_total[cuts[2] : cuts[3]].reshape(tap_count, -1),
        total[1],
        minor_total[cuts[0] : cuts[1]],
        total[2],
        total[3],
        total[4],
    )


def solution(mesh):
    placed = (
        P("row", "seq", None),
        P("row", None),
        P("seq"),
        P("seq", None),
        P("seq", None),
        P(),
        P(None, "seq"),
        P("seq", None),
        P("seq"),
        P("seq", None),
        P("seq", None),
        P("seq", None),
        P("row", "seq", None),
    )
    return jax.shard_map(
        on_device,
        mesh=mesh,
        in_specs=placed,
        out_specs=(
            P("row", "seq", None),
            P("row", "seq", None),
            P("seq"),
            P("seq", None),
            P("seq", None),
            P(),
            P(None, "seq"),
            P("seq", None),
            P("seq"),
            P("seq", None),
            P("seq", None),
            P("seq", None),
        ),
        check_vma=False,
    )
```

time: 2050 us -> 964 us (0.47)
  other arithmetic: 640 us -> 19.7 us
  matrix products: 667 us -> 148 us
  local copies, waits for them, and re-layouts: 348 us -> 36.3 us
  waiting for transfers between devices: 244 us -> 514 us
  Pallas kernels: 0 us -> 148 us
  blocking collectives: 106 us -> 63.6 us
    dot_general x136 -> x18, matrix products: 617 us -> 118 us  [the longest x1 17.4 us: on_device(): gated = jnp.dot(second, full_gate, preferred_element_type=WIDE)]
    another operation x6 -> x1, other arithmetic: 477 us -> 0.67 us  [on_device(): cols = jnp.stack(shown, axis=-1)]
    reduce_scatter x5 -> x7, waiting for transfers between devices: 59.8 us -> 292 us  [the longest x1 62.9 us: on_device(): shard_up = scatter(grad_up_w.astype(LOW))]
    pallas_call x0 -> x6, Pallas kernels: none -> 148 us  [the longest x1 89.8 us: prepare_call(): pl.pallas_call(prepare_kernel, grid=(row_count, groups), in_specs=[of_row...]
    dynamic_slice x56 -> x1, local copies, waits for them, and re-layouts: 79.6 us -> 0.59 us  [on_device(): lax.dynamic_slice_in_dim(keep_pairs, position * share, share, axis=0)]
    while x114 -> x0, local copies, waits for them, and re-layouts: 56 us -> none
    scatter-add x3 -> x0, local copies, waits for them, and re-layouts: 51.1 us -> none  [on_device(): grad_ext.at[:, rim_size - offset:rim_size - offset + slot_count]]
    all_gather x8 -> x5, waiting for transfers between devices: 76.8 us -> 32 us  [the longest x1 32 us: on_device(): full_qkv = gather(w_qkv, axis=0)]
  transfers between devices with their start and end apart: 18 -> 18, of which waited for: 6 -> 12; matrix products, arithmetic and copies ran while one was open for 74% -> 15% of each run, Pallas kernels for 0% -> 10%
where the time goes in v1:
time: 964 us; the launch traced here: 958 us
  waiting for transfers between devices  514 us (53%)
  matrix products  148 us (15%)
  Pallas kernels  148 us (15%)
  blocking collectives  63.6 us (7%)
  local copies, waits for them, and re-layouts  36.3 us (4%)
  other arithmetic  19.7 us (2%)
  between operations  14.9 us (2%)
  starting transfers between devices  12.7 us (1%)
    psum x1, waiting for transfers between devices, on_device(): lax.psum(shard, 'row').astype(WIDE)  106 us
    pallas_call x1, Pallas kernels, prepare_call(): pl.pallas_call(prepare_kernel, grid=(row_count, groups), in_specs=[of_row...  89.8 us
    reduce_scatter x1, waiting for transfers between devices, on_device(): shard_up = scatter(grad_up_w.astype(LOW))  62.9 us
    reduce_scatter x1, waiting for transfers between devices, on_device(): shard_gate = scatter(grad_gate_w.astype(LOW))  62.4 us
    reduce_scatter x1, waiting for transfers between devices, on_device(): shard_down = scatter(grad_down.astype(LOW))  62.4 us
    reduce_scatter x3, waiting for transfers between devices, on_device(): scatter(part.astype(LOW))  61.1 us
    unnamed x15, waiting for transfers between devices  45.3 us
    reduce_scatter x1, waiting for transfers between devices, on_device(): shard_out = scatter(grad_out_w.astype(LOW))  42.9 us
  transfers between devices with their start and end apart: 18, of which 12 were waited for; matrix products, arithmetic and copies ran while one was open for 15% of the time, Pallas kernels for 10%

profile of v1, /device:TPU:0, one launch (start us, length us, event | category | flops | bytes accessed | tf_op | source)
XLA Modules:
  0.0 957.9 jit_solution(6275967315981640653)
XLA Ops:
  11.0 10.7 %all-gather.1 = bf16[8,1,2816]{2,1,0:T(2,128)(2,1)S(1)} all-gather(bf16[1,1,2816]{2,1,0:T(2,128)(2,1)S(1)} %reshape.236), channel_id=2, replica_groups=mesh['seq'=8,'row'=4] {'seq'}, dimensions={0}, use_global_device_ids=true | all-gather | bytes 50688 | tf_op jit(solution)/shard_map/all_gather | solution.py:483
  24.7 1.6 broadcast_multiply_fusion
  26.3 32.0 %all-gather.8.cloned.1.call-done = bf16[1024,3072]{1,0:T(8,128)(2,1)} async-done(((bf16[128,3072]{1,0:T(8,128)(2,1)}), bf16[1024,3072]{1,0:T(8,128)(2,1)}) %all-gather.8.cloned.1.call-update) | async-done | bytes 6291472 | tf_op jit(solution)/shard_map/all_gather | solution.py:479
  58.2 8.2 fusion.14.in_q.in_k.in_v
  66.4 2.1 copy-done
  69.2 2.9 collective-permute-start
  74.9 1.6 copy.211
  76.5 1.6 copy.206
  78.2 1.3 copy.247
  79.5 2.6 stack.49.cols_ref
  82.1 1.6 pad.4.rim_q.rim_k.rim_v
  85.0 89.8 %prepare.1 = (bf16[3,8,256,128]{3,2,1,0:T(8,128)(2,1)}, f32[3,256,1024]{2,1,0:T(8,128)}, bf16[3,8,128,256]{3,2,1,0:T(8,128)(2,1)}, bf16[3,8,256,256]{3,2,1,0:T(8,128)(2,1)}, bf16[3,8,256,256]{3,2,1,0:T(8,128)(2,1)}) custom-call(f32[3,256,8]{2,1,0:T(8,128)} %stack.49.cols_ref, f32[3,8,256]{2,1,0:T(8,128)} %broadcast_in_dim.20.rows_ref, ...), custom_call_target="tpu_custom_call" | custom-call | tf_op jit(solution)/shard_map/prepare/pallas_call | solution.py:176
  174.8 3.6 all-to-all-start
  179.3 27.7 %all-to-all-done.maps_ref = bf16[8,3,128,256]{3,2,1,0:T(8,128)(2,1)S(1)} async-done(((bf16[8,3,128,256]{3,2,1,0:T(8,128)(2,1)}), bf16[8,3,128,256]{3,2,1,0:T(8,128)(2,1)S(1)}, u32[]{:S(2)}, u32[]{:S(2)}) %all-to-all-start) | async-done | bytes 1572896 | tf_op jit(solution)/shard_map/all_to_all | solution.py:249
  208.1 3.3 chain.2
  211.4 3.5 all-to-all-start.1
  215.0 11.2 %fusion.2 = f32[3,256,2816]{2,1,0:T(8,128)} fusion(bf16[2816,1024]{1,0:T(8,128)(2,1)} %all-gather.16.cloned.1.call-done, bf16[3,256,1024]{2,1,0:T(8,128)(2,1)} %param.25, f32[3,256]{1,0:T(4,128)S(1)} %compare_convert_fusion.1), kind=kOutput, calls=%fused_computation.15 | convolution fusion | flops 4431544320 | bytes 15993856 | tf_op jit(solution)/shard_map/rsd,fd->rsf/dot_general | solution.py:555
  226.2 10.0 %all-to-all-done.1 = bf16[8,3,128,128]{3,2,1,0:T(8,128)(2,1)S(1)} async-done(((bf16[8,3,128,128]{3,2,1,0:T(8,128)(2,1)}), bf16[8,3,128,128]{3,2,1,0:T(8,128)(2,1)S(1)}, u32[]{:S(2)}, u32[]{:S(2)}) %all-to-all-start.1) | async-done | bytes 786464 | tf_op jit(solution)/shard_map/all_to_all | solution.py:253
  237.1 6.2 read.1
  243.2 4.0 multiply_reduce_fusion.2
  247.2 1.6 copy-done.4
  249.2 10.0 %fusion.8 = f32[3,256,2816]{2,1,0:T(8,128)} fusion(bf16[3,256,1024]{2,1,0:T(8,128)(2,1)S(1)} %multiply_convert_fusion.4, bf16[1024,2816]{1,0:T(8,128)(2,1)} %all-gather.14.cloned.1.call-done), kind=kOutput, calls=%fused_computation.21 | convolution fusion | flops 4429185024 | bytes 15990784 | tf_op jit(solution)/shard_map/dot_general | solution.py:548
  259.2 17.4 %multiply_convert_fusion.1 = (bf16[3,256,2816]{2,1,0:T(8,128)(2,1)}, bf16[3,256,2816]{2,1,0:T(8,128)(2,1)}, bf16[3,256,2816]{2,1,0:T(8,128)(2,1)}) fusion(f32[3,256,2816]{2,1,0:T(8,128)} %fusion.2, f32[3,256,2816]{2,1,0:T(8,128)} %fusion.8, bf16[3,256,1024]{2,1,0:T(8,128)(2,1)S(1)} %multiply_convert_fusion.4, ...), kind=kOutput, calls=%fused_computation.4 | convolution fusion | flops 4463788032 | bytes 37617664 | tf_op jit(solution)/shard_map/dot_general | solution.py:547
  276.7 6.6 fusion.6
  283.4 8.0 multiply_reduce_fusion
  292.5 1.6 copy-done.6
  294.2 3.0 fusion.41.grad_ref
  297.2 5.4 pull_read.1
  302.5 16.9 %all_to_all.20.grads_ref = bf16[8,3,128,128]{3,2,1,0:T(8,128)(2,1)} all-to-all(bf16[8,3,128,128]{3,2,1,0:T(8,128)(2,1)} %bitcast.152), channel_id=1, replica_groups=mesh['seq'=8,'row'=4] {'seq'}, dimensions={0} | all-to-all | bytes 1572864 | tf_op jit(solution)/shard_map/all_to_all | solution.py:249
  319.5 3.5 chain.3
  323.0 16.8 %all_to_all.21 = bf16[8,3,128,128]{3,2,1,0:T(8,128)(2,1)} all-to-all(bf16[8,3,128,128]{3,2,1,0:T(8,128)(2,1)} %chain.3), channel_id=1, replica_groups=mesh['seq'=8,'row'=4] {'seq'}, dimensions={0} | all-to-all | bytes 1572864 | tf_op jit(solution)/shard_map/all_to_all | solution.py:253
  339.7 40.2 %mixer_back.1 = (bf16[3,256,1024]{2,1,0:T(8,128)(2,1)}, bf16[3,256,1024]{2,1,0:T(8,128)(2,1)}, bf16[3,256,1024]{2,1,0:T(8,128)(2,1)}, f32[3,8,1024]{2,1,0:T(8,12...) custom-call(f32[3,256,8]{2,1,0:T(8,128)} %stack.49.cols_ref, ...), custom_call_target="tpu_custom_call" | custom-call | tf_op jit(solution)/shard_map/mixer_back/pallas_call | solution.py:426
  384.0 1.9 collective-permute-done.1
  386.9 1.5 dynamic_update_slice.9
  388.4 4.8 bitcast_convert_fusion.6
  393.2 1.5 dynamic_update_slice.10
  394.7 4.9 bitcast_convert_fusion.5
  400.1 3.3 bitcast_convert_fusion.4
  403.5 5.8 bitcast_convert_fusion.3
  409.4 9.9 %bitcast_convert_fusion.2 = bf16[1024,2816]{1,0:T(8,128)(2,1)} fusion(bf16[3,256,1024]{2,1,0:T(8,128)(2,1)} %copy-done.11, bf16[3,256,2816]{2,1,0:T(8,128)(2,1)} %get-tuple-element.171), kind=kOutput, calls=%fused_computation.2 | convolution fusion | flops 4432068608 | bytes 11665408 | tf_op jit(solution)/shard_map/rsd,rsf->df/dot_general | solution.py:580
  419.8 10.0 %bitcast_convert_fusion.1 = bf16[1024,2816]{1,0:T(8,128)(2,1)} fusion(bf16[3,256,1024]{2,1,0:T(8,128)(2,1)} %copy-done.11, bf16[3,256,2816]{2,1,0:T(8,128)(2,1)} %get-tuple-element.173), kind=kOutput, calls=%fused_computation.1 | convolution fusion | flops 4432068608 | bytes 11665408 | tf_op jit(solution)/shard_map/rsd,rsf->df/dot_general | solution.py:581
  429.9 10.1 %bitcast_convert_fusion = bf16[2816,1024]{1,0:T(8,128)(2,1)} fusion(bf16[3,256,2816]{2,1,0:T(8,128)(2,1)} %get-tuple-element.172, bf16[3,256,1024]{2,1,0:T(8,128)(2,1)} %param.25, f32[3,256]{1,0:T(4,128)S(1)} %compare_convert_fusion.1), kind=kOutput, calls=%fused_computation | convolution fusion | flops 4434427904 | bytes 11668480 | tf_op jit(solution)/shard_map/rsf,rsd->fd/dot_general | solution.py:579
  441.5 1.8 fusion.69
  443.4 2.8 convolution_bitcast_fusion
  446.1 1.9 reshape.223
  448.1 2.5 fusion.52
  450.6 3.5 fusion.29
  454.1 3.9 fusion.28
  458.1 5.9 fusion.25
  465.0 16.6 %reduce-scatter.10.cloned.1.call-done = bf16[128,1024]{1,0:T(8,128)(2,1)} async-done(((bf16[1024,1024]{1,0:T(8,128)(2,1)}), bf16[128,1024]{1,0:T(8,128)(2,1)}) %reduce-scatter.10.cloned.1.call-update) | async-done | bytes 262160 | tf_op jit(solution)/shard_map/reduce_scatter | solution.py:611
  481.6 44.5 %reduce-scatter.12.cloned.1.call-done = bf16[128,1024]{1,0:T(8,128)(2,1)} async-done(((bf16[1024,1024]{1,0:T(8,128)(2,1)}), bf16[128,1024]{1,0:T(8,128)(2,1)}) %reduce-scatter.12.cloned.1.call-update) | async-done | bytes 262160 | tf_op jit(solution)/shard_map/reduce_scatter | solution.py:611
  526.1 2.0 pad_maximum_fusion
  528.2 42.9 %reduce-scatter.14.cloned.1.call-done = bf16[128,1024]{1,0:T(8,128)(2,1)} async-done(((bf16[1024,1024]{1,0:T(8,128)(2,1)}), bf16[128,1024]{1,0:T(8,128)(2,1)}) %reduce-scatter.14.cloned.1.call-update) | async-done | bytes 262160 | tf_op jit(solution)/shard_map/reduce_scatter | solution.py:586
  571.0 62.4 %reduce-scatter.16.cloned.1.call-done = bf16[128,2816]{1,0:T(8,128)(2,1)} async-done(((bf16[1024,2816]{1,0:T(8,128)(2,1)}), bf16[128,2816]{1,0:T(8,128)(2,1)}) %reduce-scatter.16.cloned.1.call-update) | async-done | bytes 720912 | tf_op jit(solution)/shard_map/reduce_scatter | solution.py:584
  633.4 62.9 %reduce-scatter.18.cloned.1.call-done = bf16[128,2816]{1,0:T(8,128)(2,1)} async-done(((bf16[1024,2816]{1,0:T(8,128)(2,1)}), bf16[128,2816]{1,0:T(8,128)(2,1)}) %reduce-scatter.18.cloned.1.call-update) | async-done | bytes 720912 | tf_op jit(solution)/shard_map/reduce_scatter | solution.py:585
  696.4 62.4 %reduce-scatter.20.cloned.1.call-done = bf16[352,1024]{1,0:T(8,128)(2,1)} async-done(((bf16[2816,1024]{1,0:T(8,128)(2,1)}), bf16[352,1024]{1,0:T(8,128)(2,1)}) %reduce-scatter.20.cloned.1.call-update) | async-done | bytes 720912 | tf_op jit(solution)/shard_map/reduce_scatter | solution.py:583
  759.4 10.7 %multiply_convert_fusion.3 = bf16[3,256,1024]{2,1,0:T(8,128)(2,1)} fusion(f32[3,256,1024]{2,1,0:T(8,128)} %copy-done.4, bf16[3,256,2816]{2,1,0:T(8,128)(2,1)} %get-tuple-element.172, bf16[2816,1024]{1,0:T(8,128)(2,1)} %all-gather.16.cloned.1.call-done, f32[3,256]{1,0:T(4,128)S(1)} %compare_convert_fusion.1), kind=kOutput, calls=%fused_computation.47 | convolution fusion | flops 4431544320 | bytes 14814208 | tf_op jit(solution)/shard_map/dot_general | solution.py:551
  770.1 2.0 fusion.22
  772.1 42.0 %all-reduce.6.cloned.1.call-done = f32[8,2824]{1,0:T(8,128)} async-done(((f32[8,2824]{1,0:T(8,128)}), f32[8,2824]{1,0:T(8,128)}) %all-reduce.6.cloned.1.call-update) | async-done | bytes 90384
  814.1 1.5 constant_dynamic-slice_fusion
  815.7 19.2 %psum.42 = f32[1,2824]{1,0:T(1,128)S(1)} all-reduce(f32[1,2824]{1,0:T(1,128)S(1)} %constant_dynamic-slice_fusion), channel_id=1, replica_groups=mesh['seq'=8,'row'=4] {'row'}, use_global_device_ids=true, to_apply=%region_15.16 | all-reduce | flops 2824 | bytes 22592 | tf_op jit(solution)/shard_map/psum | solution.py:645
  837.3 105.6 %all-reduce.8.cloned.1.call-done = (bf16[128,3072]{1,0:T(8,128)(2,1)}, bf16[128,1024]{1,0:T(8,128)(2,1)}, bf16[128,2816]{1,0:T(8,128)(2,1)}, bf16[128,2816]{1,0:T(8,128)(2,1)}, bf16[352,1024]{1,0:T(8,128)(2,1)}) async-done(((bf16[128,3072]{1,0:T(8,128)(2,1)}, bf16[128,1024]{1,0:T(8,128)(2,1)}, bf16[128,2816]{1,0:T(8,128)(2,1)}, bf16[128,2816]{1,0:T(8,128)(2,1)}, bf16[352,1024]{1,0:T(8,128)(2,1)}), ...) | async-done | bytes 3211280 | tf_op jit(solution)/shard_map/psum | solution.py:647
  942.9 2.5 convert_element_type.183
  945.5 2.3 convert_element_type.187
  (177 shorter events, 30.7 us)
Async XLA Ops:
  7.2 3.5 copy-start.28
  7.2 3.8 copy-start.26
  7.2 3.8 copy-start.31
  7.2 3.8 copy-start.30
  7.2 14.9 %copy-start.35 = (bf16[8]{0:T(256)(128)(2,1)S(1)}, bf16[8]{0:T(256)(128)(2,1)}, u32[]{:S(2)}) copy-start(bf16[8]{0:T(256)(128)(2,1)} %param.18) | copy-start | bytes 52
  7.2 14.9 %copy-start.29 = (s32[3,8]{1,0:T(4,128)S(1)}, s32[3,8]{1,0:T(4,128)}, u32[]{:S(2)}) copy-start(s32[3,8]{1,0:T(4,128)} %param.14) | copy-start | bytes 292
  7.2 15.6 %copy-start.1 = (bf16[3,256,1024]{2,1,0:T(8,128)(2,1)S(1)}, bf16[3,256,1024]{2,1,0:T(8,128)(2,1)}, u32[]{:S(2)}) copy-start(bf16[3,256,1024]{2,1,0:T(8,128)(2,1)} %param.13) | copy-start | bytes 4718596
  7.2 51.0 %all-gather.8.cloned.1.call-start = ((), (), s32[]{:S(2)}) async-start(), calls=%async_computation.11 | async-start | bytes 7077888 | tf_op jit(solution)/shard_map/all_gather | solution.py:479
  8.0 207.0 %all-gather.16.cloned.1.call-start = ((), (), s32[]{:S(2)}) async-start(), calls=%async_computation.15 | async-start | bytes 6488064 | tf_op jit(solution)/shard_map/all_gather | solution.py:494
  8.7 234.5 %all-gather.10.cloned.1.call-start = ((), (), s32[]{:S(2)}) async-start(), calls=%async_computation.12 | async-start | bytes 2359296 | tf_op jit(solution)/shard_map/all_gather | solution.py:491
  9.5 239.8 %all-gather.14.cloned.1.call-start = ((), (), s32[]{:S(2)}) async-start(), calls=%async_computation.14 | async-start | bytes 6488064 | tf_op jit(solution)/shard_map/all_gather | solution.py:493
  10.0 249.2 %all-gather.12.cloned.1.call-start = ((), (), s32[]{:S(2)}) async-start(), calls=%async_computation.13 | async-start | bytes 6488064 | tf_op jit(solution)/shard_map/all_gather | solution.py:492
  22.1 4.1 copy-start.12
  22.3 1.6 copy-start.22
  66.4 2.1 copy-start
  69.2 12.8 %collective-permute-start = (bf16[3,3,3072]{2,1,0:T(4,128)(2,1)}, bf16[3,3,3072]{2,1,0:T(4,128)(2,1)}, u32[]{:S(2)}, u32[]{:S(2)}) collective-permute-start(bf16[3,3,3072]{2,1,0:T(4,128)(2,1)} %slice.154), channel_id=1, source_target_pairs={{0,4},{4,8},{8,12},{12,16},{16,20},{20,24},{24,28},{1,5},{5,9},{9,... | collective-permute-start | bytes 165896 | tf_op jit(solution)/shard_map/ppermute | solution.py:453
  174.8 3.6 copy-start.23
  174.8 32.2 %all-to-all-start = ((bf16[8,3,128,256]{3,2,1,0:T(8,128)(2,1)}), bf16[8,3,128,256]{3,2,1,0:T(8,128)(2,1)S(1)}, u32[]{:S(2)}, u32[]{:S(2)}) async-start(bf16[8,3,128,256]{3,2,1,0:T(8,128)(2,1)} %bitcast.154), calls=%async_computation | async-start | bytes 3145728 | tf_op jit(solution)/shard_map/all_to_all | solution.py:249
  206.9 1.1 copy-start.3
  211.4 24.8 %all-to-all-start.1 = ((bf16[8,3,128,128]{3,2,1,0:T(8,128)(2,1)}), bf16[8,3,128,128]{3,2,1,0:T(8,128)(2,1)S(1)}, u32[]{:S(2)}, u32[]{:S(2)}) async-start(bf16[8,3,128,128]{3,2,1,0:T(8,128)(2,1)} %chain.2), calls=%async_computation.1 | async-start | bytes 1572864 | tf_op jit(solution)/shard_map/all_to_all | solution.py:253
  215.0 250.1 %reduce-scatter.8.cloned.1.call-start = ((), (), s32[]{:S(2)}) async-start(), calls=%async_computation.16 | async-start | bytes 2359296 | tf_op jit(solution)/shard_map/reduce_scatter | solution.py:611
  236.2 0.9 copy-start.8
  247.2 1.6 copy-start.4
  249.2 10.0 %copy-start.11 = (bf16[3,256,1024]{2,1,0:T(8,128)(2,1)}, bf16[3,256,1024]{2,1,0:T(8,128)(2,1)S(1)}, u32[]{:S(2)}) copy-start(bf16[3,256,1024]{2,1,0:T(8,128)(2,1)S(1)} %multiply_convert_fusion.4) | copy-start | bytes 4718596
  259.2 17.4 %copy-start.32 = (bf16[1024,2816]{1,0:T(8,128)(2,1)S(1)}, bf16[1024,2816]{1,0:T(8,128)(2,1)}, u32[]{:S(2)}) copy-start(bf16[1024,2816]{1,0:T(8,128)(2,1)} %all-gather.14.cloned.1.call-done) | copy-start | bytes 17301508
  276.7 6.7 copy-start.5
  276.7 6.7 copy-start.37
  283.3 8.1 copy-start.10
  291.4 2.8 copy-start.33
  292.5 1.7 copy-start.6
  382.7 3.2 collective-permute-start.1
  393.2 88.4 %reduce-scatter.10.cloned.1.call-start = ((), (), s32[]{:S(2)}) async-start(), calls=%async_computation.17 | async-start | bytes 2359296 | tf_op jit(solution)/shard_map/reduce_scatter | solution.py:611
  394.7 4.9 copy-start.9
  399.6 126.5 %reduce-scatter.12.cloned.1.call-start = ((), (), s32[]{:S(2)}) async-start(), calls=%async_computation.18 | async-start | bytes 2359296 | tf_op jit(solution)/shard_map/reduce_scatter | solution.py:611
  403.5 167.6 %reduce-scatter.14.cloned.1.call-start = ((), (), s32[]{:S(2)}) async-start(), calls=%async_computation.19 | async-start | bytes 2359296 | tf_op jit(solution)/shard_map/reduce_scatter | solution.py:586
  409.3 224.1 %reduce-scatter.16.cloned.1.call-start = ((), (), s32[]{:S(2)}) async-start(), calls=%async_computation.20 | async-start | bytes 6488064 | tf_op jit(solution)/shard_map/reduce_scatter | solution.py:584
  419.3 277.0 %reduce-scatter.18.cloned.1.call-start = ((), (), s32[]{:S(2)}) async-start(), calls=%async_computation.21 | async-start | bytes 6488064 | tf_op jit(solution)/shard_map/reduce_scatter | solution.py:585
  429.8 328.9 %reduce-scatter.20.cloned.1.call-start = ((), (), s32[]{:S(2)}) async-start(), calls=%async_computation.22 | async-start | bytes 6488064 | tf_op jit(solution)/shard_map/reduce_scatter | solution.py:583
  440.0 0.8 copy-start.21
  440.0 0.8 copy-start.20
  440.0 0.8 copy-start.19
  440.0 374.1 %all-reduce.6.cloned.1.call-start = ((), (), s32[]{:S(2)}) async-start(), calls=%async_computation.23 | async-start | bytes 188416
  448.1 2.5 copy-start.34
  458.0 6.0 copy-start.25
  458.0 6.0 copy-start.17
  458.0 6.0 copy-start.16
  458.1 6.0 copy-start.27
  464.0 294.8 %copy-start.36 = (u32[32]{0:T(128)S(1)}, u32[32]{0:T(128)}, u32[]{:S(2)}) copy-start(u32[32]{0:T(128)} %constant.55) | copy-start | bytes 388
  464.1 0.6 copy-start.18
  464.7 478.2 %all-reduce.8.cloned.1.call-start = ((), (), s32[]{:S(2)}) async-start(), calls=%async_computation.24 | async-start | bytes 6422528 | tf_op jit(solution)/shard_map/psum | solution.py:647
  759.3 10.7 %copy-start.2 = (f32[3,256,1024]{2,1,0:T(8,128)S(1)}, f32[3,256,1024]{2,1,0:T(8,128)}, u32[]{:S(2)}) copy-start(f32[3,256,1024]{2,1,0:T(8,128)} %get-tuple-element.197) | copy-start | bytes 9437188
  759.3 10.7 %copy-start.7 = (f32[3,256,1024]{2,1,0:T(8,128)S(1)}, f32[3,256,1024]{2,1,0:T(8,128)}, u32[]{:S(2)}) copy-start(f32[3,256,1024]{2,1,0:T(8,128)} %copy-done.6) | copy-start | bytes 9437188
  759.3 10.7 %copy-start.24 = (f32[3,256]{1,0:T(4,128)S(1)}, f32[3,256]{1,0:T(4,128)}, u32[]{:S(2)}) copy-start(f32[3,256]{1,0:T(4,128)} %get-tuple-element.188) | copy-start | bytes 9220
  942.9 4.9 copy-start.14
  942.9 6.1 copy-start.13
  945.5 4.8 copy-start.15
Sparse Core Ops, SparseCore 0:
  10.0 48.2 all-gather.7
  60.1 43.7 all-gather.15
  105.8 28.0 all-gather.9
  135.6 43.3 all-gather.13
  180.8 58.7 all-gather.11
  393.3 43.3 reduce-scatter.7
  440.4 41.2 reduce-scatter.9
  484.9 41.1 reduce-scatter.11
  529.8 41.2 reduce-scatter.13
  574.3 59.0 reduce-scatter.15
  637.3 59.0 reduce-scatter.17
  699.7 59.0 reduce-scatter.19
  762.7 51.4 all-reduce.5
  817.3 125.5 all-reduce.7

commit v2 on v1

v2 whole, which is shorter than its diff:
```python
import functools

import jax
import jax.numpy as jnp
from jax import lax
from jax.experimental import pallas as pl
from jax.experimental.pallas import tpu as pltpu
from jax.sharding import PartitionSpec as P

EPSILON = 1e-06
LOW = jnp.bfloat16
WIDE = jnp.float32
HEADS_STEP = 8
RIM = 8
VMEM_BYTES = 56 * 1024 * 1024


def nn(left, right):
    return lax.dot_general(
        left.astype(LOW), right.astype(LOW), (((1,), (0,)), ((), ())), preferred_element_type=WIDE
    )


def nt(left, right):
    return lax.dot_general(
        left.astype(LOW), right.astype(LOW), (((1,), (1,)), ((), ())), preferred_element_type=WIDE
    )


def tn(left, right):
    return lax.dot_general(
        left.astype(LOW), right.astype(LOW), (((0,), (0,)), ((), ())), preferred_element_type=WIDE
    )


def split(value):
    high = value.astype(LOW)
    return high, (value - high.astype(WIDE)).astype(LOW)


def nn_fine(left, right):
    left_high, left_low = split(left)
    right_high, right_low = split(right)
    return nn(left_high, right_high) + nn(left_high, right_low) + nn(left_low, right_high)


def rms_scale(values):
    return lax.rsqrt(jnp.mean(values * values, axis=-1, keepdims=True) + EPSILON)


def windows_of(rim, block, taps, room):
    size = block.shape[0]
    room[pl.ds(0, RIM), :] = rim
    room[pl.ds(RIM, size), :] = block
    return [block] + [room[pl.ds(RIM - step, size), :] for step in range(1, taps)]


def convolve(windows, weights, tap_masks):
    total = weights[0:1] * windows[0]
    for step in range(1, len(windows)):
        total = total + weights[step : step + 1] * (windows[step] * tap_masks[step - 1])
    return total


def pair_distance(size):
    row = lax.broadcasted_iota(jnp.int32, (size, size), 0)
    column = lax.broadcasted_iota(jnp.int32, (size, size), 1)
    return row, column


def inverse_unit_lower(stricts, corners):
    size = stricts[0].shape[0]
    row, column = pair_distance(size)
    eye = (row == column).astype(WIDE)
    results = [eye - strict * corners[0] for strict in stricts]
    level = 1
    while (1 << level) < size:
        lows = [result.astype(LOW) for result in results]
        halves = [
            nn((strict * corners[level]).astype(LOW), low).astype(LOW)
            for strict, low in zip(stricts, lows)
        ]
        results = [
            result - nn(low, half) for result, low, half in zip(results, lows, halves)
        ]
        level += 1
    if REFINE:
        rests = []
        for strict, result in zip(stricts, results):
            high, low = split(result)
            strict_high, strict_low = split(strict)
            rests.append(
                eye - result - nn(strict_high, high) - nn(strict_high, low) - nn(strict_low, high)
            )
        results = [result + nn(result, rest) for result, rest in zip(results, rests)]
    return results


REFINE = True


def unit_and_scale(values):
    scale = lax.rsqrt(jnp.sum(values * values, axis=-1, keepdims=True) + EPSILON)
    return values * scale, scale


def head_masks(cols, rows):
    doc_col, doc_row = cols[:, 0:1], rows[0:1, :]
    size = cols.shape[0]
    row, column = pair_distance(size)
    same = doc_col == doc_row
    inclusive = same & (row >= column)
    strict = same & (row > column)
    tap_masks = [cols[:, 1:2], cols[:, 2:3], cols[:, 3:4]]
    return row, column, inclusive, strict, tap_masks, cols[:, 4:5], cols[:, 5:6]


def pick_head(table, head):
    lane = lax.broadcasted_iota(jnp.int32, table.shape, 1)
    return jnp.sum(jnp.where(lane == head, table, 0.0), axis=1, keepdims=True)


def prepare_kernel(
    cols_ref, rows_ref, beta_ref, taps_q, taps_k, taps_v, rim_q, rim_k, rim_v, in_q, in_k, in_v,
    eff_ref, local_ref, maps_ref, solve_ref, weights_ref, room_ref,
):
    cols, rows = cols_ref[0], rows_ref[0]
    row, column, inclusive, strict, tap_masks, carried, last = head_masks(cols, rows)
    beta_all = beta_ref[0]
    tap_count = taps_q.shape[0]
    size = cols.shape[0]
    half = size // 2
    apart = (row ^ column)[:half, :half]
    corners = []
    level = 0
    while (1 << level) < half:
        corners.append(((apart >> level) == 1).astype(WIDE))
        level += 1
    heads = range(HEADS_STEP)
    lanes = [slice(local * 128, (local + 1) * 128) for local in heads]
    queries, keys, values, betas = [], [], [], []
    for local in heads:
        acts = []
        for index, (taps, rim, block) in enumerate(
            ((taps_q, rim_q, in_q), (taps_k, rim_k, in_k), (taps_v, rim_v, in_v))
        ):
            windows = windows_of(
                rim[0, :, lanes[local]].astype(WIDE),
                block[0, :, lanes[local]].astype(WIDE),
                tap_count,
                room_ref.at[3 * local + index],
            )
            acts.append(jax.nn.silu(convolve(windows, taps[:, lanes[local]].astype(WIDE), tap_masks)))
        queries.append(unit_and_scale(acts[0])[0])
        keys.append(unit_and_scale(acts[1])[0])
        values.append(acts[2])
        betas.append(pick_head(beta_all, pl.program_id(1) * HEADS_STEP + local))
    grams = [
        nt(jnp.concatenate([key.astype(LOW), query.astype(LOW)], axis=0), key)
        for key, query in zip(keys, queries)
    ]
    systems = [jnp.where(strict, gram[:size] * beta, 0.0) for gram, beta in zip(grams, betas)]
    scores = [jnp.where(inclusive, gram[size:], 0.0).astype(LOW) for gram in grams]
    blocks = inverse_unit_lower(
        [system[:half, :half] for system in systems] + [system[half:, half:] for system in systems],
        corners,
    )
    upper = [block.astype(LOW) for block in blocks[:HEADS_STEP]]
    lower = [block.astype(LOW) for block in blocks[HEADS_STEP:]]
    crossing = [nn(system[half:, :half], block) for system, block in zip(systems, upper)]
    crossing = [-nn(block, cross) for block, cross in zip(lower, crossing)]
    solves = [
        jnp.concatenate(
            [
                jnp.concatenate([first, jnp.zeros((half, half), LOW)], axis=1),
                jnp.concatenate([cross.astype(LOW), second], axis=1),
            ],
            axis=0,
        )
        for first, second, cross in zip(upper, lower, crossing)
    ]
    rights = [
        jnp.concatenate([(beta * carried) * key, beta * value], axis=1)
        for beta, key, value in zip(betas, keys, values)
    ]
    weights = [nn(solve, right).astype(LOW) for solve, right in zip(solves, rights)]
    mixed = [nn(score, weight) for score, weight in zip(scores, weights)]
    maps = [tn(last * key, weight) for key, weight in zip(keys, weights)]
    for local in heads:
        eff_ref[0, local] = (carried * queries[local] - mixed[local][:, :128]).astype(LOW)
        local_ref[0, :, lanes[local]] = mixed[local][:, 128:]
        maps_ref[0, local] = maps[local].astype(LOW)
        solve_ref[0, local] = solves[local]
        weights_ref[0, local] = weights[local]


def prepare_call(cols, rows, beta, taps, rim, projected):
    row_count, size, triple = projected.shape
    head_count = triple // (3 * 128)
    groups = head_count // HEADS_STEP
    wide = HEADS_STEP * 128
    tap_count = taps.shape[0]

    def of_row(block):
        return pl.BlockSpec(block, lambda r, g: (r, 0, 0))

    def part(rows_in, index):
        return pl.BlockSpec((1, rows_in, wide), lambda r, g: (r, 0, index * groups + g))

    def tap_part(index):
        return pl.BlockSpec((tap_count, wide), lambda r, g: (0, index * groups + g))

    def per_head(*block):
        return pl.BlockSpec((1, HEADS_STEP) + block, lambda r, g: (r, g, 0, 0))

    return pl.pallas_call(
        prepare_kernel,
        grid=(row_count, groups),
        in_specs=[of_row((1,) + cols.shape[1:]), of_row((1,) + rows.shape[1:]), of_row((1,) + beta.shape[1:])]
        + [tap_part(i) for i in range(3)]
        + [part(RIM, i) for i in range(3)]
        + [part(size, i) for i in range(3)],
        out_specs=[
            per_head(size, 128),
            pl.BlockSpec((1, size, wide), lambda r, g: (r, 0, g)),
            per_head(128, 256),
            per_head(size, size),
            per_head(size, 256),
        ],
        out_shape=[
            jax.ShapeDtypeStruct((row_count, head_count, size, 128), LOW),
            jax.ShapeDtypeStruct((row_count, size, head_count * 128), WIDE),
            jax.ShapeDtypeStruct((row_count, head_count, 128, 256), LOW),
            jax.ShapeDtypeStruct((row_count, head_count, size, size), LOW),
            jax.ShapeDtypeStruct((row_count, head_count, size, 256), LOW),
        ],
        scratch_shapes=[pltpu.VMEM((3 * HEADS_STEP, RIM + size, 128), WIDE)],
        compiler_params=pltpu.CompilerParams(vmem_limit_bytes=VMEM_BYTES),
        cost_estimate=timed(22),
        name="prepare",
    )(cols, rows, beta, taps, taps, taps, rim, rim, rim, projected, projected, projected)


def chain_forward_kernel(keep_ref, maps_ref, out_ref):
    count, pairs = maps_ref.shape[0], maps_ref.shape[1]
    states = [jnp.zeros((128, 128), WIDE) for _ in range(pairs)]
    for device in range(count):
        for pair in range(pairs):
            state = states[pair]
            out_ref[device, pair] = state.astype(LOW)
            decay = maps_ref[device, pair, :, :128]
            write = maps_ref[device, pair, :, 128:]
            states[pair] = (
                keep_ref[pair, device] * state - nn(decay, state) + write.astype(WIDE)
            )


def chain_backward_kernel(keep_ref, maps_ref, grads_ref, out_ref):
    count, pairs = maps_ref.shape[0], maps_ref.shape[1]
    states = [jnp.zeros((128, 128), WIDE) for _ in range(pairs)]
    for device in reversed(range(count)):
        for pair in range(pairs):
            state = states[pair]
            out_ref[device, pair] = state.astype(LOW)
            decay = maps_ref[device, pair, :, :128]
            states[pair] = (
                keep_ref[pair, device] * state
                - tn(decay, state)
                + grads_ref[device, pair].astype(WIDE)
            )


def chain_call(kernel, keep, *arrays):
    count, pairs = arrays[0].shape[:2]
    return pl.pallas_call(
        kernel,
        in_specs=[pl.BlockSpec(memory_space=pltpu.SMEM)]
        + [pl.BlockSpec(memory_space=pltpu.VMEM) for _ in arrays],
        out_specs=pl.BlockSpec(memory_space=pltpu.VMEM),
        out_shape=jax.ShapeDtypeStruct((count, pairs, 128, 128), LOW),
        compiler_params=pltpu.CompilerParams(vmem_limit_bytes=VMEM_BYTES),
        cost_estimate=timed(3),
        name="chain",
    )(keep, *arrays)


def exchange(value, count):
    pairs = value.shape[0]
    share = -(-pairs // count)
    padded = jnp.pad(value, ((0, share * count - pairs),) + ((0, 0),) * (value.ndim - 1))
    cut = padded.reshape((count, share) + value.shape[1:])
    return lax.all_to_all(cut, "seq", split_axis=0, concat_axis=0)


def to_home(value, pairs):
    moved = lax.all_to_all(value, "seq", split_axis=0, concat_axis=0)
    return moved.reshape((-1,) + value.shape[2:])[:pairs]


def feed_kernel(
    gate_moves, up_moves, position_ref, eff_ref, local_ref, state_ref, inputs_ref, cot_ref, valid_ref, gain_ref, w_out_ref,
    down_ref, *refs,
):
    count = len(gate_moves)
    (
    heads_ref, second_ref, act_ref, pair_ref, output_ref, upstream_ref,
    hidden_grad_ref, mix_ref, heads_grad_ref, local_grad_ref, gain_grad_ref,
    hidden_ref, out_sum, second_sum, gate_ref, up_ref,
    ) = refs[count + len(up_moves) :]
    put([gate_ref], refs[:count], gate_moves, position_ref[0])
    put([up_ref], refs[count : count + len(up_moves)], up_moves, position_ref[0])
    step, last_step = pl.program_id(0), pl.num_programs(0) - 1
    row_count, head_count, size = eff_ref.shape[:3]

    @pl.when(step == 0)
    def _():
        for r in range(row_count):
            tokens = slice(r * size, (r + 1) * size)
            for h in range(head_count):
                lanes = slice(h * 128, (h + 1) * 128)
                heads_ref[tokens, lanes] = (
                    local_ref[r, :, lanes] + nn(eff_ref[r, h], state_ref[r, h])
                ).astype(LOW)
        hidden = inputs_ref[...].astype(WIDE) + nn(heads_ref[...], w_out_ref[...])
        hidden_ref[...] = hidden
        second_ref[...] = (hidden * rms_scale(hidden) * gain_ref[...]).astype(LOW)
        upstream_ref[...] = (cot_ref[...].astype(WIDE) * valid_ref[:, 0:1]).astype(LOW)
        out_sum[...] = hidden
        second_sum[...] = jnp.zeros(second_sum.shape, WIDE)

    second = second_ref[...]
    gated = nn(second, gate_ref[...])
    lifted = nn(second, up_ref[...])
    grad_act = nt(upstream_ref[...], down_ref[...])
    gate = jax.nn.sigmoid(gated)
    opened = gated * gate
    act = (opened * lifted).astype(LOW)
    act_ref[...] = act
    grad_gated = (grad_act * lifted * gate * (1.0 + gated * (1.0 - gate))).astype(LOW)
    grad_lifted = (grad_act * opened).astype(LOW)
    pair_ref[0] = grad_gated
    pair_ref[1] = grad_lifted
    out_sum[...] += nn(act, down_ref[...])
    second_sum[...] += nt(grad_gated, gate_ref[...]) + nt(grad_lifted, up_ref[...])

    @pl.when(step == last_step)
    def _():
        output_ref[...] = (valid_ref[:, 0:1] * out_sum[...]).astype(LOW)
        hidden = hidden_ref[...]
        scale = rms_scale(hidden)
        grad_second = second_sum[...]
        gain_grad_ref[...] = jnp.sum(grad_second * hidden * scale, axis=0, keepdims=True)
        scaled = gain_ref[...] * grad_second
        grad_hidden = (
            upstream_ref[...].astype(WIDE)
            + scale * scaled
            - hidden * (scale * scale * scale * jnp.mean(scaled * hidden, axis=-1, keepdims=True))
        )
        hidden_grad_ref[...] = grad_hidden
        mix_ref[...] = grad_hidden.astype(LOW)
        heads_grad_ref[...] = nt(mix_ref[...], w_out_ref[...]).astype(LOW)
        for r in range(row_count):
            tokens = slice(r * size, (r + 1) * size)
            for h in range(head_count):
                lanes = slice(h * 128, (h + 1) * 128)
                local_grad_ref[r, h] = tn(eff_ref[r, h], heads_grad_ref[tokens, lanes]).astype(LOW)


def feed_call(eff, local, state, inputs, cot, valid, gain, w_out, gate, up, w_down):
    row_count, head_count, size = eff.shape[:3]
    tokens, width = inputs.shape
    pieces, position = gate[0] + up[0], gate[3]
    units = pieces[0].shape[1]
    tile = FEED_TILE

    def whole(shape):
        return pl.BlockSpec(shape, lambda j: (0,) * len(shape), pipeline_mode=pl.Buffered(1))

    token_low = jax.ShapeDtypeStruct((tokens, width), LOW)
    token_spec = whole((tokens, width))
    return pl.pallas_call(
        functools.partial(feed_kernel, gate[1], up[1]),
        grid=(units // tile,),
        in_specs=[
            pl.BlockSpec(memory_space=pltpu.SMEM), whole(eff.shape), whole(local.shape), whole(state.shape), token_spec, token_spec,
            whole(valid.shape), whole(gain.shape), whole(w_out.shape),
            pl.BlockSpec((tile, width), lambda j: (j, 0)),
        ]
        + [pl.BlockSpec((piece.shape[0], tile), lambda j: (0, j)) for piece in pieces],
        out_specs=[
            token_spec, token_spec,
            pl.BlockSpec((tokens, tile), lambda j: (0, j)),
            pl.BlockSpec((2, tokens, tile), lambda j: (0, 0, j)),
            token_spec, token_spec, token_spec, token_spec, token_spec,
            whole(state.shape), whole((1, width)),
        ],
        out_shape=[
            token_low, token_low,
            jax.ShapeDtypeStruct((tokens, units), LOW),
            jax.ShapeDtypeStruct((2, tokens, units), LOW),
            token_low, token_low,
            jax.ShapeDtypeStruct((tokens, width), WIDE),
            token_low, token_low,
            jax.ShapeDtypeStruct(state.shape, LOW),
            jax.ShapeDtypeStruct((1, width), WIDE),
        ],
        scratch_shapes=[pltpu.VMEM((tokens, width), WIDE)] * 3 + [pltpu.VMEM((width, tile), LOW)] * 2,
        compiler_params=pltpu.CompilerParams(vmem_limit_bytes=VMEM_BYTES),
        cost_estimate=timed(38),
        name="feed",
    )(position, eff, local, state, inputs, cot, valid, gain, w_out, w_down, *pieces)


FEED_TILE = 256


def project_back_kernel(
    first_ref, second_ref, weight_ref, logit_ref, extra_ref, inputs_ref, gain_ref, hidden_grad_ref,
    out_ref, gain_grad_ref, total,
):
    step = pl.program_id(0)
    half = first_ref.shape[2]

    @pl.when(step == 0)
    def _():
        high, low = split(logit_ref[...])
        total[...] = nt(high, extra_ref[...]) + nt(low, extra_ref[...])

    total[...] += nt(first_ref[0], weight_ref[:, :half]) + nt(second_ref[0], weight_ref[:, half:])

    @pl.when(step == pl.num_programs(0) - 1)
    def _():
        inputs = inputs_ref[...].astype(WIDE)
        scale = rms_scale(inputs)
        grad = total[...]
        gain_grad_ref[...] = jnp.sum(grad * inputs * scale, axis=0, keepdims=True)
        scaled = gain_ref[...] * grad
        out_ref[...] = (
            hidden_grad_ref[...]
            + scale * scaled
            - inputs * (scale * scale * scale * jnp.mean(scaled * inputs, axis=-1, keepdims=True))
        ).astype(LOW)


def project_back_call(first, second, joint, grad_logits, extra, inputs, gain, hidden_grad):
    parts, tokens, half = first.shape
    width = 2 * half

    def whole(shape):
        return pl.BlockSpec(shape, lambda j: (0,) * len(shape))

    return pl.pallas_call(
        project_back_kernel,
        grid=(parts,),
        in_specs=[
            pl.BlockSpec((1, tokens, half), lambda j: (j, 0, 0)),
            pl.BlockSpec((1, tokens, half), lambda j: (j, 0, 0)),
            pl.BlockSpec((width, width), lambda j: (0, j)),
            whole((tokens, 128)), whole((width, 128)),
            whole((tokens, width)), whole((1, width)), whole((tokens, width)),
        ],
        out_specs=[whole((tokens, width)), whole((1, width))],
        out_shape=[
            jax.ShapeDtypeStruct((tokens, width), LOW),
            jax.ShapeDtypeStruct((1, width), WIDE),
        ],
        scratch_shapes=[pltpu.VMEM((tokens, width), WIDE)],
        compiler_params=pltpu.CompilerParams(vmem_limit_bytes=VMEM_BYTES),
        cost_estimate=timed(10),
        name="project_back",
    )(first, second, joint, grad_logits, extra, inputs, gain, hidden_grad)


def back_kernel(
    first_head, cols_ref, rows_ref, beta_ref, taps_q, taps_k, taps_v, rim_q, rim_k, rim_v, in_q, in_k, in_v,
    solve_ref, weights_ref, state_ref, exit_ref, grad_ref,
    out_ref, edge_ref, tail_ref, tap_ref, rate_ref, room_ref, back_ref,
):
    cols, rows = cols_ref[0], rows_ref[0]
    row, column, inclusive, strict, tap_masks, carried, last = head_masks(cols, rows)
    beta_all = beta_ref[0]
    tap_count = taps_q.shape[0]
    size = cols.shape[0]
    heads = range(state_ref.shape[1])
    lanes = [slice(local * 128, (local + 1) * 128) for local in heads]
    parts = ((taps_q, rim_q, in_q), (taps_k, rim_k, in_k), (taps_v, rim_v, in_v))

    queries, keys, values, betas, kept = [], [], [], [], []
    for local in heads:
        acts = []
        for index, (taps, rim, block) in enumerate(parts):
            windows = windows_of(
                rim[0, :, lanes[local]].astype(WIDE),
                block[0, :, lanes[local]].astype(WIDE),
                tap_count,
                room_ref.at[3 * local + index],
            )
            convolved = convolve(windows, taps[:, lanes[local]].astype(WIDE), tap_masks)
            gate = jax.nn.sigmoid(convolved)
            acts.append(convolved * gate)
            kept.append(gate * (1.0 + convolved * (1.0 - gate)))
        queries.append(unit_and_scale(acts[0]))
        keys.append(unit_and_scale(acts[1]))
        values.append(acts[2])
        betas.append(pick_head(beta_all, first_head + local))
    eye = (row == column).astype(LOW)
    strict_low = jnp.where(strict, 1.0, 0.0).astype(LOW)
    inclusive_low = jnp.where(inclusive, 1.0, 0.0).astype(LOW)
    later_low = jnp.where(rows[0:1, :] == cols[:, 0:1], jnp.where(row <= column, 1.0, 0.0), 0.0).astype(LOW)
    later_strict_low = later_low - eye
    key_lows = [key.astype(LOW) for key, _ in keys]
    query_lows = [query.astype(LOW) for query, _ in queries]
    boths = [jnp.concatenate([key, query], axis=0) for key, query in zip(key_lows, query_lows)]
    grad_lows = [grad_ref[0, :, lanes[local]] for local in heads]
    scores_turned = [
        nt(key, query).astype(LOW) * later_low for key, query in zip(key_lows, query_lows)
    ]
    by_states = [nn(key_lows[i], state_ref[0, i]) for i in heads]
    freshes = [
        (weights_ref[0, i, :, 128:].astype(WIDE) - nn(weights_ref[0, i, :, :128], state_ref[0, i])).astype(LOW)
        for i in heads
    ]
    from_exit = [nn(key_lows[i], exit_ref[0, i]) for i in heads]
    solves_turned = [nt(eye, solve_ref[0, i]).astype(LOW) for i in heads]
    grad_fresh = [nn(scores_turned[i], grad_lows[i]) + last * from_exit[i] for i in heads]
    grad_right = [nn(solves_turned[i], grad_fresh[i]) for i in heads]
    sides = [
        jnp.concatenate([right.astype(LOW), grad], axis=0) for right, grad in zip(grad_right, grad_lows)
    ]
    outers = [nt(side, fresh).astype(LOW) for side, fresh in zip(sides, freshes)]
    outers_turned = [nt(fresh, side).astype(LOW) for side, fresh in zip(sides, freshes)]
    side_states = [nt(sides[i], state_ref[0, i]) for i in heads]
    grads = [
        jnp.concatenate([outer[:size] * strict_low, outer[size:] * inclusive_low], axis=0)
        for outer in outers
    ]
    grads_turned = [
        jnp.concatenate([outer[:, :size] * later_strict_low, outer[:, size:] * later_low], axis=1)
        for outer in outers_turned
    ]
    by_keys = [nn(grad, key) for grad, key in zip(grads, key_lows)]
    by_both = [
        nn(grads_turned[i], jnp.concatenate([(-betas[i] * keys[i][0]).astype(LOW), query_lows[i]], axis=0))
        for i in heads
    ]
    to_exit = [nt(freshes[i], exit_ref[0, i]) for i in heads]
    rates = [
        jnp.sum(
            grad_right[i] * (values[i] - carried * by_states[i]) - by_keys[i][:size] * keys[i][0],
            axis=1,
            keepdims=True,
        )
        for i in heads
    ]
    lane = lax.broadcasted_iota(jnp.int32, rate_ref.shape[1:], 1)
    rate_sum = jnp.zeros(rate_ref.shape[1:], WIDE)
    zeros = jnp.zeros((RIM, 128), WIDE)
    for local in heads:
        rate_sum = jnp.where(lane == first_head + local, rates[local], rate_sum)
        query, query_scale = queries[local]
        key, key_scale = keys[local]
        beta = betas[local]
        grad_query = carried * side_states[local][size:] + by_keys[local][size:]
        grad_key = (
            by_both[local]
            + last * to_exit[local]
            - beta * (by_keys[local][:size] + carried * side_states[local][:size])
        )
        grad_acts = (
            query_scale * (grad_query - query * jnp.sum(query * grad_query, axis=1, keepdims=True)),
            key_scale * (grad_key - key * jnp.sum(key * grad_key, axis=1, keepdims=True)),
            beta * grad_right[local],
        )
        for index in range(3):
            slot = 3 * local + index
            room = room_ref.at[slot]
            back = back_ref.at[slot]
            grad_conv = grad_acts[index] * kept[slot]
            weight = parts[index][0][:, lanes[local]].astype(WIDE)
            own = weight[0:1] * grad_conv
            edge_sum = zeros
            tap_ref[index, 0, 0:1, lanes[local]] = jnp.sum(
                grad_conv * room[pl.ds(RIM, size), :], axis=0, keepdims=True
            )
            for step in range(1, tap_count):
                masked = grad_conv * tap_masks[step - 1]
                tap_ref[index, 0, step : step + 1, lanes[local]] = jnp.sum(
                    masked * room[pl.ds(RIM - step, size), :], axis=0, keepdims=True
                )
                back[pl.ds(0, RIM), :] = zeros
                back[pl.ds(RIM, size), :] = weight[step : step + 1] * masked
                back[pl.ds(RIM + size, RIM), :] = zeros
                own = own + back[pl.ds(RIM + step, size), :]
                edge_sum = edge_sum + back[pl.ds(step, RIM), :]
            out_ref[index, 0, :, lanes[local]] = own.astype(LOW)
            edge_ref[index, 0, :, lanes[local]] = edge_sum
            tail_ref[index, 0, :, lanes[local]] = own[size - RIM :]
    rate_ref[0] = rate_sum * beta_all * (1.0 - beta_all)


def back_call(group, groups, cols, rows, beta, taps, rim, projected, solve, weights, state, exit_grad, grad):
    row_count, size, triple = projected.shape
    head_count = triple // (3 * 128)
    count = head_count // groups
    wide = count * 128
    tap_count = taps.shape[0]

    def of_row(block):
        return pl.BlockSpec(block, lambda r: (r, 0, 0))

    def part(rows_in, index):
        return pl.BlockSpec((1, rows_in, wide), lambda r: (r, 0, index * groups + group))

    def tap_part(index):
        return pl.BlockSpec((tap_count, wide), lambda r: (0, index * groups + group))

    def per_head(*block):
        return pl.BlockSpec((1, count) + block, lambda r: (r, group, 0, 0))

    def stacked(rows_in):
        return pl.BlockSpec((3, 1, rows_in, wide), lambda r: (0, r, 0, 0))

    def stacked_type(rows_in, kind):
        return jax.ShapeDtypeStruct((3, row_count, rows_in, wide), kind)

    return pl.pallas_call(
        functools.partial(back_kernel, group * count),
        grid=(row_count,),
        in_specs=[of_row((1,) + cols.shape[1:]), of_row((1,) + rows.shape[1:]), of_row((1,) + beta.shape[1:])]
        + [tap_part(i) for i in range(3)]
        + [part(RIM, i) for i in range(3)]
        + [part(size, i) for i in range(3)]
        + [per_head(size, size), per_head(size, 256), per_head(128, 128), per_head(128, 128), part(size, 0)],
        out_specs=[
            stacked(size), stacked(RIM), stacked(RIM), stacked(tap_count), of_row((1, size, 128)),
        ],
        out_shape=[
            stacked_type(size, LOW), stacked_type(RIM, WIDE), stacked_type(RIM, WIDE),
            stacked_type(tap_count, WIDE),
            jax.ShapeDtypeStruct((row_count, size, 128), WIDE),
        ],
        scratch_shapes=[
            pltpu.VMEM((3 * count, RIM + size, 128), WIDE),
            pltpu.VMEM((3 * count, size + 2 * RIM, 128), WIDE),
        ],
        compiler_params=pltpu.CompilerParams(vmem_limit_bytes=VMEM_BYTES),
        cost_estimate=timed(36 / groups),
        name="mixer_back",
    )(
        cols, rows, beta, taps, taps, taps, rim, rim, rim, projected, projected, projected,
        solve, weights, state, exit_grad, grad,
    )


def timed(microseconds):
    return pl.CostEstimate(
        flops=int(microseconds * 1.0e9), bytes_accessed=int(microseconds * 1.0e6), transcendentals=0
    )


def shifted(value, axis, steps):
    count = lax.axis_size(axis)
    leading, last = (max(0, -steps), min(count, count - steps))
    return lax.ppermute(value, axis, [(source, source + steps) for source in range(leading, last)])


def swap(value, bit):
    count = lax.axis_size("seq")
    return lax.ppermute(value, "seq", [(source, source ^ bit) for source in range(count)])


def put(outs, pieces, moves, position):
    for piece, parts in zip(pieces, moves):
        for member, relative, rows, start, source, count in parts:
            target = pl.multiple_of((position ^ relative) * rows + start, 16)
            outs[member][pl.ds(target, count), :] = piece[source : source + count, :]


def place_kernel(moves, position_ref, *refs):
    put(refs[len(moves) :], refs[: len(moves)], moves, position_ref[0])


def place(gathered):
    pieces, moves, sizes, position = gathered
    columns = pieces[0].shape[1]
    tile = next(size for size in (1408, 1024, 512, 256, 128) if columns % size == 0)
    return pl.pallas_call(
        functools.partial(place_kernel, moves),
        grid=(columns // tile,),
        in_specs=[pl.BlockSpec(memory_space=pltpu.SMEM)]
        + [pl.BlockSpec((piece.shape[0], tile), lambda j: (0, j)) for piece in pieces],
        out_specs=[pl.BlockSpec((size, tile), lambda j: (0, j)) for size in sizes],
        out_shape=[jax.ShapeDtypeStruct((size, columns), pieces[0].dtype) for size in sizes],
        compiler_params=pltpu.CompilerParams(vmem_limit_bytes=VMEM_BYTES),
        cost_estimate=timed(1 + sum(sizes) * columns / 1.2e6),
        name="place",
    )(position, *pieces)


def join(*values):
    return lax.optimization_barrier(values)


def gather_near(shard):
    return (swap(shard, 2), swap(shard, 4)) if seq_is_cube() else None


def gather_far(near):
    if not seq_is_cube():
        return None
    by_x, by_y = near
    half = by_x.shape[0] // 2
    return swap(by_x[:half], 4), swap(by_y[half:], 2)


def gather_core(shard, near, far):
    if not seq_is_cube():
        return [lax.all_gather(shard, "seq", axis=0)]
    mine = [shard, *near, *far]
    return mine + [swap(piece, 1) for piece in mine]


def placing(pieces, sizes):
    count = lax.axis_size("seq")
    if not seq_is_cube():
        parts, moves, offset = [], [], 0
        for member, size in enumerate(sizes):
            parts.append(pieces[0][:, offset : offset + size].reshape(count * size, -1))
            moves.append(((member, 0, 0, 0, 0, count * size),))
            offset += size
        return parts, tuple(moves), tuple(count * size for size in sizes), jnp.zeros((1,), jnp.int32)
    rows = sum(sizes)
    half = rows // 2
    spans = [(0, 0, rows), (2, 0, rows), (4, 0, rows), (6, 0, half), (6, half, half)]
    spans += [(relative ^ 1, first, span) for relative, first, span in spans]
    moves = []
    for relative, first, span in spans:
        parts, offset = [], 0
        for member, size in enumerate(sizes):
            low, high = max(first, offset), min(first + span, offset + size)
            if low < high:
                parts.append((member, relative, size, low - offset, low - first, high - low))
            offset += size
        moves.append(tuple(parts))
    position = lax.axis_index("seq").astype(jnp.int32).reshape(1)
    return pieces, tuple(moves), tuple(count * size for size in sizes), position


def project_kernel(
    moves, piece_count, position_ref, inputs_ref, valid_ref, bias_ref, *refs
):
    pieces, extra_pieces = refs[:piece_count], refs[piece_count : 2 * piece_count]
    joint_ref, extra_ref, normed_ref, out_ref, beta_ref, extras_ref = refs[2 * piece_count :]
    put([joint_ref], pieces, moves, position_ref[0])

    @pl.when(pl.program_id(0) == 0)
    def _():
        put([extra_ref], extra_pieces, moves, position_ref[0])
        extra = extra_ref[...]
        row = lax.broadcasted_iota(jnp.int32, (16, 128), 0)
        lane = lax.broadcasted_iota(jnp.int32, (16, 128), 1)
        extras = nt(jnp.where(lane == row + 8, 1.0, 0.0), extra)
        extras_ref[...] = extras
        inputs = inputs_ref[...].astype(WIDE)
        normed = (inputs * rms_scale(inputs) * extras[0:1]).astype(LOW)
        normed_ref[...] = normed
        beta_ref[...] = valid_ref[:, 0:1] * jax.nn.sigmoid(nn(normed, extra) + bias_ref[...])

    out_ref[...] = nn(normed_ref[...], joint_ref[...]).astype(LOW)


def project_call(gathered, inputs, valid, bias):
    pieces, moves, sizes, position = gathered
    tokens, width = inputs.shape
    columns = pieces[0].shape[1] - 128
    tile = 1024

    def whole(shape):
        return pl.BlockSpec(shape, lambda j: (0,) * len(shape))

    last = columns // 128
    return pl.pallas_call(
        functools.partial(project_kernel, moves, len(pieces)),
        grid=(columns // tile,),
        in_specs=[
            pl.BlockSpec(memory_space=pltpu.SMEM), whole((tokens, width)), whole(valid.shape), whole(bias.shape),
        ]
        + [pl.BlockSpec((piece.shape[0], tile), lambda j: (0, j)) for piece in pieces]
        + [pl.BlockSpec((piece.shape[0], 128), lambda j: (0, last)) for piece in pieces],
        out_specs=[
            pl.BlockSpec((width, tile), lambda j: (0, j)), whole((width, 128)), whole((tokens, width)),
            pl.BlockSpec((tokens, tile), lambda j: (0, j)), whole((tokens, 128)), whole((16, width)),
        ],
        out_shape=[
            jax.ShapeDtypeStruct((width, columns), LOW),
            jax.ShapeDtypeStruct((width, 128), LOW),
            jax.ShapeDtypeStruct((tokens, width), LOW),
            jax.ShapeDtypeStruct((tokens, columns), LOW),
            jax.ShapeDtypeStruct((tokens, 128), WIDE),
            jax.ShapeDtypeStruct((16, width), WIDE),
        ],
        compiler_params=pltpu.CompilerParams(vmem_limit_bytes=VMEM_BYTES),
        cost_estimate=timed(10),
        name="project",
    )(position, inputs, valid, bias, *pieces, *pieces)


def after(value, *earlier):
    return lax.optimization_barrier((value, earlier))[0]


def outer_turn_kernel(order_ref, left_ref, right_ref, out_ref, other_ref, own_ref, turned):
    rows = out_ref.shape[1]

    @pl.when(pl.program_id(0) == 0)
    def _():
        turned[...] = left_ref[...].T
        for index in range(4):
            first = pl.multiple_of(order_ref[index] * rows, 16)
            other_ref[index * rows : (index + 1) * rows, :] = turned[pl.ds(first, rows), :]
            second = pl.multiple_of(order_ref[4 + index] * rows, 16)
            own_ref[index * rows : (index + 1) * rows, :] = turned[pl.ds(second, rows), :]

    out_ref[...] = nn(other_ref[...], right_ref[0]).astype(LOW).reshape(out_ref.shape)


def outer_kernel(left_ref, right_ref, out_ref):
    out_ref[...] = nn(left_ref[...], right_ref[0]).astype(LOW).reshape(out_ref.shape)


def outer_add_kernel(left_ref, right_ref, add_ref, out_ref):
    total = nn(left_ref[...], right_ref[0])
    out_ref[...] = (
        (total + add_ref[...].reshape(total.shape).astype(WIDE)).astype(LOW).reshape(out_ref.shape)
    )


def outer_tile(parts, columns):
    sizes = (2816, 1024, 512, 256) if parts > 1 else (512, 256)
    return next(size for size in sizes if columns % size == 0)


def outer_specs(left_rows, right):
    parts, tokens, columns = right.shape
    rows = left_rows // 4
    tile = outer_tile(parts, columns)
    steps = columns // tile
    return dict(
        grid=(parts * steps,),
        left=pl.BlockSpec((left_rows, tokens), lambda j: (0, 0)),
        right=pl.BlockSpec((1, tokens, tile), lambda j: (j // steps, 0, j % steps)),
        out=pl.BlockSpec((4, rows, tile), lambda j: (0, 0, j)),
        out_type=jax.ShapeDtypeStruct((4, rows, parts * columns), LOW),
        params=pltpu.CompilerParams(vmem_limit_bytes=VMEM_BYTES),
        cost=timed(1 + tokens * left_rows * parts * columns / 1.8e8),
    )


def seq_is_cube():
    return lax.axis_size("seq") == 8


def outer_turn(left, right, position):
    tokens, features = left.shape
    if not seq_is_cube():
        return None, left, left
    specs = outer_specs(features // 2, right)
    order = position ^ jnp.array([1, 3, 5, 7, 0, 2, 4, 6], jnp.int32)
    left_type = jax.ShapeDtypeStruct((features // 2, tokens), LOW)
    return pl.pallas_call(
        outer_turn_kernel,
        grid=specs["grid"],
        in_specs=[
            pl.BlockSpec(memory_space=pltpu.SMEM),
            pl.BlockSpec((tokens, features), lambda j: (0, 0)),
            specs["right"],
        ],
        out_specs=[specs["out"], specs["left"], specs["left"]],
        out_shape=[specs["out_type"], left_type, left_type],
        scratch_shapes=[pltpu.VMEM((features, tokens), LOW)],
        compiler_params=specs["params"],
        cost_estimate=specs["cost"],
        name="outer_turn",
    )(order, left, right)


def outer(left, right):
    if not seq_is_cube():
        return None
    specs = outer_specs(left.shape[0], right)
    return pl.pallas_call(
        outer_kernel,
        grid=specs["grid"],
        in_specs=[specs["left"], specs["right"]],
        out_specs=specs["out"],
        out_shape=specs["out_type"],
        compiler_params=specs["params"],
        cost_estimate=specs["cost"],
        name="outer",
    )(left, right)


def outer_add(left, right, received):
    if not seq_is_cube():
        full = [jnp.einsum("td,te->de", left, right[i], preferred_element_type=WIDE) for i in range(right.shape[0])]
        full = jnp.concatenate(full, axis=-1).astype(LOW)
        return lax.psum_scatter(full, "seq", scatter_dimension=0, tiled=True)
    specs = outer_specs(left.shape[0], right)
    return pl.pallas_call(
        outer_add_kernel,
        grid=specs["grid"],
        in_specs=[specs["left"], specs["right"], specs["out"]],
        out_specs=specs["out"],
        out_shape=specs["out_type"],
        compiler_params=specs["params"],
        cost_estimate=specs["cost"],
        name="outer_add",
    )(left, right, received)


def send_other(other):
    return swap(other, 1) if seq_is_cube() else None


def scatter_far(own):
    if not seq_is_cube():
        return own
    half = own.shape[1] // 2
    return own, swap(own[3, :half], 2), swap(own[3, half:], 4)


def scatter_near(stage):
    if not seq_is_cube():
        return stage
    own, to_second, to_first = stage
    half = own.shape[1] // 2
    first = jnp.concatenate(
        [own[1, :half], (own[1, half:].astype(WIDE) + to_first.astype(WIDE)).astype(LOW)], axis=0
    )
    second = jnp.concatenate(
        [(own[2, :half].astype(WIDE) + to_second.astype(WIDE)).astype(LOW), own[2, half:]], axis=0
    )
    return own[0], swap(first, 2), swap(second, 4)


def scatter_end(stage):
    if not seq_is_cube():
        return stage
    own, by_x, by_y = stage
    return (own.astype(WIDE) + by_x.astype(WIDE) + by_y.astype(WIDE)).astype(LOW)


def rows_are_line():
    return lax.axis_size("row") == 4


def row_inward(value):
    if not rows_are_line():
        return lax.psum(value, "row")
    return value, lax.ppermute(value, "row", [(0, 1), (3, 2)])


def row_across(stage):
    if not rows_are_line():
        return stage
    value, received = stage
    value = (value.astype(WIDE) + received.astype(WIDE)).astype(value.dtype)
    return value, lax.ppermute(value, "row", [(1, 2), (2, 1)])


def row_outward(stage):
    if not rows_are_line():
        return stage
    value, received = stage
    value = (value.astype(WIDE) + received.astype(WIDE)).astype(value.dtype)
    return value, lax.ppermute(value, "row", [(1, 0), (2, 3)])


def row_end(stage):
    if not rows_are_line():
        return stage.astype(WIDE)
    value, received = stage
    index = lax.axis_index("row")
    return jnp.where((index == 0) | (index == 3), received, value).astype(WIDE)


def bias_rows(value):
    if not seq_is_cube():
        return lax.psum(value, ("seq", "row"))
    return row_end(row_outward(row_across(row_inward(value))))


def on_device(
    inputs,
    lengths,
    norm_gain,
    w_qkv,
    w_beta,
    beta_bias,
    w_conv,
    w_out,
    ffn_gain,
    w_gate,
    w_up,
    w_down,
    cotangent,
):
    row_count, slot_count, width = inputs.shape
    token_count = row_count * slot_count
    head_count = beta_bias.shape[0]
    tap_count = w_conv.shape[0]
    rim_size = tap_count - 1
    pairs = row_count * head_count
    shard = norm_gain.shape[0]
    seq_count = lax.axis_size("seq")
    position = lax.axis_index("seq").astype(jnp.int32)

    by_lane = jnp.transpose(w_conv.reshape(tap_count, 3, shard), (2, 0, 1)).reshape(shard, -1)
    extra = jnp.concatenate([w_beta, norm_gain[:, None], ffn_gain[:, None], by_lane], axis=1)
    extra = jnp.pad(extra, ((0, 0), (0, 128 - extra.shape[1])))
    w_joint = jnp.concatenate([w_qkv, extra], axis=1)
    joint_near = gather_near(w_joint)
    doc_ends = jnp.cumsum(lengths, axis=1, dtype=jnp.int32)
    spots = position * slot_count - rim_size + jnp.arange(slot_count + rim_size, dtype=jnp.int32)
    ext_docs = jnp.sum(
        (spots[None, :, None] >= doc_ends[:, None, :]).astype(jnp.int32), axis=2, dtype=jnp.int32
    )
    ext_docs = jnp.where(spots[None, :] < 0, -1, ext_docs)
    own_docs = ext_docs[:, rim_size:]
    valid_mask = (spots[None, rim_size:] < doc_ends[:, -1:]).astype(WIDE)
    shown = [own_docs.astype(WIDE)]
    for offset in range(1, tap_count):
        before = ext_docs[:, rim_size - offset : rim_size - offset + slot_count]
        shown.append((before == own_docs).astype(WIDE))
    shown.append((own_docs == ext_docs[:, rim_size - 1 : rim_size]).astype(WIDE))
    shown.append((own_docs == own_docs[:, -1:]).astype(WIDE))
    shown += [valid_mask, valid_mask]
    cols = jnp.stack(shown, axis=-1)
    valid = jnp.broadcast_to(valid_mask.reshape(token_count, 1), (token_count, 8))
    rows = jnp.broadcast_to(own_docs.astype(WIDE)[:, None, :], (row_count, 8, slot_count))
    bounds = jnp.arange(seq_count, dtype=jnp.int32) * slot_count
    doc_first = jnp.sum((bounds[None, :, None] - 1 >= doc_ends[:, None, :]).astype(jnp.int32), axis=2)
    doc_last = jnp.sum(
        (bounds[None, :, None] + slot_count - 1 >= doc_ends[:, None, :]).astype(jnp.int32), axis=2
    )
    keep = (doc_first == doc_last).astype(WIDE)
    share = -(-pairs // seq_count)
    keep_pairs = jnp.pad(
        jnp.repeat(keep, head_count, axis=0), ((0, share * seq_count - pairs), (0, 0))
    )
    keep_own = lax.dynamic_slice_in_dim(keep_pairs, position * share, share, axis=0)

    joint_near, cols, rows, valid, keep_own = join(joint_near, cols, rows, valid, keep_own)
    joint_far = gather_far(joint_near)
    joint_pieces = placing(gather_core(w_joint, joint_near, joint_far), (shard,))
    gate_near = gather_near(after(w_gate, joint_far))

    tokens_in = inputs.reshape(token_count, width)
    bias_row = jnp.pad(beta_bias.astype(WIDE), (0, 128 - head_count))[None]
    joint, joint_extra, normed, projected, beta, extras = project_call(
        joint_pieces, tokens_in, valid, bias_row
    )
    first_gain, second_gain = extras[0:1], extras[1:2]
    taps = extras[2 : 2 + 3 * tap_count].reshape(tap_count, 3, seq_count, shard)
    taps = jnp.swapaxes(taps, 1, 2).reshape(tap_count, 3 * width).astype(LOW)
    projected = projected.reshape(row_count, slot_count, 3 * width)
    beta = beta.reshape(row_count, slot_count, 128)
    rim = shifted(projected[:, slot_count - RIM :], "seq", 1)

    rim, projected, gate_near = join(rim, projected, gate_near)
    gate_far = gather_far(gate_near)
    up_near = gather_near(after(w_up, gate_near))
    eff, local_out, maps, solve, weights = prepare_call(cols, rows, beta, taps, rim, projected)
    maps, gate_far, up_near = join(maps, gate_far, up_near)
    maps_here = exchange(maps.reshape((pairs,) + maps.shape[2:]), seq_count)
    gate_pieces = placing(gather_core(w_gate, gate_near, gate_far), (shard,))
    up_far = gather_far(up_near)
    out_near = gather_near(after(w_out, up_near))
    maps_here, up_far, out_near = join(maps_here, up_far, out_near)
    states_here = chain_call(chain_forward_kernel, keep_own, maps_here)
    down_near = gather_near(after(w_down, states_here))
    state = to_home(states_here, pairs).reshape((row_count, head_count, 128, 128))
    out_far = gather_far(after(out_near, states_here))
    up_pieces = placing(gather_core(w_up, up_near, after(up_far, states_here)), (shard,))
    state, out_far, down_near = join(state, out_far, down_near)
    down_far = gather_far(down_near)
    (full_out,) = place(placing(gather_core(w_out, out_near, out_far), (shard,)))
    down_pieces = gather_core(w_down, down_near, after(down_far, full_out))
    (full_down,) = place(placing(down_pieces, (w_down.shape[0],)))

    (
        heads_low, second, act, grad_pair, output, upstream_low,
        grad_hidden, grad_mix_low, grad_heads, local_grad, grad_ffn_gain,
    ) = feed_call(
        eff, local_out, state, tokens_in, cotangent.reshape(token_count, width), valid, second_gain,
        full_out, gate_pieces, up_pieces, full_down,
    )
    grad_heads = grad_heads.reshape(row_count, slot_count, width)

    grads_here = exchange(local_grad.reshape((pairs, 128, 128)), seq_count)
    other_pair, _, left_pair = outer_turn(second, grad_pair, position)
    grads_here, left_pair = join(grads_here, left_pair)
    from_pair = send_other(other_pair)
    exits_here = chain_call(chain_backward_kernel, keep_own, maps_here, grads_here)
    exit_grad = to_home(exits_here, pairs).reshape((row_count, head_count, 128, 128))
    other_down, _, left_down = outer_turn(after(act, exits_here), upstream_low[None], position)
    from_down = send_other(other_down)
    own_pair = outer_add(after(left_pair, left_down), grad_pair, from_pair)
    exit_grad, own_pair = join(exit_grad, own_pair)
    far_pair = scatter_far(own_pair)

    def pull(group, exit_grad):
        grad_parts, edges, tails, tap_sums, logits = back_call(
            group, 2, cols, rows, beta, taps, rim, projected, solve, weights, state, exit_grad, grad_heads
        )
        return grad_parts, shifted(edges.astype(LOW), "seq", -1), tails, jnp.sum(tap_sums, axis=1), logits

    def fix(grad_parts, back_rim, tails):
        fixed = lax.dynamic_update_slice(
            grad_parts, (tails + back_rim.astype(WIDE)).astype(LOW), (0, 0, slot_count - RIM, 0)
        )
        return fixed.reshape(3, token_count, -1)

    first_parts, first_rim, first_tails, first_taps, first_logits = pull(0, exit_grad)
    far_pair, first_logits, from_down = join(far_pair, first_logits, from_down)
    own_down = outer_add(after(left_down, first_logits), upstream_low[None], from_down)
    first_rim, own_down, first_parts = join(first_rim, own_down, first_parts)
    near_pair = scatter_near(after(far_pair, own_down))
    first_grad = fix(first_parts, first_rim, first_tails)
    other_first, left_other, left_own = outer_turn(normed, first_grad, position)
    from_first = send_other(other_first)
    other_out, _, left_out = outer_turn(after(heads_low, left_own), grad_mix_low[None], position)
    from_out = send_other(other_out)
    second_parts, second_rim, second_tails, second_taps, second_logits = pull(1, after(exit_grad, left_out))
    near_pair, from_first, from_out, second_logits = join(near_pair, from_first, from_out, second_logits)
    shard_pair = scatter_end(near_pair)
    pair = row_inward(shard_pair)
    far_down = scatter_far(after(own_down, second_logits))
    own_first = outer_add(after(left_own, second_logits, shard_pair), first_grad, from_first)
    own_out = outer_add(after(left_out, own_first), grad_mix_low[None], from_out)
    second_rim, own_out, second_parts, own_first = join(second_rim, own_out, second_parts, own_first)
    far_first = scatter_far(own_first)
    second_grad = fix(second_parts, second_rim, second_tails)
    other_second = outer(after(left_other, own_out), second_grad)
    other_second, far_first, far_down, own_out = join(other_second, far_first, far_down, own_out)
    from_second = send_other(other_second)
    near_first = scatter_near(far_first)
    near_down = scatter_near(far_down)
    far_out = scatter_far(own_out)

    grad_logits = (first_logits + second_logits).reshape(token_count, 128)
    grad_inputs, grad_norm_gain = project_back_call(
        first_grad, after(second_grad, other_second), joint, grad_logits, joint_extra, tokens_in, first_gain, grad_hidden
    )
    grad_beta_w = jnp.einsum(
        "td,th->dh", normed.astype(WIDE), grad_logits[:, :head_count], precision=lax.Precision.HIGHEST
    )
    grad_conv_w = jnp.stack([first_taps, second_taps], axis=2)
    grad_conv_w = jnp.swapaxes(grad_conv_w, 0, 1).reshape(tap_count, seq_count, 3, shard)
    minor = jnp.concatenate(
        [
            grad_beta_w.reshape(seq_count, shard, head_count),
            grad_norm_gain.reshape(seq_count, shard, 1),
            grad_ffn_gain.reshape(seq_count, shard, 1),
            jnp.transpose(grad_conv_w, (1, 3, 0, 2)).reshape(seq_count, shard, 3 * tap_count),
        ],
        axis=2,
    )
    minor = jnp.pad(minor, ((0, 0), (0, 0), (0, 128 - minor.shape[2])))
    if seq_is_cube():
        order = position ^ jnp.array([1, 3, 5, 7, 0, 2, 4, 6], jnp.int32)
        minor = jnp.take(minor, order, axis=0)
        own_minor = (minor[4:] + swap(minor[:4].astype(LOW), 1).astype(WIDE)).astype(LOW)
    else:
        own_minor = lax.psum_scatter(
            minor.reshape(width, 128).astype(LOW), "seq", scatter_dimension=0, tiled=True
        )
    from_second, grad_inputs, near_first, far_out, own_minor, grad_logits, pair = join(
        from_second, grad_inputs, near_first, far_out, own_minor, grad_logits, pair
    )
    pair = row_across(pair)
    first = row_inward(scatter_end(near_first))
    near_out = scatter_near(far_out)
    own_second = jnp.concatenate(
        [outer_add(left_own, second_grad, from_second), own_minor], axis=-1
    )
    far_second = scatter_far(own_second)
    far_second, near_down, near_out, first = join(far_second, near_down, near_out, first)
    near_second = scatter_near(far_second)
    down = row_inward(scatter_end(near_down))
    out = row_inward(scatter_end(near_out))
    first = row_across(first)
    bias = jnp.sum(grad_logits, axis=0, keepdims=True)
    if seq_is_cube():
        bias = bias + swap(bias, 1)
    near_second, first, down, out, bias, pair = join(near_second, first, down, out, bias, pair)
    pair = row_outward(pair)
    second_ = row_inward(scatter_end(near_second))
    first = row_outward(first)
    down = row_across(down)
    out = row_across(out)
    if seq_is_cube():
        bias = bias + swap(bias, 2)
    second_, first, down, out, bias = join(second_, first, down, out, bias)
    second_ = row_across(second_)
    down = row_outward(down)
    out = row_outward(out)
    if seq_is_cube():
        bias = bias + swap(bias, 4)
    second_, down, out, bias = join(second_, down, out, bias)
    second_ = row_outward(second_)
    bias = bias_rows(bias)
    second_, pair, first, down, out = join(second_, pair, first, down, out)
    total_first, total_second, total_down, total_out = (row_end(value) for value in (first, second_, down, out))
    total_pair = row_end(pair)
    bias_total = bias[0, :head_count]
    half = width // 2
    total_qkv = jnp.concatenate(
        [
            total[:, part * half : (part + 1) * half]
            for part in range(3)
            for total in (total_first, total_second)
        ],
        axis=1,
    )
    small = total_second[:, 3 * half :]
    columns = head_count + 2
    total_conv = jnp.transpose(
        small[:, columns : columns + 3 * tap_count].reshape(shard, tap_count, 3), (1, 2, 0)
    ).reshape(tap_count, -1)
    units = w_gate.shape[1]
    return (
        output.reshape(inputs.shape),
        grad_inputs.reshape(inputs.shape),
        small[:, head_count],
        total_qkv,
        small[:, :head_count],
        bias_total,
        total_conv,
        total_out,
        small[:, head_count + 1],
        total_pair[:, :units],
        total_pair[:, units:],
        total_down,
    )


def solution(mesh):
    placed = (
        P("row", "seq", None),
        P("row", None),
        P("seq"),
        P("seq", None),
        P("seq", None),
        P(),
        P(None, "seq"),
        P("seq", None),
        P("seq"),
        P("seq", None),
        P("seq", None),
        P("seq", None),
        P("row", "seq", None),
    )
    return jax.shard_map(
        on_device,
        mesh=mesh,
        in_specs=placed,
        out_specs=(
            P("row", "seq", None),
            P("row", "seq", None),
            P("seq"),
            P("seq", None),
            P("seq", None),
            P(),
            P(None, "seq"),
            P("seq", None),
            P("seq"),
            P("seq", None),
            P("seq", None),
            P("seq", None),
        ),
        check_vma=False,
    )
```

time: 964 us -> 618 us (0.64)
  waiting for transfers between devices: 514 us -> 200 us
  matrix products: 148 us -> 0.76 us
  starting transfers between devices: 12.7 us -> 122 us
  Pallas kernels: 148 us -> 212 us
  blocking collectives: 63.6 us -> 0 us
  between operations: 14.9 us -> 2.37 us
    reduce_scatter x7 -> x0, waiting for transfers between devices: 292 us -> none  [the longest x1 62.9 us: on_device(): shard_up = scatter(grad_up_w.astype(LOW))]
    ppermute x0 -> x92, waiting for transfers between devices: none -> 176 us  [the longest x74 114 us: swap(): lax.ppermute(value, 'seq', [(source, source ^ bit) for source in range(co...]
    dot_general x22 -> x1, matrix products: 148 us -> 0.76 us  [on_device(): jnp.einsum('td,th->dh', normed.astype(WIDE), grad_logits[:, :head_count],...]
    pallas_call x3 -> x17, Pallas kernels: 51.7 us -> 183 us  [the longest x1 48.8 us: feed_call(): pl.pallas_call(functools.partial(feed_kernel, gate[1], up[1]), grid=(unit...]
    psum x1 -> x0, waiting for transfers between devices: 106 us -> none  [on_device(): lax.psum(shard, 'row').astype(WIDE)]
    ppermute x0 -> x92, starting transfers between devices: none -> 103 us  [the longest x74 56.3 us: swap(): lax.ppermute(value, 'seq', [(source, source ^ bit) for source in range(co...]
    pallas_call x1, Pallas kernels: 89.8 us -> 21.5 us  [prepare_call(): pl.pallas_call(prepare_kernel, grid=(row_count, groups), in_specs=[of_row...]
    unnamed x15 -> x0, waiting for transfers between devices: 45.3 us -> none
  transfers between devices with their start and end apart: 18 -> 99, of which waited for: 12 -> 28; matrix products, arithmetic and copies ran while one was open for 15% -> 7% of each run, Pallas kernels for 10% -> 25%
where the time goes in v2:
time: 618 us; the launch traced here: 609 us
  Pallas kernels  212 us (34%)
  waiting for transfers between devices  200 us (32%)
  starting transfers between devices  122 us (20%)
  local copies, waits for them, and re-layouts  42.6 us (7%)
  other arithmetic  28.5 us (5%)
    ppermute x74, waiting for transfers between devices, swap(): lax.ppermute(value, 'seq', [(source, source ^ bit) for source in range(co...  114 us
    ppermute x6, waiting for transfers between devices, row_outward(): return (value, lax.ppermute(value, 'row', [(1, 0), (2, 3)]))  57.3 us
    ppermute x74, starting transfers between devices, swap(): lax.ppermute(value, 'seq', [(source, source ^ bit) for source in range(co...  56.3 us
    pallas_call x1, Pallas kernels, feed_call(): pl.pallas_call(functools.partial(feed_kernel, gate[1], up[1]), grid=(unit...  48.8 us
    pallas_call x2, Pallas kernels, back_call(): pl.pallas_call(functools.partial(back_kernel, group * count), grid=(row_c...  38.6 us
    ppermute x6, starting transfers between devices, row_inward(): return (value, lax.ppermute(value, 'row', [(0, 1), (3, 2)]))  34.6 us
    pallas_call x5, Pallas kernels, outer_add(): pl.pallas_call(outer_add_kernel, grid=specs['grid'], in_specs=[specs['lef...  30.1 us
    pallas_call x4, Pallas kernels, outer_turn(): pl.pallas_call(outer_turn_kernel, grid=specs['grid'], in_specs=[pl.BlockS...  28 us
  transfers between devices with their start and end apart: 99, of which 28 were waited for; matrix products, arithmetic and copies ran while one was open for 7% of the time, Pallas kernels for 25%

profile of v2, /device:TPU:0, one launch (start us, length us, event | category | flops | bytes accessed | tf_op | source)
XLA Modules:
  0.0 608.6 jit_solution(2590623242716006104)
XLA Ops:
  3.4 3.0 collective-permute-start
  10.1 14.6 %collective-permute-done.refs_1_.refs_11_ = bf16[128,3200]{1,0:T(8,128)(2,1)S(1)} collective-permute-done((bf16[128,3200]{1,0:T(8,128)(2,1)S(1)}, bf16[128,3200]{1,0:T(8,128)(2,1)S(1)}, u32[]{:S(2)}, u32[]{:S(2)}) %collective-permute-start) | collective-permute-done | bytes 819232 | tf_op jit(solution)/shard_map/ppermute | solution.py:669
  27.8 1.6 collective-permute-start.2
  30.6 7.3 %collective-permute-done.2.refs_3_.refs_13_ = bf16[64,3200]{1,0:T(8,128)(2,1)S(1)} collective-permute-done((bf16[64,3200]{1,0:T(8,128)(2,1)S(1)}, bf16[64,3200]{1,0:T(8,128)(2,1)S(1)}, u32[]{:S(2)}, u32[]{:S(2)}) %collective-permute-start.2) | collective-permute-done | bytes 409632 | tf_op jit(solution)/shard_map/ppermute | solution.py:669
  42.4 11.2 %project.1 = (bf16[1024,3072]{1,0:T(8,128)(2,1)}, bf16[1024,128]{1,0:T(8,128)(2,1)}, bf16[768,1024]{1,0:T(8,128)(2,1)}, bf16[768,3072]{1,0:T(8,128)(2,1)}, f32[768,128]{1,0:T(8,128)}, /*index=5*/f32[16,1024]{1,0:T(8,128)}) custom-call(s32[1]{0:T(128)} %bitcast.position_ref, bf16[768,1024]{1,0:T(8,128)(2,1)} %bitcast.196, ...), custom_call_target="tpu_custom_call" | custom-call | flops 10000000000 | bytes 10000000 | tf_op jit(solution)/shard_map/project/pallas_call | solution.py:782
  54.5 1.9 collective-permute-start.9
  58.9 3.5 collective-permute-start.14
  66.5 21.5 %prepare.1 = (bf16[3,8,256,128]{3,2,1,0:T(8,128)(2,1)}, f32[3,256,1024]{2,1,0:T(8,128)}, bf16[3,8,128,256]{3,2,1,0:T(8,128)(2,1)}, bf16[3,8,256,256]{3,2,1,0:T(8,128)(2,1)}, bf16[3,8,256,256]{3,2,1,0:T(8,128)(2,1)}) custom-call(f32[3,256,8]{2,1,0:T(8,128)} %copy.185.cols_ref, f32[3,8,256]{2,1,0:T(8,128)} %broadcast_in_dim.72.rows_ref, ...), custom_call_target="tpu_custom_call" | custom-call | flops 22000001024 | bytes 22000000 | tf_op jit(solution)/shard_map/prepare/pallas_call | solution.py:216
  88.9 4.0 all-to-all-start
  93.0 2.0 collective-permute-start.16
  98.2 28.2 %collective-permute-done.18.refs_1_ = bf16[128,1024]{1,0:T(8,128)(2,1)S(1)} collective-permute-done((bf16[128,1024]{1,0:T(8,128)(2,1)}, bf16[128,1024]{1,0:T(8,128)(2,1)S(1)}, u32[]{:S(2)}, u32[]{:S(2)}) %collective-permute-start.18) | collective-permute-done | bytes 262176 | tf_op jit(solution)/shard_map/ppermute | solution.py:669
  129.0 3.4 chain.2
  136.6 18.0 %collective-permute-done.20.refs_3_ = bf16[64,1024]{1,0:T(8,128)(2,1)S(1)} collective-permute-done((bf16[64,1024]{1,0:T(8,128)(2,1)S(1)}, bf16[64,1024]{1,0:T(8,128)(2,1)S(1)}, u32[]{:S(2)}, u32[]{:S(2)}) %collective-permute-start.20) | collective-permute-done | bytes 131104 | tf_op jit(solution)/shard_map/ppermute | solution.py:669
  155.9 3.7 all-to-all-start.1
  160.2 11.9 %all-to-all-done.1 = bf16[8,3,128,128]{3,2,1,0:T(8,128)(2,1)S(1)} async-done(((bf16[8,3,128,128]{3,2,1,0:T(8,128)(2,1)}), bf16[8,3,128,128]{3,2,1,0:T(8,128)(2,1)S(1)}, u32[]{:S(2)}, u32[]{:S(2)}) %all-to-all-start.1) | async-done | bytes 786464 | tf_op jit(solution)/shard_map/all_to_all | solution.py:296
  176.7 3.2 collective-permute-done.29.refs_3_
  179.9 6.2 %collective-permute-done.30.refs_4_ = bf16[176,1024]{1,0:T(8,128)(2,1)} collective-permute-done((bf16[176,1024]{1,0:T(8,128)(2,1)S(1)}, bf16[176,1024]{1,0:T(8,128)(2,1)}, u32[]{:S(2)}, u32[]{:S(2)}) %collective-permute-start.30) | collective-permute-done | bytes 360480 | tf_op jit(solution)/shard_map/ppermute | solution.py:669
  186.1 3.0 place.2.w_out_ref
  193.6 5.5 place.3.down_ref
  200.6 48.8 %feed.1 = (bf16[768,1024]{1,0:T(8,128)(2,1)}, bf16[768,1024]{1,0:T(8,128)(2,1)}, bf16[768,2816]{1,0:T(8,128)(2,1)}, bf16[2,768,2816]{2,1,0:T(8,128)(2,1)}, bf16[...) custom-call(s32[1]{0:T(128)} %bitcast.position_ref, ...), custom_call_target="tpu_custom_call" | custom-call | flops 38000001024 | bytes 38000000 | tf_op jit(solution)/shard_map/feed/pallas_call | solution.py:381
  249.4 10.0 %outer_turn.4 = (bf16[4,128,5632]{2,1,0:T(8,128)(2,1)}, bf16[512,768]{1,0:T(8,128)(2,1)}, bf16[512,768]{1,0:T(8,128)(2,1)}) custom-call(s32[8]{0:T(128)} %broadcast_xor_fusion.order_ref, bf16[768,1024]{1,0:T(8,128)(2,1)} %get-tuple-element.240.left_ref, bf16[2,768,2816]{2,1,0:T(8,128)(2,1)} %get-tuple-element.241.right_ref), custom_call_target="tpu_custom_call" | custom-call | flops 13303291904 | bytes 13303291 | tf_op jit(solution)/shard_map/outer_turn/pallas_call | solution.py:870
  259.5 3.5 all-to-all-start.2
  263.1 12.5 %all-to-all-done.2.grads_ref = bf16[8,3,128,128]{3,2,1,0:T(8,128)(2,1)S(1)} async-done(((bf16[8,3,128,128]{3,2,1,0:T(8,128)(2,1)}), bf16[8,3,128,128]{3,2,1,0:T(8,128)(2,1)S(1)}, u32[]{:S(2)}, u32[]{:S(2)}) %all-to-all-start.2) | async-done | bytes 786464 | tf_op jit(solution)/shard_map/all_to_all | solution.py:292
  276.4 3.5 chain.3
  280.0 3.5 all-to-all-start.3
  283.5 8.2 %outer_turn.5 = (bf16[4,352,1024]{2,1,0:T(8,128)(2,1)}, bf16[1408,768]{1,0:T(8,128)(2,1)}, bf16[1408,768]{1,0:T(8,128)(2,1)}) custom-call(s32[8]{0:T(128)} %broadcast_xor_fusion.order_ref, bf16[768,2816]{1,0:T(8,128)(2,1)} %get-tuple-element.246.left_ref, bf16[1,768,1024]{2,1,0:T(8,128)(2,1)} %bitcast.205), custom_call_target="tpu_custom_call" | custom-call | flops 7151645696 | bytes 7151645 | tf_op jit(solution)/shard_map/outer_turn/pallas_call | solution.py:870
  292.1 9.7 %outer_add.5 = bf16[4,128,5632]{2,1,0:T(8,128)(2,1)} custom-call(bf16[512,768]{1,0:T(8,128)(2,1)} %get-tuple-element.249.left_ref, bf16[2,768,2816]{2,1,0:T(8,128)(2,1)} %get-tuple-element.241.right_ref, bf16[4,128,5632]{2,1,0:T(8,128)(2,1)} %collective-permute-done.46.add_ref), custom_call_target="tpu_custom_call" | custom-call | flops 13303291904 | bytes 13303291 | tf_op jit(solution)/shard_map/outer_add/pallas_call | solution.py:909
  301.9 2.6 slice_bitcast_fusion.4
  304.4 1.7 collective-permute-start.48
  307.6 19.3 %mixer_back.2 = (bf16[3,3,256,512]{3,2,1,0:T(8,128)(2,1)}, f32[3,3,8,512]{3,2,1,0:T(8,128)}, f32[3,3,8,512]{3,2,1,0:T(8,128)}, f32[3,3,4,512]{3,2,1,0:T(4,128)}, f32[3,256,128]{2,1,0:T(8,128)}) custom-call(f32[3,256,8]{2,1,0:T(8,128)} %copy.185.cols_ref, f32[3,8,256]{2,1,0:T(8,128)} %broadcast_in_dim.72.rows_ref, f32[3,256,128]{2,1,0:T(8,128)} %bitcast.208, ...), custom_call_target="tpu_custom_call" | custom-call | flops 17999998976 | bytes 18000000 | tf_op jit(solution)/shard_map/mixer_back/pallas_call | solution.py:626
  330.1 6.5 %outer_add.6 = bf16[4,352,1024]{2,1,0:T(8,128)(2,1)} custom-call(bf16[1408,768]{1,0:T(8,128)(2,1)} %get-tuple-element.258.left_ref, bf16[1,768,1024]{2,1,0:T(8,128)(2,1)} %bitcast.206, bf16[4,352,1024]{2,1,0:T(8,128)(2,1)} %collective-permute-done.50.add_ref), custom_call_target="tpu_custom_call" | custom-call | flops 7151645696 | bytes 7151645 | tf_op jit(solution)/shard_map/outer_add/pallas_call | solution.py:909
  337.1 2.1 collective-permute-start.53
  340.6 5.5 outer_turn.6
  346.1 4.3 outer_turn.7
  350.4 19.3 %mixer_back.3 = (bf16[3,3,256,512]{3,2,1,0:T(8,128)(2,1)}, f32[3,3,8,512]{3,2,1,0:T(8,128)}, f32[3,3,8,512]{3,2,1,0:T(8,128)}, f32[3,3,4,512]{3,2,1,0:T(4,128)}, f32[3,256,128]{2,1,0:T(8,128)}) custom-call(f32[3,256,8]{2,1,0:T(8,128)} %copy.185.cols_ref, f32[3,8,256]{2,1,0:T(8,128)} %broadcast_in_dim.72.rows_ref, f32[3,256,128]{2,1,0:T(8,128)} %bitcast.209, ...), custom_call_target="tpu_custom_call" | custom-call | flops 17999998976 | bytes 18000000 | tf_op jit(solution)/shard_map/mixer_back/pallas_call | solution.py:626
  375.1 2.3 add_convert_fusion.2
  377.4 4.6 collective-permute-start.66
  383.2 2.3 collective-permute-start.58
  387.0 5.4 outer_add.7
  392.3 3.6 outer_add.8
  399.2 4.8 outer.1
  405.0 13.3 %project_back.1 = (bf16[768,1024]{1,0:T(8,128)(2,1)}, f32[1,1024]{1,0:T(1,128)}) custom-call(bf16[3,768,512]{2,1,0:T(8,128)(2,1)} %bitcast.194, bf16[3,768,512]{2,1,0:T(8,128)(2,1)} %bitcast.190, bf16[1024,3072]{1,0:T(8,128)(2,1)} %get-tuple-element.300.weight_ref, f32[768,128]{1,0:T(8,128)} %bitcast.155, bf16[1024,128]{1,0:T(8,128)(2,1)} %get-tuple-element.301.extra_ref, ...), custom_call_target="tpu_custom_call" | custom-call | flops 10000000000 | bytes 10000000 | tf_op jit(solution)/shard_map/project_back/pallas_call | solution.py:452
  421.8 2.1 collective-permute-start.62
  429.3 8.4 %collective-permute-done.63 = bf16[64,1024]{1,0:T(8,128)(2,1)S(1)} collective-permute-done((bf16[64,1024]{1,0:T(8,128)(2,1)S(1)}, bf16[64,1024]{1,0:T(8,128)(2,1)S(1)}, u32[]{:S(2)}, u32[]{:S(2)}) %collective-permute-start.63) | collective-permute-done | bytes 131104 | tf_op jit(solution)/shard_map/ppermute | solution.py:669
  438.7 4.6 collective-permute-done.64
  448.1 1.6 collective-permute-start.72
  449.7 1.7 add_convert_fusion.1
  451.4 5.0 outer_add.9
  458.1 4.3 collective-permute-done.70
  466.1 5.0 collective-permute-done.67
  472.9 2.9 collective-permute-start.78
  475.9 1.7 add_convert_fusion.5
  480.6 2.0 collective-permute-done.78
  484.1 4.0 collective-permute-done.75
  488.1 2.6 collective-permute-done.74
  492.1 2.2 collective-permute-start.85
  497.8 23.0 %collective-permute-start.81 = (bf16[128,1664]{1,0:T(8,128)(2,1)S(1)}, bf16[128,1664]{1,0:T(8,128)(2,1)S(1)}, u32[]{:S(2)}, u32[]{:S(2)}) collective-permute-start(bf16[128,1664]{1,0:T(8,128)(2,1)S(1)} %add_convert_fusion.8), channel_id=1, source_target_pairs={{0,1},{3,2},{4,5},{7,6},{8,9},{11,10},{12,13},{15,14},{16,17},{19,... | collective-permute-start | bytes 1277960 | tf_op jit(solution)/shard_map/ppermute | solution.py:960
  522.4 6.0 collective-permute-done.82
  533.3 3.2 collective-permute-done.89
  536.5 38.8 %collective-permute-done.88 = bf16[128,1024]{1,0:T(8,128)(2,1)S(1)} collective-permute-done((bf16[128,1024]{1,0:T(8,128)(2,1)S(1)}, bf16[128,1024]{1,0:T(8,128)(2,1)S(1)}, u32[]{:S(2)}, u32[]{:S(2)}) %collective-permute-start.88) | collective-permute-done | bytes 262176 | tf_op jit(solution)/shard_map/ppermute | solution.py:976
  583.3 6.1 collective-permute-done.94
  589.9 6.5 %collective-permute-done.90 = bf16[128,1664]{1,0:T(8,128)(2,1)S(1)} collective-permute-done((bf16[128,1664]{1,0:T(8,128)(2,1)S(1)}, bf16[128,1664]{1,0:T(8,128)(2,1)S(1)}, u32[]{:S(2)}, u32[]{:S(2)}) %collective-permute-start.90) | collective-permute-done | bytes 426016 | tf_op jit(solution)/shard_map/ppermute | solution.py:976
  597.2 1.6 select_convert_fusion
  598.8 1.8 fusion.23
  (432 shorter events, 120.4 us)
Async XLA Ops:
  3.4 21.2 %collective-permute-start = (bf16[128,3200]{1,0:T(8,128)(2,1)S(1)}, bf16[128,3200]{1,0:T(8,128)(2,1)S(1)}, u32[]{:S(2)}, u32[]{:S(2)}) collective-permute-start(bf16[128,3200]{1,0:T(8,128)(2,1)S(1)} %fusion.3.refs_0_.refs_10_), channel_id=1, source_target_pairs={{0,8},{4,12},{8,0},{12,4},{16,24},{20,28},{24,16},{28,20},{1,9},{5... | collective-permute-start | bytes 2457608 | tf_op jit(solution)/shard_map/ppermute | solution.py:669
  6.4 19.7 %collective-permute-start.1 = (bf16[128,3200]{1,0:T(8,128)(2,1)S(1)}, bf16[128,3200]{1,0:T(8,128)(2,1)S(1)}, u32[]{:S(2)}, u32[]{:S(2)}) collective-permute-start(bf16[128,3200]{1,0:T(8,128)(2,1)S(1)} %fusion.3.refs_0_.refs_10_), channel_id=1, source_target_pairs={{0,16},{4,20},{8,24},{12,28},{16,0},{20,4},{24,8},{28,12},{1,17},{... | collective-permute-start | bytes 2457608 | tf_op jit(solution)/shard_map/ppermute | solution.py:669
  8.0 31.8 %collective-permute-start.4 = (bf16[128,3200]{1,0:T(8,128)(2,1)S(1)}, bf16[128,3200]{1,0:T(8,128)(2,1)}, u32[]{:S(2)}, u32[]{:S(2)}) collective-permute-start(bf16[128,3200]{1,0:T(8,128)(2,1)S(1)} %fusion.3.refs_0_.refs_10_), channel_id=1, source_target_pairs={{0,4},{4,0},{8,12},{12,8},{16,20},{20,16},{24,28},{28,24},{1,5},{5... | collective-permute-start | bytes 2457608 | tf_op jit(solution)/shard_map/ppermute | solution.py:669
  30.0 11.1 %collective-permute-start.5 = (bf16[128,3200]{1,0:T(8,128)(2,1)S(1)}, bf16[128,3200]{1,0:T(8,128)(2,1)S(1)}, u32[]{:S(2)}, u32[]{:S(2)}) collective-permute-start(bf16[128,3200]{1,0:T(8,128)(2,1)S(1)} %collective-permute-done.refs_1_.refs_11_), channel_id=1, source_target_pairs={{0,4},{4,0},{8,12},{12,8},{16,20},{20,16},{24,28},{28,24},{1,5},{5... | collective-permute-start | bytes 2457608 | tf_op jit(solution)/shard_map/ppermute | solution.py:669
  30.0 11.1 %collective-permute-start.6 = (bf16[128,3200]{1,0:T(8,128)(2,1)S(1)}, bf16[128,3200]{1,0:T(8,128)(2,1)S(1)}, u32[]{:S(2)}, u32[]{:S(2)}) collective-permute-start(bf16[128,3200]{1,0:T(8,128)(2,1)S(1)} %collective-permute-done.1.refs_2_.refs_12_), channel_id=1, source_target_pairs={{0,4},{4,0},{8,12},{12,8},{16,20},{20,16},{24,28},{28,24},{1,5},{5... | collective-permute-start | bytes 2457608 | tf_op jit(solution)/shard_map/ppermute | solution.py:669
  39.7 19.1 %collective-permute-start.10 = (bf16[128,2816]{1,0:T(8,128)(2,1)}, bf16[128,2816]{1,0:T(8,128)(2,1)S(1)}, u32[]{:S(2)}, u32[]{:S(2)}) collective-permute-start(bf16[128,2816]{1,0:T(8,128)(2,1)} %refs_0_.5), channel_id=1, source_target_pairs={{0,8},{4,12},{8,0},{12,4},{16,24},{20,28},{24,16},{28,20},{1,9},{5... | collective-permute-start | bytes 2162696 | tf_op jit(solution)/shard_map/ppermute | solution.py:669
  40.4 18.5 %collective-permute-start.11 = (bf16[128,2816]{1,0:T(8,128)(2,1)}, bf16[128,2816]{1,0:T(8,128)(2,1)}, u32[]{:S(2)}, u32[]{:S(2)}) collective-permute-start(bf16[128,2816]{1,0:T(8,128)(2,1)} %refs_0_.5), channel_id=1, source_target_pairs={{0,16},{4,20},{8,24},{12,28},{16,0},{20,4},{24,8},{28,12},{1,17},{... | collective-permute-start | bytes 2162696 | tf_op jit(solution)/shard_map/ppermute | solution.py:669
  58.9 29.1 %collective-permute-start.14 = (bf16[128,2816]{1,0:T(8,128)(2,1)}, bf16[128,2816]{1,0:T(8,128)(2,1)S(1)}, u32[]{:S(2)}, u32[]{:S(2)}) collective-permute-start(bf16[128,2816]{1,0:T(8,128)(2,1)} %refs_10_.1), channel_id=1, source_target_pairs={{0,8},{4,12},{8,0},{12,4},{16,24},{20,28},{24,16},{28,20},{1,9},{5... | collective-permute-start | bytes 2162696 | tf_op jit(solution)/shard_map/ppermute | solution.py:669
  62.4 26.4 %collective-permute-start.15 = (bf16[128,2816]{1,0:T(8,128)(2,1)}, bf16[128,2816]{1,0:T(8,128)(2,1)}, u32[]{:S(2)}, u32[]{:S(2)}) collective-permute-start(bf16[128,2816]{1,0:T(8,128)(2,1)} %refs_10_.1), channel_id=1, source_target_pairs={{0,16},{4,20},{8,24},{12,28},{16,0},{20,4},{24,8},{28,12},{1,17},{... | collective-permute-start | bytes 2162696 | tf_op jit(solution)/shard_map/ppermute | solution.py:669
  64.8 23.2 %collective-permute-start.12 = (bf16[64,2816]{1,0:T(8,128)(2,1)S(1)}, bf16[64,2816]{1,0:T(8,128)(2,1)S(1)}, u32[]{:S(2)}, u32[]{:S(2)}) collective-permute-start(bf16[64,2816]{1,0:T(8,128)(2,1)S(1)} %slice.239), channel_id=1, source_target_pairs={{0,16},{4,20},{8,24},{12,28},{16,0},{20,4},{24,8},{28,12},{1,17},{... | collective-permute-start | bytes 1081352 | tf_op jit(solution)/shard_map/ppermute | solution.py:669
  65.5 22.5 %collective-permute-start.13 = (bf16[64,2816]{1,0:T(8,128)(2,1)S(1)}, bf16[64,2816]{1,0:T(8,128)(2,1)S(1)}, u32[]{:S(2)}, u32[]{:S(2)}) collective-permute-start(bf16[64,2816]{1,0:T(8,128)(2,1)S(1)} %slice.240), channel_id=1, source_target_pairs={{0,8},{4,12},{8,0},{12,4},{16,24},{20,28},{24,16},{28,20},{1,9},{5... | collective-permute-start | bytes 1081352 | tf_op jit(solution)/shard_map/ppermute | solution.py:669
  88.9 39.0 %all-to-all-start = ((bf16[8,3,128,256]{3,2,1,0:T(8,128)(2,1)}), bf16[8,3,128,256]{3,2,1,0:T(8,128)(2,1)S(1)}, u32[]{:S(2)}, u32[]{:S(2)}) async-start(bf16[8,3,128,256]{3,2,1,0:T(8,128)(2,1)} %bitcast.157), calls=%async_computation | async-start | bytes 3145728 | tf_op jit(solution)/shard_map/all_to_all | solution.py:292
  93.0 33.4 %collective-permute-start.16 = (bf16[64,2816]{1,0:T(8,128)(2,1)S(1)}, bf16[64,2816]{1,0:T(8,128)(2,1)S(1)}, u32[]{:S(2)}, u32[]{:S(2)}) collective-permute-start(bf16[64,2816]{1,0:T(8,128)(2,1)S(1)} %slice.241), channel_id=1, source_target_pairs={{0,16},{4,20},{8,24},{12,28},{16,0},{20,4},{24,8},{28,12},{1,17},{... | collective-permute-start | bytes 1081352 | tf_op jit(solution)/shard_map/ppermute | solution.py:669
  96.0 31.8 %collective-permute-start.17 = (bf16[64,2816]{1,0:T(8,128)(2,1)S(1)}, bf16[64,2816]{1,0:T(8,128)(2,1)}, u32[]{:S(2)}, u32[]{:S(2)}) collective-permute-start(bf16[64,2816]{1,0:T(8,128)(2,1)S(1)} %slice.242), channel_id=1, source_target_pairs={{0,8},{4,12},{8,0},{12,4},{16,24},{20,28},{24,16},{28,20},{1,9},{5... | collective-permute-start | bytes 1081352 | tf_op jit(solution)/shard_map/ppermute | solution.py:669
  97.5 28.8 %collective-permute-start.18 = (bf16[128,1024]{1,0:T(8,128)(2,1)}, bf16[128,1024]{1,0:T(8,128)(2,1)S(1)}, u32[]{:S(2)}, u32[]{:S(2)}) collective-permute-start(bf16[128,1024]{1,0:T(8,128)(2,1)} %refs_0_.3), channel_id=1, source_target_pairs={{0,8},{4,12},{8,0},{12,4},{16,24},{20,28},{24,16},{28,20},{1,9},{5... | collective-permute-start | bytes 786440 | tf_op jit(solution)/shard_map/ppermute | solution.py:669
  98.1 28.2 %collective-permute-start.19 = (bf16[128,1024]{1,0:T(8,128)(2,1)}, bf16[128,1024]{1,0:T(8,128)(2,1)S(1)}, u32[]{:S(2)}, u32[]{:S(2)}) collective-permute-start(bf16[128,1024]{1,0:T(8,128)(2,1)} %refs_0_.3), channel_id=1, source_target_pairs={{0,16},{4,20},{8,24},{12,28},{16,0},{20,4},{24,8},{28,12},{1,17},{... | collective-permute-start | bytes 786440 | tf_op jit(solution)/shard_map/ppermute | solution.py:669
  98.2 38.4 %collective-permute-start.24 = (bf16[128,1024]{1,0:T(8,128)(2,1)}, bf16[128,1024]{1,0:T(8,128)(2,1)}, u32[]{:S(2)}, u32[]{:S(2)}) collective-permute-start(bf16[128,1024]{1,0:T(8,128)(2,1)} %refs_0_.3), channel_id=1, source_target_pairs={{0,4},{4,0},{8,12},{12,8},{16,20},{20,16},{24,28},{28,24},{1,5},{5... | collective-permute-start | bytes 786440 | tf_op jit(solution)/shard_map/ppermute | solution.py:669
  132.4 27.2 %collective-permute-start.22 = (bf16[352,1024]{1,0:T(8,128)(2,1)}, bf16[352,1024]{1,0:T(8,128)(2,1)S(1)}, u32[]{:S(2)}, u32[]{:S(2)}) collective-permute-start(bf16[352,1024]{1,0:T(8,128)(2,1)} %refs_0_.4), channel_id=1, source_target_pairs={{0,8},{4,12},{8,0},{12,4},{16,24},{20,28},{24,16},{28,20},{1,9},{5... | collective-permute-start | bytes 2162696 | tf_op jit(solution)/shard_map/ppermute | solution.py:669
  133.7 26.4 %collective-permute-start.23 = (bf16[352,1024]{1,0:T(8,128)(2,1)}, bf16[352,1024]{1,0:T(8,128)(2,1)}, u32[]{:S(2)}, u32[]{:S(2)}) collective-permute-start(bf16[352,1024]{1,0:T(8,128)(2,1)} %refs_0_.4), channel_id=1, source_target_pairs={{0,16},{4,20},{8,24},{12,28},{16,0},{20,4},{24,8},{28,12},{1,17},{... | collective-permute-start | bytes 2162696 | tf_op jit(solution)/shard_map/ppermute | solution.py:669
  134.4 20.1 %collective-permute-start.20 = (bf16[64,1024]{1,0:T(8,128)(2,1)S(1)}, bf16[64,1024]{1,0:T(8,128)(2,1)S(1)}, u32[]{:S(2)}, u32[]{:S(2)}) collective-permute-start(bf16[64,1024]{1,0:T(8,128)(2,1)S(1)} %slice.243), channel_id=1, source_target_pairs={{0,16},{4,20},{8,24},{12,28},{16,0},{20,4},{24,8},{28,12},{1,17},{... | collective-permute-start | bytes 393224 | tf_op jit(solution)/shard_map/ppermute | solution.py:669
  135.8 18.7 %collective-permute-start.21 = (bf16[64,1024]{1,0:T(8,128)(2,1)S(1)}, bf16[64,1024]{1,0:T(8,128)(2,1)S(1)}, u32[]{:S(2)}, u32[]{:S(2)}) collective-permute-start(bf16[64,1024]{1,0:T(8,128)(2,1)S(1)} %slice.244), channel_id=1, source_target_pairs={{0,8},{4,12},{8,0},{12,4},{16,24},{20,28},{24,16},{28,20},{1,9},{5... | collective-permute-start | bytes 393224 | tf_op jit(solution)/shard_map/ppermute | solution.py:669
  136.6 35.6 %collective-permute-start.31 = (bf16[352,1024]{1,0:T(8,128)(2,1)}, bf16[352,1024]{1,0:T(8,128)(2,1)}, u32[]{:S(2)}, u32[]{:S(2)}) collective-permute-start(bf16[352,1024]{1,0:T(8,128)(2,1)} %refs_0_.4), channel_id=1, source_target_pairs={{0,4},{4,0},{8,12},{12,8},{16,20},{20,16},{24,28},{28,24},{1,5},{5... | collective-permute-start | bytes 2162696 | tf_op jit(solution)/shard_map/ppermute | solution.py:669
  154.6 18.2 %collective-permute-start.36 = (bf16[128,2816]{1,0:T(8,128)(2,1)}, bf16[128,2816]{1,0:T(8,128)(2,1)}, u32[]{:S(2)}, u32[]{:S(2)}) collective-permute-start(bf16[128,2816]{1,0:T(8,128)(2,1)} %refs_0_.5), channel_id=1, source_target_pairs={{0,4},{4,0},{8,12},{12,8},{16,20},{20,16},{24,28},{28,24},{1,5},{5... | collective-permute-start | bytes 2162696 | tf_op jit(solution)/shard_map/ppermute | solution.py:669
  155.9 16.9 %collective-permute-start.41 = (bf16[128,2816]{1,0:T(8,128)(2,1)}, bf16[128,2816]{1,0:T(8,128)(2,1)}, u32[]{:S(2)}, u32[]{:S(2)}) collective-permute-start(bf16[128,2816]{1,0:T(8,128)(2,1)} %refs_10_.1), channel_id=1, source_target_pairs={{0,4},{4,0},{8,12},{12,8},{16,20},{20,16},{24,28},{28,24},{1,5},{5... | collective-permute-start | bytes 2162696 | tf_op jit(solution)/shard_map/ppermute | solution.py:669
  155.9 16.3 %all-to-all-start.1 = ((bf16[8,3,128,128]{3,2,1,0:T(8,128)(2,1)}), bf16[8,3,128,128]{3,2,1,0:T(8,128)(2,1)S(1)}, u32[]{:S(2)}, u32[]{:S(2)}) async-start(bf16[8,3,128,128]{3,2,1,0:T(8,128)(2,1)} %chain.2), calls=%async_computation.1 | async-start | bytes 1572864 | tf_op jit(solution)/shard_map/all_to_all | solution.py:296
  159.6 13.7 %collective-permute-start.25 = (bf16[128,1024]{1,0:T(8,128)(2,1)S(1)}, bf16[128,1024]{1,0:T(8,128)(2,1)}, u32[]{:S(2)}, u32[]{:S(2)}) collective-permute-start(bf16[128,1024]{1,0:T(8,128)(2,1)S(1)} %collective-permute-done.18.refs_1_), channel_id=1, source_target_pairs={{0,4},{4,0},{8,12},{12,8},{16,20},{20,16},{24,28},{28,24},{1,5},{5... | collective-permute-start | bytes 786440 | tf_op jit(solution)/shard_map/ppermute | solution.py:669
  160.1 13.2 %collective-permute-start.26 = (bf16[128,1024]{1,0:T(8,128)(2,1)}, bf16[128,1024]{1,0:T(8,128)(2,1)}, u32[]{:S(2)}, u32[]{:S(2)}) collective-permute-start(bf16[128,1024]{1,0:T(8,128)(2,1)} %copy-done.33), channel_id=1, source_target_pairs={{0,4},{4,0},{8,12},{12,8},{16,20},{20,16},{24,28},{28,24},{1,5},{5... | collective-permute-start | bytes 786440 | tf_op jit(solution)/shard_map/ppermute | solution.py:669
  172.7 16.3 %collective-permute-start.37 = (bf16[128,2816]{1,0:T(8,128)(2,1)S(1)}, bf16[128,2816]{1,0:T(8,128)(2,1)S(1)}, u32[]{:S(2)}, u32[]{:S(2)}) collective-permute-start(bf16[128,2816]{1,0:T(8,128)(2,1)S(1)} %collective-permute-done.10.refs_1_), channel_id=1, source_target_pairs={{0,4},{4,0},{8,12},{12,8},{16,20},{20,16},{24,28},{28,24},{1,5},{5... | collective-permute-start | bytes 2162696 | tf_op jit(solution)/shard_map/ppermute | solution.py:669
  172.8 16.9 %collective-permute-start.38 = (bf16[128,2816]{1,0:T(8,128)(2,1)}, bf16[128,2816]{1,0:T(8,128)(2,1)S(1)}, u32[]{:S(2)}, u32[]{:S(2)}) collective-permute-start(bf16[128,2816]{1,0:T(8,128)(2,1)} %collective-permute-done.11.refs_2_), channel_id=1, source_target_pairs={{0,4},{4,0},{8,12},{12,8},{16,20},{20,16},{24,28},{28,24},{1,5},{5... | collective-permute-start | bytes 2162696 | tf_op jit(solution)/shard_map/ppermute | solution.py:669
  176.6 13.6 %collective-permute-start.32 = (bf16[352,1024]{1,0:T(8,128)(2,1)S(1)}, bf16[352,1024]{1,0:T(8,128)(2,1)S(1)}, u32[]{:S(2)}, u32[]{:S(2)}) collective-permute-start(bf16[352,1024]{1,0:T(8,128)(2,1)S(1)} %collective-permute-done.22.refs_1_), channel_id=1, source_target_pairs={{0,4},{4,0},{8,12},{12,8},{16,20},{20,16},{24,28},{28,24},{1,5},{5... | collective-permute-start | bytes 2162696 | tf_op jit(solution)/shard_map/ppermute | solution.py:669
  259.3 32.8 %collective-permute-start.46 = (bf16[4,128,5632]{2,1,0:T(8,128)(2,1)}, bf16[4,128,5632]{2,1,0:T(8,128)(2,1)}, u32[]{:S(2)}, u32[]{:S(2)}) collective-permute-start(bf16[4,128,5632]{2,1,0:T(8,128)(2,1)} %get-tuple-element.250), channel_id=1, source_target_pairs={{0,4},{4,0},{8,12},{12,8},{16,20},{20,16},{24,28},{28,24},{1,5},{5... | collective-permute-start | bytes 17301512 | tf_op jit(solution)/shard_map/ppermute | solution.py:669
  259.5 16.1 %all-to-all-start.2 = ((bf16[8,3,128,128]{3,2,1,0:T(8,128)(2,1)}), bf16[8,3,128,128]{3,2,1,0:T(8,128)(2,1)S(1)}, u32[]{:S(2)}, u32[]{:S(2)}) async-start(bf16[8,3,128,128]{3,2,1,0:T(8,128)(2,1)} %bitcast.21), calls=%async_computation.2 | async-start | bytes 1572864 | tf_op jit(solution)/shard_map/all_to_all | solution.py:292
  280.0 21.9 %all-to-all-start.3 = ((bf16[8,3,128,128]{3,2,1,0:T(8,128)(2,1)}), bf16[8,3,128,128]{3,2,1,0:T(8,128)(2,1)S(1)}, u32[]{:S(2)}, u32[]{:S(2)}) async-start(bf16[8,3,128,128]{3,2,1,0:T(8,128)(2,1)} %chain.3), calls=%async_computation.3 | async-start | bytes 1572864 | tf_op jit(solution)/shard_map/all_to_all | solution.py:296
  291.8 38.3 %collective-permute-start.50 = (bf16[4,352,1024]{2,1,0:T(8,128)(2,1)}, bf16[4,352,1024]{2,1,0:T(8,128)(2,1)}, u32[]{:S(2)}, u32[]{:S(2)}) collective-permute-start(bf16[4,352,1024]{2,1,0:T(8,128)(2,1)} %get-tuple-element.256), channel_id=1, source_target_pairs={{0,4},{4,0},{8,12},{12,8},{16,20},{20,16},{24,28},{28,24},{1,5},{5... | collective-permute-start | bytes 8650760 | tf_op jit(solution)/shard_map/ppermute | solution.py:669
  304.4 25.6 %collective-permute-start.48 = (bf16[64,5632]{1,0:T(8,128)(2,1)}, bf16[64,5632]{1,0:T(8,128)(2,1)S(1)}, u32[]{:S(2)}, u32[]{:S(2)}) collective-permute-start(bf16[64,5632]{1,0:T(8,128)(2,1)} %get-tuple-element.497), channel_id=1, source_target_pairs={{0,8},{4,12},{8,0},{12,4},{16,24},{20,28},{24,16},{28,20},{1,9},{5... | collective-permute-start | bytes 2162696 | tf_op jit(solution)/shard_map/ppermute | solution.py:669
  306.1 24.0 %collective-permute-start.49 = (bf16[64,5632]{1,0:T(8,128)(2,1)S(1)}, bf16[64,5632]{1,0:T(8,128)(2,1)S(1)}, u32[]{:S(2)}, u32[]{:S(2)}) collective-permute-start(bf16[64,5632]{1,0:T(8,128)(2,1)S(1)} %get-tuple-element.496), channel_id=1, source_target_pairs={{0,16},{4,20},{8,24},{12,28},{16,0},{20,4},{24,8},{28,12},{1,17},{... | collective-permute-start | bytes 2162696 | tf_op jit(solution)/shard_map/ppermute | solution.py:669
  337.1 38.0 %collective-permute-start.53 = (bf16[128,5632]{1,0:T(8,128)(2,1)S(1)}, bf16[128,5632]{1,0:T(8,128)(2,1)}, u32[]{:S(2)}, u32[]{:S(2)}) collective-permute-start(bf16[128,5632]{1,0:T(8,128)(2,1)S(1)} %pad_maximum_fusion.2), channel_id=1, source_target_pairs={{0,16},{4,20},{8,24},{12,28},{16,0},{20,4},{24,8},{28,12},{1,17},{... | collective-permute-start | bytes 4325384 | tf_op jit(solution)/shard_map/ppermute | solution.py:669
  339.3 35.8 %collective-permute-start.52 = (bf16[128,5632]{1,0:T(8,128)(2,1)S(1)}, bf16[128,5632]{1,0:T(8,128)(2,1)}, u32[]{:S(2)}, u32[]{:S(2)}) collective-permute-start(bf16[128,5632]{1,0:T(8,128)(2,1)S(1)} %pad_maximum_fusion.1), channel_id=1, source_target_pairs={{0,8},{4,12},{8,0},{12,4},{16,24},{20,28},{24,16},{28,20},{1,9},{5... | collective-permute-start | bytes 4325384 | tf_op jit(solution)/shard_map/ppermute | solution.py:669
  350.4 24.7 %collective-permute-start.54 = (bf16[4,128,1536]{2,1,0:T(8,128)(2,1)}, bf16[4,128,1536]{2,1,0:T(8,128)(2,1)}, u32[]{:S(2)}, u32[]{:S(2)}) collective-permute-start(bf16[4,128,1536]{2,1,0:T(8,128)(2,1)} %get-tuple-element.279), channel_id=1, source_target_pairs={{0,4},{4,0},{8,12},{12,8},{16,20},{20,16},{24,28},{28,24},{1,5},{5... | collective-permute-start | bytes 4718600 | tf_op jit(solution)/shard_map/ppermute | solution.py:669
  372.3 23.6 %collective-permute-start.51 = (bf16[3,3,8,512]{3,2,1,0:T(8,128)(2,1)S(1)}, bf16[3,3,8,512]{3,2,1,0:T(8,128)(2,1)S(1)}, u32[]{:S(2)}, u32[]{:S(2)}) collective-permute-start(bf16[3,3,8,512]{3,2,1,0:T(8,128)(2,1)S(1)} %convert_element_type.379), channel_id=1, source_target_pairs={{4,0},{8,4},{12,8},{16,12},{20,16},{24,20},{28,24},{5,1},{9,5},{13... | collective-permute-start | bytes 221192 | tf_op jit(solution)/shard_map/ppermute | solution.py:664
  377.4 67.0 %collective-permute-start.66 = (bf16[128,5632]{1,0:T(8,128)(2,1)S(1)}, bf16[128,5632]{1,0:T(8,128)(2,1)}, u32[]{:S(2)}, u32[]{:S(2)}) collective-permute-start(bf16[128,5632]{1,0:T(8,128)(2,1)S(1)} %add_convert_fusion.2), channel_id=1, source_target_pairs={{0,1},{3,2},{4,5},{7,6},{8,9},{11,10},{12,13},{15,14},{16,17},{19,... | collective-permute-start | bytes 4325384 | tf_op jit(solution)/shard_map/ppermute | solution.py:960
  383.2 21.7 %collective-permute-start.58 = (bf16[176,1024]{1,0:T(8,128)(2,1)S(1)}, bf16[176,1024]{1,0:T(8,128)(2,1)S(1)}, u32[]{:S(2)}, u32[]{:S(2)}) collective-permute-start(bf16[176,1024]{1,0:T(8,128)(2,1)S(1)} %get-tuple-element.505), channel_id=1, source_target_pairs={{0,8},{4,12},{8,0},{12,4},{16,24},{20,28},{24,16},{28,20},{1,9},{5... | collective-permute-start | bytes 1081352 | tf_op jit(solution)/shard_map/ppermute | solution.py:669
  385.5 19.4 %collective-permute-start.59 = (bf16[176,1024]{1,0:T(8,128)(2,1)S(1)}, bf16[176,1024]{1,0:T(8,128)(2,1)S(1)}, u32[]{:S(2)}, u32[]{:S(2)}) collective-permute-start(bf16[176,1024]{1,0:T(8,128)(2,1)S(1)} %get-tuple-element.504), channel_id=1, source_target_pairs={{0,16},{4,20},{8,24},{12,28},{16,0},{20,4},{24,8},{28,12},{1,17},{... | collective-permute-start | bytes 1081352 | tf_op jit(solution)/shard_map/ppermute | solution.py:669
  404.9 40.3 %collective-permute-start.60 = (bf16[4,128,1536]{2,1,0:T(8,128)(2,1)}, bf16[4,128,1536]{2,1,0:T(8,128)(2,1)}, u32[]{:S(2)}, u32[]{:S(2)}) collective-permute-start(bf16[4,128,1536]{2,1,0:T(8,128)(2,1)} %outer.1), channel_id=1, source_target_pairs={{0,4},{4,0},{8,12},{12,8},{16,20},{20,16},{24,28},{28,24},{1,5},{5... | collective-permute-start | bytes 4718600 | tf_op jit(solution)/shard_map/ppermute | solution.py:669
  421.8 21.8 %collective-permute-start.62 = (bf16[128,1536]{1,0:T(8,128)(2,1)S(1)}, bf16[128,1536]{1,0:T(8,128)(2,1)S(1)}, u32[]{:S(2)}, u32[]{:S(2)}) collective-permute-start(bf16[128,1536]{1,0:T(8,128)(2,1)S(1)} %pad_maximum_fusion.8), channel_id=1, source_target_pairs={{0,16},{4,20},{8,24},{12,28},{16,0},{20,4},{24,8},{28,12},{1,17},{... | collective-permute-start | bytes 1179656 | tf_op jit(solution)/shard_map/ppermute | solution.py:669
  423.9 20.5 %collective-permute-start.61 = (bf16[128,1536]{1,0:T(8,128)(2,1)S(1)}, bf16[128,1536]{1,0:T(8,128)(2,1)S(1)}, u32[]{:S(2)}, u32[]{:S(2)}) collective-permute-start(bf16[128,1536]{1,0:T(8,128)(2,1)S(1)} %pad_maximum_fusion.7), channel_id=1, source_target_pairs={{0,8},{4,12},{8,0},{12,4},{16,24},{20,28},{24,16},{28,20},{1,9},{5... | collective-permute-start | bytes 1179656 | tf_op jit(solution)/shard_map/ppermute | solution.py:669
  426.0 11.7 %collective-permute-start.63 = (bf16[64,1024]{1,0:T(8,128)(2,1)S(1)}, bf16[64,1024]{1,0:T(8,128)(2,1)S(1)}, u32[]{:S(2)}, u32[]{:S(2)}) collective-permute-start(bf16[64,1024]{1,0:T(8,128)(2,1)S(1)} %get-tuple-element.523), channel_id=1, source_target_pairs={{0,8},{4,12},{8,0},{12,4},{16,24},{20,28},{24,16},{28,20},{1,9},{5... | collective-permute-start | bytes 393224 | tf_op jit(solution)/shard_map/ppermute | solution.py:669
  443.3 19.0 %collective-permute-start.70 = (bf16[352,1024]{1,0:T(8,128)(2,1)}, bf16[352,1024]{1,0:T(8,128)(2,1)}, u32[]{:S(2)}, u32[]{:S(2)}) collective-permute-start(bf16[352,1024]{1,0:T(8,128)(2,1)} %pad_maximum_fusion.4), channel_id=1, source_target_pairs={{0,16},{4,20},{8,24},{12,28},{16,0},{20,4},{24,8},{28,12},{1,17},{... | collective-permute-start | bytes 2162696 | tf_op jit(solution)/shard_map/ppermute | solution.py:669
  443.6 20.3 %collective-permute-start.69 = (bf16[352,1024]{1,0:T(8,128)(2,1)}, bf16[352,1024]{1,0:T(8,128)(2,1)}, u32[]{:S(2)}, u32[]{:S(2)}) collective-permute-start(bf16[352,1024]{1,0:T(8,128)(2,1)} %pad_maximum_fusion.3), channel_id=1, source_target_pairs={{0,8},{4,12},{8,0},{12,4},{16,24},{20,28},{24,16},{28,20},{1,9},{5... | collective-permute-start | bytes 2162696 | tf_op jit(solution)/shard_map/ppermute | solution.py:669
  445.3 20.1 %collective-permute-start.79 = (f32[1,128]{1,0:T(1,128)S(1)}, f32[1,128]{1,0:T(1,128)S(1)}, u32[]{:S(2)}, u32[]{:S(2)}) collective-permute-start(f32[1,128]{1,0:T(1,128)S(1)} %bitcast.186), channel_id=1, source_target_pairs={{0,4},{4,0},{8,12},{12,8},{16,20},{20,16},{24,28},{28,24},{1,5},{5... | collective-permute-start | bytes 1544 | tf_op jit(solution)/shard_map/ppermute | solution.py:669
  446.6 25.2 %collective-permute-start.73 = (bf16[128,1536]{1,0:T(8,128)(2,1)S(1)}, bf16[128,1536]{1,0:T(8,128)(2,1)S(1)}, u32[]{:S(2)}, u32[]{:S(2)}) collective-permute-start(bf16[128,1536]{1,0:T(8,128)(2,1)S(1)} %add_convert_fusion.11), channel_id=1, source_target_pairs={{0,1},{3,2},{4,5},{7,6},{8,9},{11,10},{12,13},{15,14},{16,17},{19,... | collective-permute-start | bytes 1179656 | tf_op jit(solution)/shard_map/ppermute | solution.py:960
  448.1 23.7 %collective-permute-start.72 = (bf16[128,1024]{1,0:T(8,128)(2,1)S(1)}, bf16[128,1024]{1,0:T(8,128)(2,1)}, u32[]{:S(2)}, u32[]{:S(2)}) collective-permute-start(bf16[128,1024]{1,0:T(8,128)(2,1)S(1)} %pad_maximum_fusion.10), channel_id=1, source_target_pairs={{0,16},{4,20},{8,24},{12,28},{16,0},{20,4},{24,8},{28,12},{1,17},{... | collective-permute-start | bytes 786440 | tf_op jit(solution)/shard_map/ppermute | solution.py:669
  471.1 21.0 %collective-permute-start.80 = (bf16[128,5632]{1,0:T(8,128)(2,1)S(1)}, bf16[128,5632]{1,0:T(8,128)(2,1)S(1)}, u32[]{:S(2)}, u32[]{:S(2)}) collective-permute-start(bf16[128,5632]{1,0:T(8,128)(2,1)S(1)} %add_convert_fusion.1), channel_id=1, source_target_pairs={{1,2},{2,1},{5,6},{6,5},{9,10},{10,9},{13,14},{14,13},{17,18},{18,... | collective-permute-start | bytes 4325384 | tf_op jit(solution)/shard_map/ppermute | solution.py:968
  477.6 14.5 %collective-permute-start.77 = (bf16[352,1024]{1,0:T(8,128)(2,1)S(1)}, bf16[352,1024]{1,0:T(8,128)(2,1)S(1)}, u32[]{:S(2)}, u32[]{:S(2)}) collective-permute-start(bf16[352,1024]{1,0:T(8,128)(2,1)S(1)} %add_convert_fusion.5), channel_id=1, source_target_pairs={{0,1},{3,2},{4,5},{7,6},{8,9},{11,10},{12,13},{15,14},{16,17},{19,... | collective-permute-start | bytes 2162696 | tf_op jit(solution)/shard_map/ppermute | solution.py:960
  492.1 29.0 %collective-permute-start.85 = (f32[1,128]{1,0:T(1,128)S(1)}, f32[1,128]{1,0:T(1,128)S(1)}, u32[]{:S(2)}, u32[]{:S(2)}) collective-permute-start(f32[1,128]{1,0:T(1,128)S(1)} %bitcast_add_fusion), channel_id=1, source_target_pairs={{0,8},{4,12},{8,0},{12,4},{16,24},{20,28},{24,16},{28,20},{1,9},{5... | collective-permute-start | bytes 1544 | tf_op jit(solution)/shard_map/ppermute | solution.py:669
  494.4 28.1 %collective-permute-start.84 = (bf16[128,1024]{1,0:T(8,128)(2,1)S(1)}, bf16[128,1024]{1,0:T(8,128)(2,1)S(1)}, u32[]{:S(2)}, u32[]{:S(2)}) collective-permute-start(bf16[128,1024]{1,0:T(8,128)(2,1)S(1)} %add_convert_fusion.13), channel_id=1, source_target_pairs={{1,2},{2,1},{5,6},{6,5},{9,10},{10,9},{13,14},{14,13},{17,18},{18,... | collective-permute-start | bytes 786440 | tf_op jit(solution)/shard_map/ppermute | solution.py:968
  495.3 33.8 %collective-permute-start.83 = (bf16[352,1024]{1,0:T(8,128)(2,1)S(1)}, bf16[352,1024]{1,0:T(8,128)(2,1)S(1)}, u32[]{:S(2)}, u32[]{:S(2)}) collective-permute-start(bf16[352,1024]{1,0:T(8,128)(2,1)S(1)} %add_convert_fusion.4), channel_id=1, source_target_pairs={{1,2},{2,1},{5,6},{6,5},{9,10},{10,9},{13,14},{14,13},{17,18},{18,... | collective-permute-start | bytes 2162696 | tf_op jit(solution)/shard_map/ppermute | solution.py:968
  496.1 32.3 %collective-permute-start.82 = (bf16[128,1536]{1,0:T(8,128)(2,1)S(1)}, bf16[128,1536]{1,0:T(8,128)(2,1)S(1)}, u32[]{:S(2)}, u32[]{:S(2)}) collective-permute-start(bf16[128,1536]{1,0:T(8,128)(2,1)S(1)} %add_convert_fusion.9), channel_id=1, source_target_pairs={{1,0},{2,3},{5,4},{6,7},{9,8},{10,11},{13,12},{14,15},{17,16},{18,... | collective-permute-start | bytes 1179656 | tf_op jit(solution)/shard_map/ppermute | solution.py:976
  497.8 30.6 %collective-permute-start.81 = (bf16[128,1664]{1,0:T(8,128)(2,1)S(1)}, bf16[128,1664]{1,0:T(8,128)(2,1)S(1)}, u32[]{:S(2)}, u32[]{:S(2)}) collective-permute-start(bf16[128,1664]{1,0:T(8,128)(2,1)S(1)} %add_convert_fusion.8), channel_id=1, source_target_pairs={{0,1},{3,2},{4,5},{7,6},{8,9},{11,10},{12,13},{15,14},{16,17},{19,... | collective-permute-start | bytes 1277960 | tf_op jit(solution)/shard_map/ppermute | solution.py:960
  521.1 68.8 %collective-permute-start.91 = (bf16[128,5632]{1,0:T(8,128)(2,1)S(1)}, bf16[128,5632]{1,0:T(8,128)(2,1)}, u32[]{:S(2)}, u32[]{:S(2)}) collective-permute-start(bf16[128,5632]{1,0:T(8,128)(2,1)S(1)} %add_convert_fusion), channel_id=1, source_target_pairs={{1,0},{2,3},{5,4},{6,7},{9,8},{10,11},{13,12},{14,15},{17,16},{18,... | collective-permute-start | bytes 4325384 | tf_op jit(solution)/shard_map/ppermute | solution.py:976
  529.4 45.9 %collective-permute-start.87 = (bf16[352,1024]{1,0:T(8,128)(2,1)S(1)}, bf16[352,1024]{1,0:T(8,128)(2,1)S(1)}, u32[]{:S(2)}, u32[]{:S(2)}) collective-permute-start(bf16[352,1024]{1,0:T(8,128)(2,1)S(1)} %add_convert_fusion.3), channel_id=1, source_target_pairs={{1,0},{2,3},{5,4},{6,7},{9,8},{10,11},{13,12},{14,15},{17,16},{18,... | collective-permute-start | bytes 2162696 | tf_op jit(solution)/shard_map/ppermute | solution.py:976
  530.8 44.5 %collective-permute-start.86 = (bf16[128,1664]{1,0:T(8,128)(2,1)S(1)}, bf16[128,1664]{1,0:T(8,128)(2,1)S(1)}, u32[]{:S(2)}, u32[]{:S(2)}) collective-permute-start(bf16[128,1664]{1,0:T(8,128)(2,1)S(1)} %add_convert_fusion.7), channel_id=1, source_target_pairs={{1,2},{2,1},{5,6},{6,5},{9,10},{10,9},{13,14},{14,13},{17,18},{18,... | collective-permute-start | bytes 1277960 | tf_op jit(solution)/shard_map/ppermute | solution.py:968
  531.6 43.7 %collective-permute-start.88 = (bf16[128,1024]{1,0:T(8,128)(2,1)S(1)}, bf16[128,1024]{1,0:T(8,128)(2,1)S(1)}, u32[]{:S(2)}, u32[]{:S(2)}) collective-permute-start(bf16[128,1024]{1,0:T(8,128)(2,1)S(1)} %add_convert_fusion.12), channel_id=1, source_target_pairs={{1,0},{2,3},{5,4},{6,7},{9,8},{10,11},{13,12},{14,15},{17,16},{18,... | collective-permute-start | bytes 786440 | tf_op jit(solution)/shard_map/ppermute | solution.py:976
  582.0 14.3 %collective-permute-start.90 = (bf16[128,1664]{1,0:T(8,128)(2,1)S(1)}, bf16[128,1664]{1,0:T(8,128)(2,1)S(1)}, u32[]{:S(2)}, u32[]{:S(2)}) collective-permute-start(bf16[128,1664]{1,0:T(8,128)(2,1)S(1)} %add_convert_fusion.6), channel_id=1, source_target_pairs={{1,0},{2,3},{5,4},{6,7},{9,8},{10,11},{13,12},{14,15},{17,16},{18,... | collective-permute-start | bytes 1277960 | tf_op jit(solution)/shard_map/ppermute | solution.py:976
  (101 other events, 877.6 us)

commit v3 on v2

--- a/solution.py
+++ b/solution.py
@@ -42,6 +42,18 @@
     left_high, left_low = split(left)
     right_high, right_low = split(right)
     return nn(left_high, right_high) + nn(left_high, right_low) + nn(left_low, right_high)
+
+
+def call_after(ready, kernel, in_specs, **settings):
+    ready = jax.tree.leaves(ready)
+
+    def run(*refs):
+        kernel(*refs[len(ready) :])
+
+    made = pl.pallas_call(
+        run, in_specs=[pl.BlockSpec(memory_space=pl.ANY) for _ in ready] + list(in_specs), **settings
+    )
+    return lambda *arrays: made(*ready, *arrays)
 
 
 def rms_scale(values):
@@ -270,9 +282,10 @@
             )
 
 
-def chain_call(kernel, keep, *arrays):
+def chain_call(kernel, keep, *arrays, ready=()):
     count, pairs = arrays[0].shape[:2]
-    return pl.pallas_call(
+    return call_after(
+        ready,
         kernel,
         in_specs=[pl.BlockSpec(memory_space=pltpu.SMEM)]
         + [pl.BlockSpec(memory_space=pltpu.VMEM) for _ in arrays],
@@ -442,14 +455,15 @@
         ).astype(LOW)
 
 
-def project_back_call(first, second, joint, grad_logits, extra, inputs, gain, hidden_grad):
+def project_back_call(first, second, joint, grad_logits, extra, inputs, gain, hidden_grad, ready=()):
     parts, tokens, half = first.shape
     width = 2 * half
 
     def whole(shape):
         return pl.BlockSpec(shape, lambda j: (0,) * len(shape))
 
-    return pl.pallas_call(
+    return call_after(
+        ready,
         project_back_kernel,
         grid=(parts,),
         in_specs=[
@@ -598,7 +612,9 @@
     rate_ref[0] = rate_sum * beta_all * (1.0 - beta_all)
 
 
-def back_call(group, groups, cols, rows, beta, taps, rim, projected, solve, weights, state, exit_grad, grad):
+def back_call(
+    group, groups, cols, rows, beta, taps, rim, projected, solve, weights, state, exit_grad, grad, ready=()
+):
     row_count, size, triple = projected.shape
     head_count = triple // (3 * 128)
     count = head_count // groups
@@ -623,7 +639,8 @@
     def stacked_type(rows_in, kind):
         return jax.ShapeDtypeStruct((3, row_count, rows_in, wide), kind)
 
-    return pl.pallas_call(
+    return call_after(
+        ready,
         functools.partial(back_kernel, group * count),
         grid=(row_count,),
         in_specs=[of_row((1,) + cols.shape[1:]), of_row((1,) + rows.shape[1:]), of_row((1,) + beta.shape[1:])]
@@ -695,6 +712,125 @@
         cost_estimate=timed(1 + sum(sizes) * columns / 1.2e6),
         name="place",
     )(position, *pieces)
+
+
+def join(*values):
+    return lax.optimization_barrier(values)
+
+
+def gather_near(shard):
+    return (swap(shard, 2), swap(shard, 4)) if seq_is_cube() else None
+
+
+def gather_far(near):
+    if not seq_is_cube():
+        return None
+    by_x, by_y = near
+    half = by_x.shape[0] // 2
+    return swap(by_x[:half], 4), swap(by_y[half:], 2)
+
+
+def gather_core(shard, near, far):
+    if not seq_is_cube():
+        return [lax.all_gather(shard, "seq", axis=0)]
+    mine = jnp.concatenate([shard, *near, *far], axis=0)
+    return [mine, swap(mine, 1)]
+
+
+def gather_core_parts(shard, near, far):
+    if not seq_is_cube():
+        return [lax.all_gather(shard, "seq", axis=0)]
+    mine = [shard, *near, *far]
+    return mine + [swap(piece, 1) for piece in mine]
+
+
+def placing(pieces, sizes):
+    count = lax.axis_size("seq")
+    if not seq_is_cube():
+        parts, moves, offset = [], [], 0
+        for member, size in enumerate(sizes):
+            parts.append(pieces[0][:, offset : offset + size].reshape(count * size, -1))
+            moves.append(((member, 0, 0, 0, 0, count * size),))
+            offset += size
+        return parts, tuple(moves), tuple(count * size for size in sizes), jnp.zeros((1,), jnp.int32)
+    rows = sum(sizes)
+    half = rows // 2
+    spans = [(0, 0, rows), (2, 0, rows), (4, 0, rows), (6, 0, half), (6, half, half)]
+    spans += [(relative ^ 1, first, span) for relative, first, span in spans]
+    moves, index, source = [], 0, 0
+    parts = []
+    for relative, first, span in spans:
+        offset = 0
+        for member, size in enumerate(sizes):
+            low, high = max(first, offset), min(first + span, offset + size)
+            if low < high:
+                parts.append((member, relative, size, low - offset, source + low - first, high - low))
+            offset += size
+        source += span
+        if source == pieces[index].shape[0]:
+            moves.append(tuple(parts))
+            parts, index, source = [], index + 1, 0
+    position = lax.axis_index("seq").astype(jnp.int32).reshape(1)
+    return pieces, tuple(moves), tuple(count * size for size in sizes), position
+
+
+def project_kernel(
+    moves, piece_count, position_ref, inputs_ref, valid_ref, bias_ref, *refs
+):
+    pieces, extra_pieces = refs[:piece_count], refs[piece_count : 2 * piece_count]
+    joint_ref, extra_ref, normed_ref, out_ref, beta_ref, extras_ref = refs[2 * piece_count :]
+    put([joint_ref], pieces, moves, position_ref[0])
+
+    @pl.when(pl.program_id(0) == 0)
+    def _():
+        put([extra_ref], extra_pieces, moves, position_ref[0])
+        extra = extra_ref[...]
+        row = lax.broadcasted_iota(jnp.int32, (16, 128), 0)
+        lane = lax.broadcasted_iota(jnp.int32, (16, 128), 1)
+        extras = nt(jnp.where(lane == row + 8, 1.0, 0.0), extra)
+        extras_ref[...] = extras
+        inputs = inputs_ref[...].astype(WIDE)
+        normed = (inputs * rms_scale(inputs) * extras[0:1]).astype(LOW)
+        normed_ref[...] = normed
+        beta_ref[...] = valid_ref[:, 0:1] * jax.nn.sigmoid(nn(normed, extra) + bias_ref[...])
+
+    out_ref[...] = nn(normed_ref[...], joint_ref[...]).astype(LOW)
+
+
+def project_call(gathered, inputs, valid, bias):
+    pieces, moves, sizes, position = gathered
+    tokens, width = inputs.shape
+    columns = pieces[0].shape[1] - 128
+    tile = 1024
+
+    def whole(shape):
+        return pl.BlockSpec(shape, lambda j: (0,) * len(shape))
+
+    last = columns // 128
+    return pl.pallas_call(
+        functools.partial(project_kernel, moves, len(pieces)),
+        grid=(columns // tile,),
+        in_specs=[
+            pl.BlockSpec(memory_space=pltpu.SMEM), whole((tokens, width)), whole(valid.shape), whole(bias.shape),
+        ]
+        + [pl.BlockSpec((piece.shape[0], tile), lambda j: (0, j)) for piece in pieces]
+        + [pl.BlockSpec((piece.shape[0], 128), lambda j: (0, last)) for piece in pieces],
+        out_specs=[
+            pl.BlockSpec((width, tile), lambda j: (0, j)), whole((width, 128)), whole((tokens, width)),
+            pl.BlockSpec((tokens, tile), lambda j: (0, j)), whole((tokens, 128)), whole((16, width)),
+        ],
+        out_shape=[
+            jax.ShapeDtypeStruct((width, columns), LOW),
+            jax.ShapeDtypeStruct((width, 128), LOW),
+            jax.ShapeDtypeStruct((tokens, width), LOW),
+            jax.ShapeDtypeStruct((tokens, columns), LOW),
+            jax.ShapeDtypeStruct((tokens, 128), WIDE),
+            jax.ShapeDtypeStruct((16, width), WIDE),
+        ],
+        compiler_params=pltpu.CompilerParams(vmem_limit_bytes=VMEM_BYTES),
+        cost_estimate=timed(10),
+        name="project",
+    )(position, inputs, valid, bias, *pieces, *pieces)
 
 
 def join(*values):
@@ -860,14 +996,15 @@
     return lax.axis_size("seq") == 8
 
 
-def outer_turn(left, right, position):
+def outer_turn(left, right, position, ready=()):
     tokens, features = left.shape
     if not seq_is_cube():
         return None, left, left
     specs = outer_specs(features // 2, right)
     order = position ^ jnp.array([1, 3, 5, 7, 0, 2, 4, 6], jnp.int32)
     left_type = jax.ShapeDtypeStruct((features // 2, tokens), LOW)
-    return pl.pallas_call(
+    return call_after(
+        ready,
         outer_turn_kernel,
         grid=specs["grid"],
         in_specs=[
@@ -884,11 +1021,12 @@
     )(order, left, right)
 
 
-def outer(left, right):
+def outer(left, right, ready=()):
     if not seq_is_cube():
         return None
     specs = outer_specs(left.shape[0], right)
-    return pl.pallas_call(
+    return call_after(
+        ready,
         outer_kernel,
         grid=specs["grid"],
         in_specs=[specs["left"], specs["right"]],
@@ -900,13 +1038,14 @@
     )(left, right)
 
 
-def outer_add(left, right, received):
+def outer_add(left, right, received, ready=()):
     if not seq_is_cube():
         full = [jnp.einsum("td,te->de", left, right[i], preferred_element_type=WIDE) for i in range(right.shape[0])]
         full = jnp.concatenate(full, axis=-1).astype(LOW)
         return lax.psum_scatter(full, "seq", scatter_dimension=0, tiled=True)
     specs = outer_specs(left.shape[0], right)
-    return pl.pallas_call(
+    return call_after(
+        ready,
         outer_add_kernel,
         grid=specs["grid"],
         in_specs=[specs["left"], specs["right"], specs["out"]],
@@ -918,6 +1057,90 @@
     )(left, right, received)
 
 
+def outer_two_turn_kernel(
+    order_ref, left_a, left_b, right_a, right_b, out_ref, own_a, own_b, turned_a, turned_b, other_a, other_b
+):
+    first_rows = other_a.shape[0] // 4
+
+    @pl.when(pl.program_id(0) == 0)
+    def _():
+        for left, turned, other, own in ((left_a, turned_a, other_a, own_a), (left_b, turned_b, other_b, own_b)):
+            rows = other.shape[0] // 4
+            turned[...] = left[...].T
+            for index in range(4):
+                first = pl.multiple_of(order_ref[index] * rows, 16)
+                other[index * rows : (index + 1) * rows, :] = turned[pl.ds(first, rows), :]
+                second = pl.multiple_of(order_ref[4 + index] * rows, 16)
+                own[index * rows : (index + 1) * rows, :] = turned[pl.ds(second, rows), :]
+
+    tile = out_ref.shape[2]
+    out_ref[:, :first_rows] = nn(other_a[...], right_a[...]).astype(LOW).reshape(4, -1, tile)
+    out_ref[:, first_rows:] = nn(other_b[...], right_b[...]).astype(LOW).reshape(4, -1, tile)
+
+
+def outer_two_add_kernel(left_a, left_b, right_a, right_b, add_ref, out_ref):
+    first_rows = left_a.shape[0] // 4
+    tile = out_ref.shape[2]
+    for left, right, rows in (
+        (left_a, right_a, slice(0, first_rows)), (left_b, right_b, slice(first_rows, out_ref.shape[1]))
+    ):
+        total = nn(left[...], right[...]).reshape(4, -1, tile)
+        out_ref[:, rows] = (total + add_ref[:, rows].astype(WIDE)).astype(LOW)
+
+
+def outer_two_turn(lefts, rights, position, ready=()):
+    if not seq_is_cube():
+        return None, lefts
+    tokens, columns = rights[0].shape
+    halves = [left.shape[1] // 2 for left in lefts]
+    rows = sum(halves) // 4
+    tile = 512
+    order = position ^ jnp.array([1, 3, 5, 7, 0, 2, 4, 6], jnp.int32)
+    whole = [pl.BlockSpec(left.shape, lambda j: (0, 0)) for left in lefts]
+    half_specs = [pl.BlockSpec((half, tokens), lambda j: (0, 0)) for half in halves]
+    right_spec = pl.BlockSpec((tokens, tile), lambda j: (0, j))
+    other, *own = call_after(
+        ready,
+        outer_two_turn_kernel,
+        grid=(columns // tile,),
+        in_specs=[pl.BlockSpec(memory_space=pltpu.SMEM), *whole, right_spec, right_spec],
+        out_specs=[pl.BlockSpec((4, rows, tile), lambda j: (0, 0, j)), *half_specs],
+        out_shape=[
+            jax.ShapeDtypeStruct((4, rows, columns), LOW),
+            *[jax.ShapeDtypeStruct((half, tokens), LOW) for half in halves],
+        ],
+        scratch_shapes=[pltpu.VMEM((2 * half, tokens), LOW) for half in halves]
+        + [pltpu.VMEM((half, tokens), LOW) for half in halves],
+        compiler_params=pltpu.CompilerParams(vmem_limit_bytes=VMEM_BYTES),
+        cost_estimate=timed(12),
+        name="outer_two_turn",
+    )(order, *lefts, *rights)
+    return other, own
+
+
+def outer_two_add(lefts, rights, received, ready=()):
+    if not seq_is_cube():
+        return jnp.concatenate(
+            [outer_add(left, right[None], None) for left, right in zip(lefts, rights)], axis=0
+        )
+    tokens, columns = rights[0].shape
+    rows = sum(left.shape[0] for left in lefts) // 4
+    tile = 512
+    right_spec = pl.BlockSpec((tokens, tile), lambda j: (0, j))
+    out_spec = pl.BlockSpec((4, rows, tile), lambda j: (0, 0, j))
+    return call_after(
+        ready,
+        outer_two_add_kernel,
+        grid=(columns // tile,),
+        in_specs=[pl.BlockSpec(left.shape, lambda j: (0, 0)) for left in lefts] + [right_spec, right_spec, out_spec],
+        out_specs=out_spec,
+        out_shape=jax.ShapeDtypeStruct((4, rows, columns), LOW),
+        compiler_params=pltpu.CompilerParams(vmem_limit_bytes=VMEM_BYTES),
+        cost_estimate=timed(9),
+        name="outer_two_add",
+    )(*lefts, *rights, received)
+
+
 def send_other(other):
     return swap(other, 1) if seq_is_cube() else None
 
@@ -929,7 +1152,7 @@
     return own, swap(own[3, :half], 2), swap(own[3, half:], 4)
 
 
-def scatter_near(stage):
+def scatter_mid(stage):
     if not seq_is_cube():
         return stage
     own, to_second, to_first = stage
@@ -940,7 +1163,14 @@
     second = jnp.concatenate(
         [(own[2, :half].astype(WIDE) + to_second.astype(WIDE)).astype(LOW), own[2, half:]], axis=0
     )
-    return own[0], swap(first, 2), swap(second, 4)
+    return own[0], first, second
+
+
+def scatter_near(stage):
+    if not seq_is_cube():
+        return stage
+    own, first, second = stage
+    return own, swap(first, 2), swap(second, 4)
 
 
 def scatter_end(stage):
@@ -982,12 +1212,6 @@
     value, received = stage
     index = lax.axis_index("row")
     return jnp.where((index == 0) | (index == 3), received, value).astype(WIDE)
-
-
-def bias_rows(value):
-    if not seq_is_cube():
-        return lax.psum(value, ("seq", "row"))
-    return row_end(row_outward(row_across(row_inward(value))))
 
 
 def on_device(
@@ -1052,8 +1276,9 @@
 
     joint_near, cols, rows, valid, keep_own = join(joint_near, cols, rows, valid, keep_own)
     joint_far = gather_far(joint_near)
-    joint_pieces = placing(gather_core(w_joint, joint_near, joint_far), (shard,))
-    gate_near = gather_near(after(w_gate, joint_far))
+    joint_far, gate_shard = join(joint_far, w_gate)
+    joint_pieces = placing(gather_core_parts(w_joint, joint_near, joint_far), (shard,))
+    gate_near = gather_near(gate_shard)
 
     tokens_in = inputs.reshape(token_count, width)
     bias_row = jnp.pad(beta_bias.astype(WIDE), (0, 128 - head_count))[None]
@@ -1067,26 +1292,26 @@
     beta = beta.reshape(row_count, slot_count, 128)
     rim = shifted(projected[:, slot_count - RIM :], "seq", 1)
 
-    rim, projected, gate_near = join(rim, projected, gate_near)
+    rim, projected, gate_near, up_shard = join(rim, projected, gate_near, w_up)
     gate_far = gather_far(gate_near)
-    up_near = gather_near(after(w_up, gate_near))
+    up_near = gather_near(up_shard)
+    w_rest = jnp.concatenate([w_out, w_down], axis=0)
     eff, local_out, maps, solve, weights = prepare_call(cols, rows, beta, taps, rim, projected)
-    maps, gate_far, up_near = join(maps, gate_far, up_near)
+    maps, gate_far, up_near, w_rest = join(maps, gate_far, up_near, w_rest)
+    up_far = gather_far(up_near)
     maps_here = exchange(maps.reshape((pairs,) + maps.shape[2:]), seq_count)
-    gate_pieces = placing(gather_core(w_gate, gate_near, gate_far), (shard,))
-    up_far = gather_far(up_near)
-    out_near = gather_near(after(w_out, up_near))
-    maps_here, up_far, out_near = join(maps_here, up_far, out_near)
+    gate_pieces = placing(gather_core(gate_shard, gate_near, gate_far), (shard,))
+    maps_here, up_far, gate_whole, rest_shard = join(maps_here, up_far, gate_pieces[0], w_rest)
+    gate_pieces = (gate_whole,) + gate_pieces[1:]
     states_here = chain_call(chain_forward_kernel, keep_own, maps_here)
-    down_near = gather_near(after(w_down, states_here))
+    rest_near = gather_near(rest_shard)
     state = to_home(states_here, pairs).reshape((row_count, head_count, 128, 128))
-    out_far = gather_far(after(out_near, states_here))
-    up_pieces = placing(gather_core(w_up, up_near, after(up_far, states_here)), (shard,))
-    state, out_far, down_near = join(state, out_far, down_near)
-    down_far = gather_far(down_near)
-    (full_out,) = place(placing(gather_core(w_out, out_near, out_far), (shard,)))
-    down_pieces = gather_core(w_down, down_near, after(down_far, full_out))
-    (full_down,) = place(placing(down_pieces, (w_down.shape[0],)))
+    up_pieces = placing(gather_core(up_shard, up_near, up_far), (shard,))
+    state, rest_near = join(state, rest_near)
+    rest_far = gather_far(rest_near)
+    full_out, full_down = place(
+        placing(gather_core_parts(w_rest, rest_near, rest_far), (shard, w_down.shape[0]))
+    )
 
     (
         heads_low, second, act, grad_pair, output, upstream_low,
@@ -1099,19 +1324,19 @@
 
     grads_here = exchange(local_grad.reshape((pairs, 128, 128)), seq_count)
     other_pair, _, left_pair = outer_turn(second, grad_pair, position)
-    grads_here, left_pair = join(grads_here, left_pair)
     from_pair = send_other(other_pair)
-    exits_here = chain_call(chain_backward_kernel, keep_own, maps_here, grads_here)
+    exits_here = chain_call(chain_backward_kernel, keep_own, maps_here, grads_here, ready=left_pair)
     exit_grad = to_home(exits_here, pairs).reshape((row_count, head_count, 128, 128))
-    other_down, _, left_down = outer_turn(after(act, exits_here), upstream_low[None], position)
-    from_down = send_other(other_down)
-    own_pair = outer_add(after(left_pair, left_down), grad_pair, from_pair)
+    rights = (grad_mix_low, upstream_low)
+    other_rest, left_rest = outer_two_turn((heads_low, act), rights, position, ready=exits_here)
+    from_rest = send_other(other_rest)
+    own_pair = outer_add(left_pair, grad_pair, from_pair, ready=left_rest)
     exit_grad, own_pair = join(exit_grad, own_pair)
     far_pair = scatter_far(own_pair)
 
-    def pull(group, exit_grad):
+    def pull(group, ready):
         grad_parts, edges, tails, tap_sums, logits = back_call(
-            group, 2, cols, rows, beta, taps, rim, projected, solve, weights, state, exit_grad, grad_heads
+            group, 2, cols, rows, beta, taps, rim, projected, solve, weights, state, exit_grad, grad_heads, ready
         )
         return grad_parts, shifted(edges.astype(LOW), "seq", -1), tails, jnp.sum(tap_sums, axis=1), logits
 
@@ -1121,36 +1346,43 @@
         )
         return fixed.reshape(3, token_count, -1)
 
-    first_parts, first_rim, first_tails, first_taps, first_logits = pull(0, exit_grad)
-    far_pair, first_logits, from_down = join(far_pair, first_logits, from_down)
-    own_down = outer_add(after(left_down, first_logits), upstream_low[None], from_down)
-    first_rim, own_down, first_parts = join(first_rim, own_down, first_parts)
-    near_pair = scatter_near(after(far_pair, own_down))
+    first_parts, first_rim, first_tails, first_taps, first_logits = pull(0, own_pair)
+    far_pair, first_logits, from_rest = join(far_pair, first_logits, from_rest)
+    own_rest = outer_two_add(left_rest, rights, from_rest, ready=first_logits)
+    first_rim, own_rest, first_parts, far_pair = join(first_rim, own_rest, first_parts, far_pair)
+    mid_pair = scatter_mid(far_pair)
+    near_pair = scatter_near(mid_pair)
     first_grad = fix(first_parts, first_rim, first_tails)
-    other_first, left_other, left_own = outer_turn(normed, first_grad, position)
+    other_first, left_other, left_own = outer_turn(normed, first_grad, position, ready=mid_pair)
     from_first = send_other(other_first)
-    other_out, _, left_out = outer_turn(after(heads_low, left_own), grad_mix_low[None], position)
-    from_out = send_other(other_out)
-    second_parts, second_rim, second_tails, second_taps, second_logits = pull(1, after(exit_grad, left_out))
-    near_pair, from_first, from_out, second_logits = join(near_pair, from_first, from_out, second_logits)
-    shard_pair = scatter_end(near_pair)
-    pair = row_inward(shard_pair)
-    far_down = scatter_far(after(own_down, second_logits))
-    own_first = outer_add(after(left_own, second_logits, shard_pair), first_grad, from_first)
-    own_out = outer_add(after(left_out, own_first), grad_mix_low[None], from_out)
-    second_rim, own_out, second_parts, own_first = join(second_rim, own_out, second_parts, own_first)
+    second_parts, second_rim, second_tails, second_taps, second_logits = pull(1, (left_own, mid_pair))
+    near_pair, from_first, second_logits, own_rest = join(near_pair, from_first, second_logits, own_rest)
+    pair = scatter_end(near_pair)
+    units = w_gate.shape[1]
+    gate, up = row_inward(pair[:, :units]), row_inward(pair[:, units:])
+    far_rest = scatter_far(own_rest)
+    own_first = outer_add(left_own, first_grad, from_first, ready=(second_logits, gate[0], up[0]))
+    second_rim, second_parts, own_first, far_rest = join(second_rim, second_parts, own_first, far_rest)
     far_first = scatter_far(own_first)
+    bias = jnp.sum(first_logits + second_logits, axis=(0, 1))[None]
+    if seq_is_cube():
+        bias = bias + swap(bias, 1)
+        bias = bias + swap(bias, 2)
+    mid_rest = scatter_mid(far_rest)
     second_grad = fix(second_parts, second_rim, second_tails)
-    other_second = outer(after(left_other, own_out), second_grad)
-    other_second, far_first, far_down, own_out = join(other_second, far_first, far_down, own_out)
+    other_second = outer(left_other, second_grad, ready=mid_rest)
+    far_first, other_second, gate, up, bias, mid_rest = join(
+        far_first, other_second, gate, up, bias, mid_rest
+    )
     from_second = send_other(other_second)
-    near_first = scatter_near(far_first)
-    near_down = scatter_near(far_down)
-    far_out = scatter_far(own_out)
+    gate, up = row_across(gate), row_across(up)
+    near_rest = scatter_near(mid_rest)
+    mid_first = scatter_mid(far_first)
 
     grad_logits = (first_logits + second_logits).reshape(token_count, 128)
     grad_inputs, grad_norm_gain = project_back_call(
-        first_grad, after(second_grad, other_second), joint, grad_logits, joint_extra, tokens_in, first_gain, grad_hidden
+        first_grad, second_grad, joint, grad_logits, joint_extra, tokens_in, first_gain, grad_hidden,
+        ready=(other_second, mid_first, gate[0], up[0]),
     )
     grad_beta_w = jnp.einsum(
         "td,th->dh", normed.astype(WIDE), grad_logits[:, :head_count], precision=lax.Precision.HIGHEST
@@ -1175,45 +1407,45 @@
         own_minor = lax.psum_scatter(
             minor.reshape(width, 128).astype(LOW), "seq", scatter_dimension=0, tiled=True
         )
-    from_second, grad_inputs, near_first, far_out, own_minor, grad_logits, pair = join(
-        from_second, grad_inputs, near_first, far_out, own_minor, grad_logits, pair
-    )
-    pair = row_across(pair)
-    first = row_inward(scatter_end(near_first))
-    near_out = scatter_near(far_out)
+    from_second, grad_inputs, own_minor, near_rest, gate = join(
+        from_second, grad_inputs, own_minor, near_rest, gate
+    )
+    gate = row_outward(gate)
+    rest = row_inward(scatter_end(near_rest))
+    near_first = scatter_near(mid_first)
     own_second = jnp.concatenate(
-        [outer_add(left_own, second_grad, from_second), own_minor], axis=-1
-    )
+        [outer_add(left_own, second_grad, from_second, ready=(gate[0], rest[0])), own_minor], axis=-1
+    )
+    own_second, near_first = join(own_second, near_first)
     far_second = scatter_far(own_second)
-    far_second, near_down, near_out, first = join(far_second, near_down, near_out, first)
-    near_second = scatter_near(far_second)
-    down = row_inward(scatter_end(near_down))
-    out = row_inward(scatter_end(near_out))
-    first = row_across(first)
-    bias = jnp.sum(grad_logits, axis=0, keepdims=True)
-    if seq_is_cube():
-        bias = bias + swap(bias, 1)
-    near_second, first, down, out, bias, pair = join(near_second, first, down, out, bias, pair)
-    pair = row_outward(pair)
-    second_ = row_inward(scatter_end(near_second))
-    first = row_outward(first)
-    down = row_across(down)
-    out = row_across(out)
-    if seq_is_cube():
-        bias = bias + swap(bias, 2)
-    second_, first, down, out, bias = join(second_, first, down, out, bias)
-    second_ = row_across(second_)
-    down = row_outward(down)
-    out = row_outward(out)
+    shard_first = scatter_end(near_first)
+    far_second, rest, up, gate, shard_first, bias = join(far_second, rest, up, gate, shard_first, bias)
+    near_second = scatter_near(scatter_mid(far_second))
+    rest = row_across(rest)
+    up = row_outward(up)
+    first = row_inward(shard_first)
     if seq_is_cube():
         bias = bias + swap(bias, 4)
-    second_, down, out, bias = join(second_, down, out, bias)
+    total_gate = row_end(gate)
+    near_second, rest, up, bias, first, total_gate = join(near_second, rest, up, bias, first, total_gate)
+    second_ = row_inward(scatter_end(near_second))
+    first = row_across(first)
+    rest = row_outward(rest)
+    bias = row_inward(bias) if seq_is_cube() else bias
+    total_up = row_end(up)
+    second_, rest, first, bias, total_up = join(second_, rest, first, bias, total_up)
+    second_ = row_across(second_)
+    first = row_outward(first)
+    bias = row_across(bias) if seq_is_cube() else bias
+    total_rest = row_end(rest)
+    first, second_, bias, total_rest = join(first, second_, bias, total_rest)
     second_ = row_outward(second_)
-    bias = bias_rows(bias)
-    second_, pair, first, down, out = join(second_, pair, first, down, out)
-    total_first, total_second, total_down, total_out = (row_end(value) for value in (first, second_, down, out))
-    total_pair = row_end(pair)
+    bias = row_end(row_outward(bias)) if seq_is_cube() else lax.psum(bias, ("seq", "row"))
+    total_first = row_end(first)
+    second_, bias, total_first = join(second_, bias, total_first)
+    total_second = row_end(second_)
     bias_total = bias[0, :head_count]
+    total_out, total_down = total_rest[:shard], total_rest[shard:]
     half = width // 2
     total_qkv = jnp.concatenate(
         [
@@ -1228,7 +1460,6 @@
     total_conv = jnp.transpose(
         small[:, columns : columns + 3 * tap_count].reshape(shard, tap_count, 3), (1, 2, 0)
     ).reshape(tap_count, -1)
-    units = w_gate.shape[1]
     return (
         output.reshape(inputs.shape),
         grad_inputs.reshape(inputs.shape),
@@ -1239,8 +1470,8 @@
         total_conv,
         total_out,
         small[:, head_count + 1],
-        total_pair[:, :units],
-        total_pair[:, units:],
+        total_gate,
+        total_up,
         total_down,
     )
 

time: 618 us -> 553 us (0.89)
  waiting for transfers between devices: 200 us -> 150 us
  local copies, waits for them, and re-layouts: 42.6 us -> 34.4 us
  starting transfers between devices: 122 us -> 115 us
    ppermute x74 -> x60, waiting for transfers between devices: 114 us -> 70.3 us  [swap(): lax.ppermute(value, 'seq', [(source, source ^ bit) for source in range(co...]
    ppermute x6, waiting for transfers between devices: 57.3 us -> 28.1 us  [row_outward(): return (value, lax.ppermute(value, 'row', [(1, 0), (2, 3)]))]
    all_to_all x2, waiting for transfers between devices: 11.9 us -> 23.9 us  [to_home(): moved = lax.all_to_all(value, 'seq', split_axis=0, concat_axis=0)]
    ppermute x6, waiting for transfers between devices: 4.61 us -> 14.6 us  [row_inward(): return (value, lax.ppermute(value, 'row', [(0, 1), (3, 2)]))]
    ppermute x74 -> x60, starting transfers between devices: 56.3 us -> 48.3 us  [swap(): lax.ppermute(value, 'seq', [(source, source ^ bit) for source in range(co...]
    unnamed x141 -> x137, local copies, waits for them, and re-layouts: 16.7 us -> 9.25 us
    pallas_call x15 -> x13, Pallas kernels: 122 us -> 117 us  [call_after(): return lambda *arrays: made(*ready, *arrays)]
  transfers between devices with their start and end apart: 99 -> 85, of which waited for: 28 -> 29; matrix products, arithmetic and copies ran while one was open for 7% -> 9% of each run, Pallas kernels for 25% -> 27%
where the time goes in v3:
time: 553 us; the launch traced here: 543 us
  Pallas kernels  206 us (37%)
  waiting for transfers between devices  150 us (27%)
  starting transfers between devices  115 us (21%)
  local copies, waits for them, and re-layouts  34.4 us (6%)
  other arithmetic  33.8 us (6%)
    pallas_call x13, Pallas kernels, call_after(): return lambda *arrays: made(*ready, *arrays)  117 us
    ppermute x60, waiting for transfers between devices, swap(): lax.ppermute(value, 'seq', [(source, source ^ bit) for source in range(co...  70.3 us
    pallas_call x1, Pallas kernels, feed_call(): pl.pallas_call(functools.partial(feed_kernel, gate[1], up[1]), grid=(unit...  48.8 us
    ppermute x60, starting transfers between devices, swap(): lax.ppermute(value, 'seq', [(source, source ^ bit) for source in range(co...  48.3 us
    ppermute x6, starting transfers between devices, row_inward(): return (value, lax.ppermute(value, 'row', [(0, 1), (3, 2)]))  34.7 us
    ppermute x6, waiting for transfers between devices, row_outward(): return (value, lax.ppermute(value, 'row', [(1, 0), (2, 3)]))  28.1 us
    all_to_all x2, waiting for transfers between devices, to_home(): moved = lax.all_to_all(value, 'seq', split_axis=0, concat_axis=0)  23.9 us
    pallas_call x1, Pallas kernels, prepare_call(): pl.pallas_call(prepare_kernel, grid=(row_count, groups), in_specs=[of_row...  21.6 us
  transfers between devices with their start and end apart: 85, of which 29 were waited for; matrix products, arithmetic and copies ran while one was open for 9% of the time, Pallas kernels for 27%

profile of v3, /device:TPU:0, one launch (start us, length us, event | category | flops | bytes accessed | tf_op | source)
XLA Modules:
  0.0 543.2 jit_solution(14680906179277982868)
XLA Ops:
  3.4 3.0 collective-permute-start
  10.0 14.7 %collective-permute-done.refs_1_.refs_11_ = bf16[128,3200]{1,0:T(8,128)(2,1)S(1)} collective-permute-done((bf16[128,3200]{1,0:T(8,128)(2,1)S(1)}, bf16[128,3200]{1,0:T(8,128)(2,1)S(1)}, u32[]{:S(2)}, u32[]{:S(2)}) %collective-permute-start) | collective-permute-done | bytes 819232 | tf_op jit(solution)/shard_map/ppermute | solution.py:686
  27.8 1.6 collective-permute-start.2
  30.5 7.3 %collective-permute-done.2.refs_3_.refs_13_ = bf16[64,3200]{1,0:T(8,128)(2,1)S(1)} collective-permute-done((bf16[64,3200]{1,0:T(8,128)(2,1)S(1)}, bf16[64,3200]{1,0:T(8,128)(2,1)S(1)}, u32[]{:S(2)}, u32[]{:S(2)}) %collective-permute-start.2) | collective-permute-done | bytes 409632 | tf_op jit(solution)/shard_map/ppermute | solution.py:686
  42.8 11.2 %project.1 = (bf16[1024,3072]{1,0:T(8,128)(2,1)}, bf16[1024,128]{1,0:T(8,128)(2,1)}, bf16[768,1024]{1,0:T(8,128)(2,1)}, bf16[768,3072]{1,0:T(8,128)(2,1)}, f32[768,128]{1,0:T(8,128)}, /*index=5*/f32[16,1024]{1,0:T(8,128)}) custom-call(s32[1]{0:T(128)} %bitcast.position_ref, bf16[768,1024]{1,0:T(8,128)(2,1)} %bitcast.177, ...), custom_call_target="tpu_custom_call" | custom-call | flops 10000000000 | bytes 10000000 | tf_op jit(solution)/shard_map/project/pallas_call | solution.py:918
  55.0 2.0 collective-permute-start.9
  59.4 3.4 collective-permute-start.14
  68.1 21.6 %prepare.1 = (bf16[3,8,256,128]{3,2,1,0:T(8,128)(2,1)}, f32[3,256,1024]{2,1,0:T(8,128)}, bf16[3,8,128,256]{3,2,1,0:T(8,128)(2,1)}, bf16[3,8,256,256]{3,2,1,0:T(8,128)(2,1)}, bf16[3,8,256,256]{3,2,1,0:T(8,128)(2,1)}) custom-call(f32[3,256,8]{2,1,0:T(8,128)} %copy.184.cols_ref.refs_1_.refs_4_, f32[3,8,256]{2,1,0:T(8,128)} %broadcast_in_dim.64.rows_ref.refs_2_.refs_5_, ...), custom_call_target="tpu_custom_call" | custom-call | flops 22000001024 | bytes 22000000 | tf_op jit(solution)/shard_map/prepare/pallas_call | solution.py:228
  90.6 4.0 all-to-all-start
  95.7 1.8 collective-permute-start.16
  98.5 1.5 collective-permute-start.17
  100.5 21.8 %collective-permute-done.16.refs_13_ = bf16[64,2816]{1,0:T(8,128)(2,1)S(1)} collective-permute-done((bf16[64,2816]{1,0:T(8,128)(2,1)S(1)}, bf16[64,2816]{1,0:T(8,128)(2,1)S(1)}, u32[]{:S(2)}, u32[]{:S(2)}) %collective-permute-start.16) | collective-permute-done | bytes 360480 | tf_op jit(solution)/shard_map/ppermute | solution.py:686
  124.0 1.5 collective-permute-start.23
  126.1 3.3 chain.2
  129.4 3.7 all-to-all-start.1
  133.5 23.9 %all-to-all-done.1 = bf16[8,3,128,128]{3,2,1,0:T(8,128)(2,1)S(1)} async-done(((bf16[8,3,128,128]{3,2,1,0:T(8,128)(2,1)}), bf16[8,3,128,128]{3,2,1,0:T(8,128)(2,1)S(1)}, u32[]{:S(2)}, u32[]{:S(2)}) %all-to-all-start.1) | async-done | bytes 786464 | tf_op jit(solution)/shard_map/all_to_all | solution.py:309
  160.8 7.8 %collective-permute-done.25.refs_3_ = bf16[240,1024]{1,0:T(8,128)(2,1)S(1)} collective-permute-done((bf16[240,1024]{1,0:T(8,128)(2,1)S(1)}, bf16[240,1024]{1,0:T(8,128)(2,1)S(1)}, u32[]{:S(2)}, u32[]{:S(2)}) %collective-permute-start.25) | collective-permute-done | bytes 491552 | tf_op jit(solution)/shard_map/ppermute | solution.py:686
  168.6 1.8 collective-permute-done.26.refs_4_
  175.8 6.8 %place.1 = (bf16[1024,1024]{1,0:T(8,128)(2,1)}, bf16[2816,1024]{1,0:T(8,128)(2,1)}) custom-call(s32[1]{0:T(128)} %bitcast.position_ref, bf16[480,1024]{1,0:T(8,128)(2,1)} %copy-done.17, bf16[480,1024]{1,0:T(8,128)(2,1)} %copy-done.26, bf16[480,1024]{1,0:T(8,128)(2,1)} %collective-permute-done.24.refs_2_, bf16[240,1024]{1,0:T(8,128)(2,1)} %copy-done.48, ...), custom_call_target="tpu_custom_call" | custom-call | flops 4276800000 | bytes 4276800 | tf_op jit(solution)/shard_map/place/pallas_call | solution.py:704
  184.1 48.8 %feed.1 = (bf16[768,1024]{1,0:T(8,128)(2,1)}, bf16[768,1024]{1,0:T(8,128)(2,1)}, bf16[768,2816]{1,0:T(8,128)(2,1)}, bf16[2,768,2816]{2,1,0:T(8,128)(2,1)}, bf16[...) custom-call(s32[1]{0:T(128)} %bitcast.position_ref, ...), custom_call_target="tpu_custom_call" | custom-call | flops 38000001024 | bytes 38000000 | tf_op jit(solution)/shard_map/feed/pallas_call | solution.py:394
  233.0 9.9 %outer_turn.2 = (bf16[4,128,5632]{2,1,0:T(8,128)(2,1)}, bf16[512,768]{1,0:T(8,128)(2,1)}, bf16[512,768]{1,0:T(8,128)(2,1)}) custom-call(s32[8]{0:T(128)} %broadcast_xor_fusion.refs_0_.refs_1_.refs_3_, bf16[768,1024]{1,0:T(8,128)(2,1)} %get-tuple-element.230.refs_1_, bf16[2,768,2816]{2,1,0:T(8,128)(2,1)} %get-tuple-element.231.refs_2_.refs_3_), custom_call_target="tpu_custom_call" | custom-call | flops 13303291904 | bytes 13303291 | tf_op jit(solution)/shard_map/outer_turn/pallas_call | solution.py:56
  243.2 3.5 all-to-all-start.2
  246.8 12.5 %all-to-all-done.2.refs_3_ = bf16[8,3,128,128]{3,2,1,0:T(8,128)(2,1)S(1)} async-done(((bf16[8,3,128,128]{3,2,1,0:T(8,128)(2,1)}), bf16[8,3,128,128]{3,2,1,0:T(8,128)(2,1)S(1)}, u32[]{:S(2)}, u32[]{:S(2)}) %all-to-all-start.2) | async-done | bytes 786464 | tf_op jit(solution)/shard_map/all_to_all | solution.py:305
  260.1 3.5 chain.3.refs_0_
  263.7 3.5 all-to-all-start.3
  267.2 10.0 %outer_two_turn.1 = (bf16[4,480,1024]{2,1,0:T(8,128)(2,1)}, bf16[512,768]{1,0:T(8,128)(2,1)}, bf16[1408,768]{1,0:T(8,128)(2,1)}) custom-call(bf16[8,3,128,128]{3,2,1,0:T(8,128)(2,1)} %chain.3.refs_0_, s32[8]{0:T(128)} %broadcast_xor_fusion.refs_0_.refs_1_.refs_3_, bf16[768,1024]{1,0:T(8,128)(2,1)} %get-tuple-element.234.refs_2_, ...), custom_call_target="tpu_custom_call" | custom-call | flops 12000000000 | bytes 12000000 | tf_op jit(solution)/shard_map/outer_two_turn/pallas_call | solution.py:56
  277.6 9.8 %outer_add.3.refs_0_ = bf16[4,128,5632]{2,1,0:T(8,128)(2,1)} custom-call(bf16[512,768]{1,0:T(8,128)(2,1)} %get-tuple-element.238.refs_0_.refs_1_, bf16[1408,768]{1,0:T(8,128)(2,1)} %get-tuple-element.239.refs_1_.refs_2_, bf16[512,768]{1,0:T(8,128)(2,1)} %get-tuple-element.232.refs_0_.refs_2_, bf16[2,768,2816]{2,1,0:T(8,128)(2,1)} %get-tuple-element.231.refs_2_.refs_3_, ...), custom_call_target="tpu_custom_call" | custom-call | flops 13303291904 | bytes 13303291 | tf_op jit(solution)/shard_map/outer_add/pallas_call | solution.py:56
  287.4 2.6 slice_bitcast_fusion.4
  290.0 1.7 collective-permute-start.39
  293.1 19.3 %mixer_back.2 = (bf16[3,3,256,512]{3,2,1,0:T(8,128)(2,1)}, f32[3,3,8,512]{3,2,1,0:T(8,128)}, f32[3,3,8,512]{3,2,1,0:T(8,128)}, f32[3,3,4,512]{3,2,1,0:T(4,128)}, f32[3,256,128]{2,1,0:T(8,128)}) custom-call(bf16[4,128,5632]{2,1,0:T(8,128)(2,1)} %outer_add.3.refs_0_, f32[3,256,8]{2,1,0:T(8,128)} %copy.184.cols_ref.refs_1_.refs_4_, ...), custom_call_target="tpu_custom_call" | custom-call | flops 17999998976 | bytes 18000000 | tf_op jit(solution)/shard_map/mixer_back/pallas_call | solution.py:56
  315.6 8.5 %outer_two_add.1 = bf16[4,480,1024]{2,1,0:T(8,128)(2,1)} custom-call(f32[3,256,128]{2,1,0:T(8,128)} %get-tuple-element.249.refs_0_, bf16[512,768]{1,0:T(8,128)(2,1)} %get-tuple-element.238.refs_0_.refs_1_, bf16[1408,768]{1,0:T(8,128)(2,1)} %get-tuple-element.239.refs_1_.refs_2_, bf16[768,1024]{1,0:T(8,128)(2,1)} %get-tuple-element.236.refs_4_.refs_3_, ...), custom_call_target="tpu_custom_call" | custom-call | flops 8999999488 | bytes 9000000 | tf_op jit(solution)/shard_map/outer_two_add/pallas_call | solution.py:56
  326.0 2.1 collective-permute-start.44
  330.4 5.5 %outer_turn.3 = (bf16[4,128,1536]{2,1,0:T(8,128)(2,1)}, bf16[512,768]{1,0:T(8,128)(2,1)}, bf16[512,768]{1,0:T(8,128)(2,1)}) custom-call(bf16[128,5632]{1,0:T(8,128)(2,1)} %slice_bitcast_fusion.refs_0_.refs_1_, bf16[128,5632]{1,0:T(8,128)(2,1)} %pad_maximum_fusion.1.refs_1_.refs_2_, bf16[128,5632]{1,0:T(8,128)(2,1)} %copy-done.16, ...), custom_call_target="tpu_custom_call" | custom-call | flops 4355443200 | bytes 4355443 | tf_op jit(solution)/shard_map/outer_turn/pallas_call | solution.py:56
  336.0 19.4 %mixer_back.3 = (bf16[3,3,256,512]{3,2,1,0:T(8,128)(2,1)}, f32[3,3,8,512]{3,2,1,0:T(8,128)}, f32[3,3,8,512]{3,2,1,0:T(8,128)}, f32[3,3,4,512]{3,2,1,0:T(4,128)}, f32[3,256,128]{2,1,0:T(8,128)}) custom-call(bf16[512,768]{1,0:T(8,128)(2,1)} %get-tuple-element.262.refs_0_.refs_3_.refs_2_, bf16[128,5632]{1,0:T(8,128)(2,1)} %slice_bitcast_fusion.refs_0_.refs_1_, ...), custom_call_target="tpu_custom_call" | custom-call | flops 17999998976 | bytes 18000000 | tf_op jit(solution)/shard_map/mixer_back/pallas_call | solution.py:56
  356.5 1.6 convert_element_type.351
  360.4 2.0 collective-permute-done.43
  363.8 2.5 add_convert_fusion
  368.7 1.7 collective-permute-start.47
  370.4 3.5 collective-permute-start.50
  374.0 5.0 outer_add.4
  379.0 1.5 collective-permute-start.53
  380.5 2.3 convolution_bitcast_fusion
  382.8 3.1 collective-permute-start.51
  387.1 1.7 collective-permute-start.49
  388.8 1.5 fusion.3
  394.9 4.8 outer.1.refs_0_
  399.7 5.3 collective-permute-done.51
  414.4 13.3 %project_back.1 = (bf16[768,1024]{1,0:T(8,128)(2,1)}, f32[1,1024]{1,0:T(1,128)}) custom-call(bf16[4,128,1536]{2,1,0:T(8,128)(2,1)} %outer.1.refs_0_, bf16[128,1536]{1,0:T(8,128)(2,1)} %slice_bitcast_fusion.11.refs_1_, bf16[128,1536]{1,0:T(8,128)(2,1)} %pad_maximum_fusion.8.refs_2_, bf16[128,1536]{1,0:T(8,128)(2,1)} %pad_maximum_fusion.9.refs_3_, ...), custom_call_target="tpu_custom_call" | custom-call | flops 10000000000 | bytes 10000000 | tf_op jit(solution)/shard_map/project_back/pallas_call | solution.py:56
  436.0 2.1 add_convert_fusion.3.refs_1_
  438.1 7.0 %collective-permute-start.63 = (bf16[480,1024]{1,0:T(8,128)(2,1)S(1)}, bf16[480,1024]{1,0:T(8,128)(2,1)S(1)}, u32[]{:S(2)}, u32[]{:S(2)}) collective-permute-start(bf16[480,1024]{1,0:T(8,128)(2,1)S(1)} %add_convert_fusion.3.refs_1_), channel_id=1, source_target_pairs={{0,1},{3,2},{4,5},{7,6},{8,9},{11,10},{12,13},{15,14},{16,17},{19,... | collective-permute-start | bytes 2949128 | tf_op jit(solution)/shard_map/ppermute | solution.py:1190
  447.7 5.0 outer_add.5
  452.7 1.6 pad_maximum_fusion
  454.4 1.5 collective-permute-start.61
  456.6 4.0 collective-permute-done.61
  461.9 3.6 collective-permute-done.65
  468.7 1.8 collective-permute-start.67
  470.5 1.5 collective-permute-start.66
  473.3 7.3 %collective-permute-start.71 = (bf16[128,1536]{1,0:T(8,128)(2,1)S(1)}, bf16[128,1536]{1,0:T(8,128)(2,1)S(1)}, u32[]{:S(2)}, u32[]{:S(2)}) collective-permute-start(bf16[128,1536]{1,0:T(8,128)(2,1)S(1)} %add_convert_fusion.13), channel_id=1, source_target_pairs={{0,1},{3,2},{4,5},{7,6},{8,9},{11,10},{12,13},{15,14},{16,17},{19,... | collective-permute-start | bytes 1179656 | tf_op jit(solution)/shard_map/ppermute | solution.py:1190
  480.7 5.6 %collective-permute-done.71 = bf16[128,1536]{1,0:T(8,128)(2,1)S(1)} collective-permute-done((bf16[128,1536]{1,0:T(8,128)(2,1)S(1)}, bf16[128,1536]{1,0:T(8,128)(2,1)S(1)}, u32[]{:S(2)}, u32[]{:S(2)}) %collective-permute-start.71) | collective-permute-done | bytes 393248 | tf_op jit(solution)/shard_map/ppermute | solution.py:1190
  488.9 12.5 %collective-permute-start.72 = (bf16[128,1664]{1,0:T(8,128)(2,1)S(1)}, bf16[128,1664]{1,0:T(8,128)(2,1)S(1)}, u32[]{:S(2)}, u32[]{:S(2)}) collective-permute-start(bf16[128,1664]{1,0:T(8,128)(2,1)S(1)} %add_convert_fusion.10), channel_id=1, source_target_pairs={{0,1},{3,2},{4,5},{7,6},{8,9},{11,10},{12,13},{15,14},{16,17},{19,... | collective-permute-start | bytes 1277960 | tf_op jit(solution)/shard_map/ppermute | solution.py:1190
  503.9 3.6 collective-permute-done.75
  507.5 10.5 %collective-permute-done.73 = bf16[480,1024]{1,0:T(8,128)(2,1)S(1)} collective-permute-done((bf16[480,1024]{1,0:T(8,128)(2,1)S(1)}, bf16[480,1024]{1,0:T(8,128)(2,1)S(1)}, u32[]{:S(2)}, u32[]{:S(2)}) %collective-permute-start.73) | collective-permute-done | bytes 983072 | tf_op jit(solution)/shard_map/ppermute | solution.py:1206
  521.0 7.5 %collective-permute-done.76 = bf16[128,1536]{1,0:T(8,128)(2,1)S(1)} collective-permute-done((bf16[128,1536]{1,0:T(8,128)(2,1)S(1)}, bf16[128,1536]{1,0:T(8,128)(2,1)S(1)}, u32[]{:S(2)}, u32[]{:S(2)}) %collective-permute-start.76) | collective-permute-done | bytes 393248 | tf_op jit(solution)/shard_map/ppermute | solution.py:1206
  534.0 6.0 %collective-permute-done.79 = bf16[128,1664]{1,0:T(8,128)(2,1)S(1)} collective-permute-done((bf16[128,1664]{1,0:T(8,128)(2,1)S(1)}, bf16[128,1664]{1,0:T(8,128)(2,1)S(1)}, u32[]{:S(2)}, u32[]{:S(2)}) %collective-permute-start.79) | collective-permute-done | bytes 426016 | tf_op jit(solution)/shard_map/ppermute | solution.py:1206
  (390 shorter events, 106.4 us)
Async XLA Ops:
  3.4 21.2 %collective-permute-start = (bf16[128,3200]{1,0:T(8,128)(2,1)S(1)}, bf16[128,3200]{1,0:T(8,128)(2,1)S(1)}, u32[]{:S(2)}, u32[]{:S(2)}) collective-permute-start(bf16[128,3200]{1,0:T(8,128)(2,1)S(1)} %fusion.5.refs_0_.refs_10_), channel_id=1, source_target_pairs={{0,8},{4,12},{8,0},{12,4},{16,24},{20,28},{24,16},{28,20},{1,9},{5... | collective-permute-start | bytes 2457608 | tf_op jit(solution)/shard_map/ppermute | solution.py:686
  6.4 19.7 %collective-permute-start.1 = (bf16[128,3200]{1,0:T(8,128)(2,1)S(1)}, bf16[128,3200]{1,0:T(8,128)(2,1)S(1)}, u32[]{:S(2)}, u32[]{:S(2)}) collective-permute-start(bf16[128,3200]{1,0:T(8,128)(2,1)S(1)} %fusion.5.refs_0_.refs_10_), channel_id=1, source_target_pairs={{0,16},{4,20},{8,24},{12,28},{16,0},{20,4},{24,8},{28,12},{1,17},{... | collective-permute-start | bytes 2457608 | tf_op jit(solution)/shard_map/ppermute | solution.py:686
  27.8 10.1 %collective-permute-start.2 = (bf16[64,3200]{1,0:T(8,128)(2,1)S(1)}, bf16[64,3200]{1,0:T(8,128)(2,1)S(1)}, u32[]{:S(2)}, u32[]{:S(2)}) collective-permute-start(bf16[64,3200]{1,0:T(8,128)(2,1)S(1)} %slice.214), channel_id=1, source_target_pairs={{0,16},{4,20},{8,24},{12,28},{16,0},{20,4},{24,8},{28,12},{1,17},{... | collective-permute-start | bytes 1228808 | tf_op jit(solution)/shard_map/ppermute | solution.py:686
  30.0 10.2 %collective-permute-start.4 = (bf16[128,3200]{1,0:T(8,128)(2,1)S(1)}, bf16[128,3200]{1,0:T(8,128)(2,1)S(1)}, u32[]{:S(2)}, u32[]{:S(2)}) collective-permute-start(bf16[128,3200]{1,0:T(8,128)(2,1)S(1)} %fusion.5.refs_0_.refs_10_), channel_id=1, source_target_pairs={{0,4},{4,0},{8,12},{12,8},{16,20},{20,16},{24,28},{28,24},{1,5},{5... | collective-permute-start | bytes 2457608 | tf_op jit(solution)/shard_map/ppermute | solution.py:686
  30.0 11.5 %collective-permute-start.5 = (bf16[128,3200]{1,0:T(8,128)(2,1)S(1)}, bf16[128,3200]{1,0:T(8,128)(2,1)S(1)}, u32[]{:S(2)}, u32[]{:S(2)}) collective-permute-start(bf16[128,3200]{1,0:T(8,128)(2,1)S(1)} %collective-permute-done.refs_1_.refs_11_), channel_id=1, source_target_pairs={{0,4},{4,0},{8,12},{12,8},{16,20},{20,16},{24,28},{28,24},{1,5},{5... | collective-permute-start | bytes 2457608 | tf_op jit(solution)/shard_map/ppermute | solution.py:686
  30.5 11.0 %collective-permute-start.6 = (bf16[128,3200]{1,0:T(8,128)(2,1)S(1)}, bf16[128,3200]{1,0:T(8,128)(2,1)S(1)}, u32[]{:S(2)}, u32[]{:S(2)}) collective-permute-start(bf16[128,3200]{1,0:T(8,128)(2,1)S(1)} %collective-permute-done.1.refs_2_.refs_12_), channel_id=1, source_target_pairs={{0,4},{4,0},{8,12},{12,8},{16,20},{20,16},{24,28},{28,24},{1,5},{5... | collective-permute-start | bytes 2457608 | tf_op jit(solution)/shard_map/ppermute | solution.py:686
  40.2 18.8 %collective-permute-start.10 = (bf16[128,2816]{1,0:T(8,128)(2,1)}, bf16[128,2816]{1,0:T(8,128)(2,1)}, u32[]{:S(2)}, u32[]{:S(2)}) collective-permute-start(bf16[128,2816]{1,0:T(8,128)(2,1)} %refs_0_), channel_id=1, source_target_pairs={{0,8},{4,12},{8,0},{12,4},{16,24},{20,28},{24,16},{28,20},{1,9},{5... | collective-permute-start | bytes 2162696 | tf_op jit(solution)/shard_map/ppermute | solution.py:686
  40.9 18.5 %collective-permute-start.11 = (bf16[128,2816]{1,0:T(8,128)(2,1)}, bf16[128,2816]{1,0:T(8,128)(2,1)}, u32[]{:S(2)}, u32[]{:S(2)}) collective-permute-start(bf16[128,2816]{1,0:T(8,128)(2,1)} %refs_0_), channel_id=1, source_target_pairs={{0,16},{4,20},{8,24},{12,28},{16,0},{20,4},{24,8},{28,12},{1,17},{... | collective-permute-start | bytes 2162696 | tf_op jit(solution)/shard_map/ppermute | solution.py:686
  59.4 30.3 %collective-permute-start.14 = (bf16[128,2816]{1,0:T(8,128)(2,1)}, bf16[128,2816]{1,0:T(8,128)(2,1)S(1)}, u32[]{:S(2)}, u32[]{:S(2)}) collective-permute-start(bf16[128,2816]{1,0:T(8,128)(2,1)} %refs_10_), channel_id=1, source_target_pairs={{0,8},{4,12},{8,0},{12,4},{16,24},{20,28},{24,16},{28,20},{1,9},{5... | collective-permute-start | bytes 2162696 | tf_op jit(solution)/shard_map/ppermute | solution.py:686
  62.8 27.7 %collective-permute-start.15 = (bf16[128,2816]{1,0:T(8,128)(2,1)}, bf16[128,2816]{1,0:T(8,128)(2,1)}, u32[]{:S(2)}, u32[]{:S(2)}) collective-permute-start(bf16[128,2816]{1,0:T(8,128)(2,1)} %refs_10_), channel_id=1, source_target_pairs={{0,16},{4,20},{8,24},{12,28},{16,0},{20,4},{24,8},{28,12},{1,17},{... | collective-permute-start | bytes 2162696 | tf_op jit(solution)/shard_map/ppermute | solution.py:686
  65.3 24.4 %collective-permute-start.12 = (bf16[64,2816]{1,0:T(8,128)(2,1)S(1)}, bf16[64,2816]{1,0:T(8,128)(2,1)S(1)}, u32[]{:S(2)}, u32[]{:S(2)}) collective-permute-start(bf16[64,2816]{1,0:T(8,128)(2,1)S(1)} %slice.218), channel_id=1, source_target_pairs={{0,16},{4,20},{8,24},{12,28},{16,0},{20,4},{24,8},{28,12},{1,17},{... | collective-permute-start | bytes 1081352 | tf_op jit(solution)/shard_map/ppermute | solution.py:686
  66.9 22.8 %collective-permute-start.13 = (bf16[64,2816]{1,0:T(8,128)(2,1)S(1)}, bf16[64,2816]{1,0:T(8,128)(2,1)S(1)}, u32[]{:S(2)}, u32[]{:S(2)}) collective-permute-start(bf16[64,2816]{1,0:T(8,128)(2,1)S(1)} %slice.219), channel_id=1, source_target_pairs={{0,8},{4,12},{8,0},{12,4},{16,24},{20,28},{24,16},{28,20},{1,9},{5... | collective-permute-start | bytes 1081352 | tf_op jit(solution)/shard_map/ppermute | solution.py:686
  90.6 33.4 %all-to-all-start = ((bf16[8,3,128,256]{3,2,1,0:T(8,128)(2,1)}), bf16[8,3,128,256]{3,2,1,0:T(8,128)(2,1)S(1)}, u32[]{:S(2)}, u32[]{:S(2)}) async-start(bf16[8,3,128,256]{3,2,1,0:T(8,128)(2,1)} %bitcast.136), calls=%async_computation | async-start | bytes 3145728 | tf_op jit(solution)/shard_map/all_to_all | solution.py:305
  95.7 26.7 %collective-permute-start.16 = (bf16[64,2816]{1,0:T(8,128)(2,1)S(1)}, bf16[64,2816]{1,0:T(8,128)(2,1)S(1)}, u32[]{:S(2)}, u32[]{:S(2)}) collective-permute-start(bf16[64,2816]{1,0:T(8,128)(2,1)S(1)} %slice.220), channel_id=1, source_target_pairs={{0,16},{4,20},{8,24},{12,28},{16,0},{20,4},{24,8},{28,12},{1,17},{... | collective-permute-start | bytes 1081352 | tf_op jit(solution)/shard_map/ppermute | solution.py:686
  98.5 24.0 %collective-permute-start.17 = (bf16[64,2816]{1,0:T(8,128)(2,1)S(1)}, bf16[64,2816]{1,0:T(8,128)(2,1)S(1)}, u32[]{:S(2)}, u32[]{:S(2)}) collective-permute-start(bf16[64,2816]{1,0:T(8,128)(2,1)S(1)} %slice.221), channel_id=1, source_target_pairs={{0,8},{4,12},{8,0},{12,4},{16,24},{20,28},{24,16},{28,20},{1,9},{5... | collective-permute-start | bytes 1081352 | tf_op jit(solution)/shard_map/ppermute | solution.py:686
  100.0 22.4 %collective-permute-start.21 = (bf16[64,2816]{1,0:T(8,128)(2,1)}, bf16[64,2816]{1,0:T(8,128)(2,1)S(1)}, u32[]{:S(2)}, u32[]{:S(2)}) collective-permute-start(bf16[64,2816]{1,0:T(8,128)(2,1)} %copy-done.55), channel_id=1, source_target_pairs={{0,4},{4,0},{8,12},{12,8},{16,20},{20,16},{24,28},{28,24},{1,5},{5... | collective-permute-start | bytes 1081352 | tf_op jit(solution)/shard_map/ppermute | solution.py:686
  100.0 23.9 %collective-permute-start.22 = (bf16[64,2816]{1,0:T(8,128)(2,1)}, bf16[64,2816]{1,0:T(8,128)(2,1)}, u32[]{:S(2)}, u32[]{:S(2)}) collective-permute-start(bf16[64,2816]{1,0:T(8,128)(2,1)} %copy-done.56), channel_id=1, source_target_pairs={{0,4},{4,0},{8,12},{12,8},{16,20},{20,16},{24,28},{28,24},{1,5},{5... | collective-permute-start | bytes 1081352 | tf_op jit(solution)/shard_map/ppermute | solution.py:686
  124.0 33.4 %collective-permute-start.23 = (bf16[480,1024]{1,0:T(8,128)(2,1)S(1)}, bf16[480,1024]{1,0:T(8,128)(2,1)S(1)}, u32[]{:S(2)}, u32[]{:S(2)}) collective-permute-start(bf16[480,1024]{1,0:T(8,128)(2,1)S(1)} %pad_maximum_fusion.3.refs_0_), channel_id=1, source_target_pairs={{0,8},{4,12},{8,0},{12,4},{16,24},{20,28},{24,16},{28,20},{1,9},{5... | collective-permute-start | bytes 2949128 | tf_op jit(solution)/shard_map/ppermute | solution.py:686
  125.5 31.9 %collective-permute-start.24 = (bf16[480,1024]{1,0:T(8,128)(2,1)S(1)}, bf16[480,1024]{1,0:T(8,128)(2,1)}, u32[]{:S(2)}, u32[]{:S(2)}) collective-permute-start(bf16[480,1024]{1,0:T(8,128)(2,1)S(1)} %pad_maximum_fusion.3.refs_0_), channel_id=1, source_target_pairs={{0,16},{4,20},{8,24},{12,28},{16,0},{20,4},{24,8},{28,12},{1,17},{... | collective-permute-start | bytes 2949128 | tf_op jit(solution)/shard_map/ppermute | solution.py:686
  129.4 28.0 %all-to-all-start.1 = ((bf16[8,3,128,128]{3,2,1,0:T(8,128)(2,1)}), bf16[8,3,128,128]{3,2,1,0:T(8,128)(2,1)S(1)}, u32[]{:S(2)}, u32[]{:S(2)}) async-start(bf16[8,3,128,128]{3,2,1,0:T(8,128)(2,1)} %chain.2), calls=%async_computation.1 | async-start | bytes 1572864 | tf_op jit(solution)/shard_map/all_to_all | solution.py:309
  133.1 37.3 %collective-permute-start.27 = (bf16[480,1024]{1,0:T(8,128)(2,1)S(1)}, bf16[480,1024]{1,0:T(8,128)(2,1)}, u32[]{:S(2)}, u32[]{:S(2)}) collective-permute-start(bf16[480,1024]{1,0:T(8,128)(2,1)S(1)} %pad_maximum_fusion.3.refs_0_), channel_id=1, source_target_pairs={{0,4},{4,0},{8,12},{12,8},{16,20},{20,16},{24,28},{28,24},{1,5},{5... | collective-permute-start | bytes 2949128 | tf_op jit(solution)/shard_map/ppermute | solution.py:686
  157.4 11.1 %collective-permute-start.25 = (bf16[240,1024]{1,0:T(8,128)(2,1)S(1)}, bf16[240,1024]{1,0:T(8,128)(2,1)S(1)}, u32[]{:S(2)}, u32[]{:S(2)}) collective-permute-start(bf16[240,1024]{1,0:T(8,128)(2,1)S(1)} %slice.223), channel_id=1, source_target_pairs={{0,16},{4,20},{8,24},{12,28},{16,0},{20,4},{24,8},{28,12},{1,17},{... | collective-permute-start | bytes 1474568 | tf_op jit(solution)/shard_map/ppermute | solution.py:686
  159.1 11.3 %collective-permute-start.26 = (bf16[240,1024]{1,0:T(8,128)(2,1)S(1)}, bf16[240,1024]{1,0:T(8,128)(2,1)S(1)}, u32[]{:S(2)}, u32[]{:S(2)}) collective-permute-start(bf16[240,1024]{1,0:T(8,128)(2,1)S(1)} %slice.224), channel_id=1, source_target_pairs={{0,8},{4,12},{8,0},{12,4},{16,24},{20,28},{24,16},{28,20},{1,9},{5... | collective-permute-start | bytes 1474568 | tf_op jit(solution)/shard_map/ppermute | solution.py:686
  160.2 14.1 %collective-permute-start.28 = (bf16[480,1024]{1,0:T(8,128)(2,1)S(1)}, bf16[480,1024]{1,0:T(8,128)(2,1)S(1)}, u32[]{:S(2)}, u32[]{:S(2)}) collective-permute-start(bf16[480,1024]{1,0:T(8,128)(2,1)S(1)} %collective-permute-done.23.refs_1_), channel_id=1, source_target_pairs={{0,4},{4,0},{8,12},{12,8},{16,20},{20,16},{24,28},{28,24},{1,5},{5... | collective-permute-start | bytes 2949128 | tf_op jit(solution)/shard_map/ppermute | solution.py:686
  160.3 14.6 %collective-permute-start.29 = (bf16[480,1024]{1,0:T(8,128)(2,1)}, bf16[480,1024]{1,0:T(8,128)(2,1)S(1)}, u32[]{:S(2)}, u32[]{:S(2)}) collective-permute-start(bf16[480,1024]{1,0:T(8,128)(2,1)} %collective-permute-done.24.refs_2_), channel_id=1, source_target_pairs={{0,4},{4,0},{8,12},{12,8},{16,20},{20,16},{24,28},{28,24},{1,5},{5... | collective-permute-start | bytes 2949128 | tf_op jit(solution)/shard_map/ppermute | solution.py:686
  170.4 12.1 %collective-permute-start.32 = (bf16[128,2816]{1,0:T(8,128)(2,1)}, bf16[128,2816]{1,0:T(8,128)(2,1)S(1)}, u32[]{:S(2)}, u32[]{:S(2)}) collective-permute-start(bf16[128,2816]{1,0:T(8,128)(2,1)} %refs_10_), channel_id=1, source_target_pairs={{0,4},{4,0},{8,12},{12,8},{16,20},{20,16},{24,28},{28,24},{1,5},{5... | collective-permute-start | bytes 2162696 | tf_op jit(solution)/shard_map/ppermute | solution.py:686
  170.9 11.7 %collective-permute-start.33 = (bf16[128,2816]{1,0:T(8,128)(2,1)}, bf16[128,2816]{1,0:T(8,128)(2,1)S(1)}, u32[]{:S(2)}, u32[]{:S(2)}) collective-permute-start(bf16[128,2816]{1,0:T(8,128)(2,1)} %copy-done.29), channel_id=1, source_target_pairs={{0,4},{4,0},{8,12},{12,8},{16,20},{20,16},{24,28},{28,24},{1,5},{5... | collective-permute-start | bytes 2162696 | tf_op jit(solution)/shard_map/ppermute | solution.py:686
  172.3 10.3 %collective-permute-start.34 = (bf16[128,2816]{1,0:T(8,128)(2,1)}, bf16[128,2816]{1,0:T(8,128)(2,1)S(1)}, u32[]{:S(2)}, u32[]{:S(2)}) collective-permute-start(bf16[128,2816]{1,0:T(8,128)(2,1)} %collective-permute-done.15.refs_12_), channel_id=1, source_target_pairs={{0,4},{4,0},{8,12},{12,8},{16,20},{20,16},{24,28},{28,24},{1,5},{5... | collective-permute-start | bytes 2162696 | tf_op jit(solution)/shard_map/ppermute | solution.py:686
  242.9 34.7 %collective-permute-start.37 = (bf16[4,128,5632]{2,1,0:T(8,128)(2,1)}, bf16[4,128,5632]{2,1,0:T(8,128)(2,1)}, u32[]{:S(2)}, u32[]{:S(2)}) collective-permute-start(bf16[4,128,5632]{2,1,0:T(8,128)(2,1)} %get-tuple-element.240), channel_id=1, source_target_pairs={{0,4},{4,0},{8,12},{12,8},{16,20},{20,16},{24,28},{28,24},{1,5},{5... | collective-permute-start | bytes 17301512 | tf_op jit(solution)/shard_map/ppermute | solution.py:686
  243.2 16.1 %all-to-all-start.2 = ((bf16[8,3,128,128]{3,2,1,0:T(8,128)(2,1)}), bf16[8,3,128,128]{3,2,1,0:T(8,128)(2,1)S(1)}, u32[]{:S(2)}, u32[]{:S(2)}) async-start(bf16[8,3,128,128]{3,2,1,0:T(8,128)(2,1)} %bitcast.21), calls=%async_computation.2 | async-start | bytes 1572864 | tf_op jit(solution)/shard_map/all_to_all | solution.py:305
  263.7 23.7 %all-to-all-start.3 = ((bf16[8,3,128,128]{3,2,1,0:T(8,128)(2,1)}), bf16[8,3,128,128]{3,2,1,0:T(8,128)(2,1)S(1)}, u32[]{:S(2)}, u32[]{:S(2)}) async-start(bf16[8,3,128,128]{3,2,1,0:T(8,128)(2,1)} %chain.3.refs_0_), calls=%async_computation.3 | async-start | bytes 1572864 | tf_op jit(solution)/shard_map/all_to_all | solution.py:309
  277.2 38.4 %collective-permute-start.41 = (bf16[4,480,1024]{2,1,0:T(8,128)(2,1)}, bf16[4,480,1024]{2,1,0:T(8,128)(2,1)}, u32[]{:S(2)}, u32[]{:S(2)}) collective-permute-start(bf16[4,480,1024]{2,1,0:T(8,128)(2,1)} %get-tuple-element.248), channel_id=1, source_target_pairs={{0,4},{4,0},{8,12},{12,8},{16,20},{20,16},{24,28},{28,24},{1,5},{5... | collective-permute-start | bytes 11796488 | tf_op jit(solution)/shard_map/ppermute | solution.py:686
  290.0 25.7 %collective-permute-start.39 = (bf16[64,5632]{1,0:T(8,128)(2,1)}, bf16[64,5632]{1,0:T(8,128)(2,1)S(1)}, u32[]{:S(2)}, u32[]{:S(2)}) collective-permute-start(bf16[64,5632]{1,0:T(8,128)(2,1)} %get-tuple-element.479), channel_id=1, source_target_pairs={{0,8},{4,12},{8,0},{12,4},{16,24},{20,28},{24,16},{28,20},{1,9},{5... | collective-permute-start | bytes 2162696 | tf_op jit(solution)/shard_map/ppermute | solution.py:686
  291.6 24.0 %collective-permute-start.40 = (bf16[64,5632]{1,0:T(8,128)(2,1)S(1)}, bf16[64,5632]{1,0:T(8,128)(2,1)S(1)}, u32[]{:S(2)}, u32[]{:S(2)}) collective-permute-start(bf16[64,5632]{1,0:T(8,128)(2,1)S(1)} %get-tuple-element.478), channel_id=1, source_target_pairs={{0,16},{4,20},{8,24},{12,28},{16,0},{20,4},{24,8},{28,12},{1,17},{... | collective-permute-start | bytes 2162696 | tf_op jit(solution)/shard_map/ppermute | solution.py:686
  313.4 10.8 %collective-permute-start.38 = (bf16[3,3,8,512]{3,2,1,0:T(8,128)(2,1)S(1)}, bf16[3,3,8,512]{3,2,1,0:T(8,128)(2,1)S(1)}, u32[]{:S(2)}, u32[]{:S(2)}) collective-permute-start(bf16[3,3,8,512]{3,2,1,0:T(8,128)(2,1)S(1)} %convert_element_type.340), channel_id=1, source_target_pairs={{4,0},{8,4},{12,8},{16,12},{20,16},{24,20},{28,24},{5,1},{9,5},{13... | collective-permute-start | bytes 221192 | tf_op jit(solution)/shard_map/ppermute | solution.py:681
  326.0 34.5 %collective-permute-start.44 = (bf16[128,5632]{1,0:T(8,128)(2,1)S(1)}, bf16[128,5632]{1,0:T(8,128)(2,1)}, u32[]{:S(2)}, u32[]{:S(2)}) collective-permute-start(bf16[128,5632]{1,0:T(8,128)(2,1)S(1)} %pad_maximum_fusion.2.refs_2_.refs_3_), channel_id=1, source_target_pairs={{0,16},{4,20},{8,24},{12,28},{16,0},{20,4},{24,8},{28,12},{1,17},{... | collective-permute-start | bytes 4325384 | tf_op jit(solution)/shard_map/ppermute | solution.py:686
  329.2 33.2 %collective-permute-start.43 = (bf16[128,5632]{1,0:T(8,128)(2,1)}, bf16[128,5632]{1,0:T(8,128)(2,1)}, u32[]{:S(2)}, u32[]{:S(2)}) collective-permute-start(bf16[128,5632]{1,0:T(8,128)(2,1)} %pad_maximum_fusion.1.refs_1_.refs_2_), channel_id=1, source_target_pairs={{0,8},{4,12},{8,0},{12,4},{16,24},{20,28},{24,16},{28,20},{1,9},{5... | collective-permute-start | bytes 4325384 | tf_op jit(solution)/shard_map/ppermute | solution.py:686
  335.9 26.5 %collective-permute-start.45 = (bf16[4,128,1536]{2,1,0:T(8,128)(2,1)}, bf16[4,128,1536]{2,1,0:T(8,128)(2,1)}, u32[]{:S(2)}, u32[]{:S(2)}) collective-permute-start(bf16[4,128,1536]{2,1,0:T(8,128)(2,1)} %get-tuple-element.265), channel_id=1, source_target_pairs={{0,4},{4,0},{8,12},{12,8},{16,20},{20,16},{24,28},{28,24},{1,5},{5... | collective-permute-start | bytes 4718600 | tf_op jit(solution)/shard_map/ppermute | solution.py:686
  358.1 27.9 %collective-permute-start.42 = (bf16[3,3,8,512]{3,2,1,0:T(8,128)(2,1)}, bf16[3,3,8,512]{3,2,1,0:T(8,128)(2,1)}, u32[]{:S(2)}, u32[]{:S(2)}) collective-permute-start(bf16[3,3,8,512]{3,2,1,0:T(8,128)(2,1)} %convert_element_type.351), channel_id=1, source_target_pairs={{4,0},{8,4},{12,8},{16,12},{20,16},{24,20},{28,24},{5,1},{9,5},{13... | collective-permute-start | bytes 221192 | tf_op jit(solution)/shard_map/ppermute | solution.py:681
  363.7 15.3 %collective-permute-start.52 = (f32[1,128]{1,0:T(1,128)S(1)}, f32[1,128]{1,0:T(1,128)S(1)}, u32[]{:S(2)}, u32[]{:S(2)}) collective-permute-start(f32[1,128]{1,0:T(1,128)S(1)} %bitcast.167), channel_id=1, source_target_pairs={{0,4},{4,0},{8,12},{12,8},{16,20},{20,16},{24,28},{28,24},{1,5},{5... | collective-permute-start | bytes 1544 | tf_op jit(solution)/shard_map/ppermute | solution.py:686
  368.4 17.5 %collective-permute-start.46 = (bf16[240,1024]{1,0:T(8,128)(2,1)}, bf16[240,1024]{1,0:T(8,128)(2,1)}, u32[]{:S(2)}, u32[]{:S(2)}) collective-permute-start(bf16[240,1024]{1,0:T(8,128)(2,1)} %get-tuple-element.485), channel_id=1, source_target_pairs={{0,8},{4,12},{8,0},{12,4},{16,24},{20,28},{24,16},{28,20},{1,9},{5... | collective-permute-start | bytes 1474568 | tf_op jit(solution)/shard_map/ppermute | solution.py:686
  368.7 17.2 %collective-permute-start.47 = (bf16[240,1024]{1,0:T(8,128)(2,1)}, bf16[240,1024]{1,0:T(8,128)(2,1)}, u32[]{:S(2)}, u32[]{:S(2)}) collective-permute-start(bf16[240,1024]{1,0:T(8,128)(2,1)} %get-tuple-element.484), channel_id=1, source_target_pairs={{0,16},{4,20},{8,24},{12,28},{16,0},{20,4},{24,8},{28,12},{1,17},{... | collective-permute-start | bytes 1474568 | tf_op jit(solution)/shard_map/ppermute | solution.py:686
  370.4 29.3 %collective-permute-start.50 = (bf16[128,2816]{1,0:T(8,128)(2,1)}, bf16[128,2816]{1,0:T(8,128)(2,1)S(1)}, u32[]{:S(2)}, u32[]{:S(2)}) collective-permute-start(bf16[128,2816]{1,0:T(8,128)(2,1)} %get-tuple-element.286.refs_1_), channel_id=1, source_target_pairs={{0,1},{3,2},{4,5},{7,6},{8,9},{11,10},{12,13},{15,14},{16,17},{19,... | collective-permute-start | bytes 2162696 | tf_op jit(solution)/shard_map/ppermute | solution.py:1190
  382.8 22.2 %collective-permute-start.51 = (bf16[128,2816]{1,0:T(8,128)(2,1)S(1)}, bf16[128,2816]{1,0:T(8,128)(2,1)S(1)}, u32[]{:S(2)}, u32[]{:S(2)}) collective-permute-start(bf16[128,2816]{1,0:T(8,128)(2,1)S(1)} %copy-done.9), channel_id=1, source_target_pairs={{0,1},{3,2},{4,5},{7,6},{8,9},{11,10},{12,13},{15,14},{16,17},{19,... | collective-permute-start | bytes 2162696 | tf_op jit(solution)/shard_map/ppermute | solution.py:1190
  386.8 12.9 %collective-permute-start.48 = (bf16[64,1536]{1,0:T(8,128)(2,1)}, bf16[64,1536]{1,0:T(8,128)(2,1)S(1)}, u32[]{:S(2)}, u32[]{:S(2)}) collective-permute-start(bf16[64,1536]{1,0:T(8,128)(2,1)} %get-tuple-element.497), channel_id=1, source_target_pairs={{0,8},{4,12},{8,0},{12,4},{16,24},{20,28},{24,16},{28,20},{1,9},{5... | collective-permute-start | bytes 589832 | tf_op jit(solution)/shard_map/ppermute | solution.py:686
  387.1 12.6 %collective-permute-start.49 = (bf16[64,1536]{1,0:T(8,128)(2,1)}, bf16[64,1536]{1,0:T(8,128)(2,1)S(1)}, u32[]{:S(2)}, u32[]{:S(2)}) collective-permute-start(bf16[64,1536]{1,0:T(8,128)(2,1)} %get-tuple-element.496), channel_id=1, source_target_pairs={{0,16},{4,20},{8,24},{12,28},{16,0},{20,4},{24,8},{28,12},{1,17},{... | collective-permute-start | bytes 589832 | tf_op jit(solution)/shard_map/ppermute | solution.py:686
  408.0 24.2 %collective-permute-start.58 = (bf16[128,2816]{1,0:T(8,128)(2,1)S(1)}, bf16[128,2816]{1,0:T(8,128)(2,1)}, u32[]{:S(2)}, u32[]{:S(2)}) collective-permute-start(bf16[128,2816]{1,0:T(8,128)(2,1)S(1)} %add_convert_fusion.7.refs_4_), channel_id=1, source_target_pairs={{1,2},{2,1},{5,6},{6,5},{9,10},{10,9},{13,14},{14,13},{17,18},{18,... | collective-permute-start | bytes 2162696 | tf_op jit(solution)/shard_map/ppermute | solution.py:1198
  409.6 26.4 %collective-permute-start.54 = (bf16[4,128,1536]{2,1,0:T(8,128)(2,1)}, bf16[4,128,1536]{2,1,0:T(8,128)(2,1)}, u32[]{:S(2)}, u32[]{:S(2)}) collective-permute-start(bf16[4,128,1536]{2,1,0:T(8,128)(2,1)} %outer.1.refs_0_), channel_id=1, source_target_pairs={{0,4},{4,0},{8,12},{12,8},{16,20},{20,16},{24,28},{28,24},{1,5},{5... | collective-permute-start | bytes 4718600 | tf_op jit(solution)/shard_map/ppermute | solution.py:686
  409.6 24.5 %collective-permute-start.56 = (bf16[480,1024]{1,0:T(8,128)(2,1)}, bf16[480,1024]{1,0:T(8,128)(2,1)}, u32[]{:S(2)}, u32[]{:S(2)}) collective-permute-start(bf16[480,1024]{1,0:T(8,128)(2,1)} %pad_maximum_fusion.4.refs_1_), channel_id=1, source_target_pairs={{0,8},{4,12},{8,0},{12,4},{16,24},{20,28},{24,16},{28,20},{1,9},{5... | collective-permute-start | bytes 2949128 | tf_op jit(solution)/shard_map/ppermute | solution.py:686
  411.0 24.9 %collective-permute-start.57 = (bf16[480,1024]{1,0:T(8,128)(2,1)}, bf16[480,1024]{1,0:T(8,128)(2,1)}, u32[]{:S(2)}, u32[]{:S(2)}) collective-permute-start(bf16[480,1024]{1,0:T(8,128)(2,1)} %pad_maximum_fusion.5.refs_2_), channel_id=1, source_target_pairs={{0,16},{4,20},{8,24},{12,28},{16,0},{20,4},{24,8},{28,12},{1,17},{... | collective-permute-start | bytes 2949128 | tf_op jit(solution)/shard_map/ppermute | solution.py:686
  430.7 23.6 %collective-permute-start.60 = (bf16[128,1536]{1,0:T(8,128)(2,1)}, bf16[128,1536]{1,0:T(8,128)(2,1)S(1)}, u32[]{:S(2)}, u32[]{:S(2)}) collective-permute-start(bf16[128,1536]{1,0:T(8,128)(2,1)} %pad_maximum_fusion.9.refs_3_), channel_id=1, source_target_pairs={{0,16},{4,20},{8,24},{12,28},{16,0},{20,4},{24,8},{28,12},{1,17},{... | collective-permute-start | bytes 1179656 | tf_op jit(solution)/shard_map/ppermute | solution.py:686
  432.2 22.1 %collective-permute-start.59 = (bf16[128,1536]{1,0:T(8,128)(2,1)}, bf16[128,1536]{1,0:T(8,128)(2,1)S(1)}, u32[]{:S(2)}, u32[]{:S(2)}) collective-permute-start(bf16[128,1536]{1,0:T(8,128)(2,1)} %pad_maximum_fusion.8.refs_2_), channel_id=1, source_target_pairs={{0,8},{4,12},{8,0},{12,4},{16,24},{20,28},{24,16},{28,20},{1,9},{5... | collective-permute-start | bytes 1179656 | tf_op jit(solution)/shard_map/ppermute | solution.py:686
  434.0 22.6 %collective-permute-start.64 = (bf16[128,2816]{1,0:T(8,128)(2,1)S(1)}, bf16[128,2816]{1,0:T(8,128)(2,1)S(1)}, u32[]{:S(2)}, u32[]{:S(2)}) collective-permute-start(bf16[128,2816]{1,0:T(8,128)(2,1)S(1)} %copy-done.6), channel_id=1, source_target_pairs={{1,2},{2,1},{5,6},{6,5},{9,10},{10,9},{13,14},{14,13},{17,18},{18,... | collective-permute-start | bytes 2162696 | tf_op jit(solution)/shard_map/ppermute | solution.py:1198
  438.1 27.5 %collective-permute-start.63 = (bf16[480,1024]{1,0:T(8,128)(2,1)S(1)}, bf16[480,1024]{1,0:T(8,128)(2,1)S(1)}, u32[]{:S(2)}, u32[]{:S(2)}) collective-permute-start(bf16[480,1024]{1,0:T(8,128)(2,1)S(1)} %add_convert_fusion.3.refs_1_), channel_id=1, source_target_pairs={{0,1},{3,2},{4,5},{7,6},{8,9},{11,10},{12,13},{15,14},{16,17},{19,... | collective-permute-start | bytes 2949128 | tf_op jit(solution)/shard_map/ppermute | solution.py:1190
  446.4 19.0 %collective-permute-start.65 = (bf16[128,2816]{1,0:T(8,128)(2,1)S(1)}, bf16[128,2816]{1,0:T(8,128)(2,1)S(1)}, u32[]{:S(2)}, u32[]{:S(2)}) collective-permute-start(bf16[128,2816]{1,0:T(8,128)(2,1)S(1)} %add_convert_fusion.5.refs_0_), channel_id=1, source_target_pairs={{1,0},{2,3},{5,4},{6,7},{9,8},{10,11},{13,12},{14,15},{17,16},{18,... | collective-permute-start | bytes 2162696 | tf_op jit(solution)/shard_map/ppermute | solution.py:1206
  466.1 20.2 %collective-permute-start.69 = (bf16[128,2816]{1,0:T(8,128)(2,1)S(1)}, bf16[128,2816]{1,0:T(8,128)(2,1)S(1)}, u32[]{:S(2)}, u32[]{:S(2)}) collective-permute-start(bf16[128,2816]{1,0:T(8,128)(2,1)S(1)} %add_convert_fusion.4), channel_id=1, source_target_pairs={{1,0},{2,3},{5,4},{6,7},{9,8},{10,11},{13,12},{14,15},{17,16},{18,... | collective-permute-start | bytes 2162696 | tf_op jit(solution)/shard_map/ppermute | solution.py:1206
  467.8 18.5 %collective-permute-start.68 = (bf16[480,1024]{1,0:T(8,128)(2,1)S(1)}, bf16[480,1024]{1,0:T(8,128)(2,1)S(1)}, u32[]{:S(2)}, u32[]{:S(2)}) collective-permute-start(bf16[480,1024]{1,0:T(8,128)(2,1)S(1)} %add_convert_fusion.2), channel_id=1, source_target_pairs={{1,2},{2,1},{5,6},{6,5},{9,10},{10,9},{13,14},{14,13},{17,18},{18,... | collective-permute-start | bytes 2949128 | tf_op jit(solution)/shard_map/ppermute | solution.py:1198
  468.7 17.6 %collective-permute-start.67 = (bf16[128,1664]{1,0:T(8,128)(2,1)S(1)}, bf16[128,1664]{1,0:T(8,128)(2,1)S(1)}, u32[]{:S(2)}, u32[]{:S(2)}) collective-permute-start(bf16[128,1664]{1,0:T(8,128)(2,1)S(1)} %pad_maximum_fusion.7), channel_id=1, source_target_pairs={{0,16},{4,20},{8,24},{12,28},{16,0},{20,4},{24,8},{28,12},{1,17},{... | collective-permute-start | bytes 1277960 | tf_op jit(solution)/shard_map/ppermute | solution.py:686
  470.5 15.8 %collective-permute-start.66 = (bf16[128,1664]{1,0:T(8,128)(2,1)S(1)}, bf16[128,1664]{1,0:T(8,128)(2,1)S(1)}, u32[]{:S(2)}, u32[]{:S(2)}) collective-permute-start(bf16[128,1664]{1,0:T(8,128)(2,1)S(1)} %pad_maximum_fusion.6), channel_id=1, source_target_pairs={{0,8},{4,12},{8,0},{12,4},{16,24},{20,28},{24,16},{28,20},{1,9},{5... | collective-permute-start | bytes 1277960 | tf_op jit(solution)/shard_map/ppermute | solution.py:686
  473.3 13.0 %collective-permute-start.71 = (bf16[128,1536]{1,0:T(8,128)(2,1)S(1)}, bf16[128,1536]{1,0:T(8,128)(2,1)S(1)}, u32[]{:S(2)}, u32[]{:S(2)}) collective-permute-start(bf16[128,1536]{1,0:T(8,128)(2,1)S(1)} %add_convert_fusion.13), channel_id=1, source_target_pairs={{0,1},{3,2},{4,5},{7,6},{8,9},{11,10},{12,13},{15,14},{16,17},{19,... | collective-permute-start | bytes 1179656 | tf_op jit(solution)/shard_map/ppermute | solution.py:1190
  486.4 21.1 %collective-permute-start.74 = (bf16[128,1536]{1,0:T(8,128)(2,1)S(1)}, bf16[128,1536]{1,0:T(8,128)(2,1)S(1)}, u32[]{:S(2)}, u32[]{:S(2)}) collective-permute-start(bf16[128,1536]{1,0:T(8,128)(2,1)S(1)} %add_convert_fusion.12), channel_id=1, source_target_pairs={{1,2},{2,1},{5,6},{6,5},{9,10},{10,9},{13,14},{14,13},{17,18},{18,... | collective-permute-start | bytes 1179656 | tf_op jit(solution)/shard_map/ppermute | solution.py:1198
  487.5 30.5 %collective-permute-start.73 = (bf16[480,1024]{1,0:T(8,128)(2,1)S(1)}, bf16[480,1024]{1,0:T(8,128)(2,1)S(1)}, u32[]{:S(2)}, u32[]{:S(2)}) collective-permute-start(bf16[480,1024]{1,0:T(8,128)(2,1)S(1)} %add_convert_fusion.1), channel_id=1, source_target_pairs={{1,0},{2,3},{5,4},{6,7},{9,8},{10,11},{13,12},{14,15},{17,16},{18,... | collective-permute-start | bytes 2949128 | tf_op jit(solution)/shard_map/ppermute | solution.py:1206
  488.9 18.6 %collective-permute-start.72 = (bf16[128,1664]{1,0:T(8,128)(2,1)S(1)}, bf16[128,1664]{1,0:T(8,128)(2,1)S(1)}, u32[]{:S(2)}, u32[]{:S(2)}) collective-permute-start(bf16[128,1664]{1,0:T(8,128)(2,1)S(1)} %add_convert_fusion.10), channel_id=1, source_target_pairs={{0,1},{3,2},{4,5},{7,6},{8,9},{11,10},{12,13},{15,14},{16,17},{19,... | collective-permute-start | bytes 1277960 | tf_op jit(solution)/shard_map/ppermute | solution.py:1190
  518.1 10.5 %collective-permute-start.77 = (bf16[128,1664]{1,0:T(8,128)(2,1)S(1)}, bf16[128,1664]{1,0:T(8,128)(2,1)S(1)}, u32[]{:S(2)}, u32[]{:S(2)}) collective-permute-start(bf16[128,1664]{1,0:T(8,128)(2,1)S(1)} %add_convert_fusion.9), channel_id=1, source_target_pairs={{1,2},{2,1},{5,6},{6,5},{9,10},{10,9},{13,14},{14,13},{17,18},{18,... | collective-permute-start | bytes 1277960 | tf_op jit(solution)/shard_map/ppermute | solution.py:1198
  (85 other events, 680.3 us)
